TPU v7x, 512 devices: a whole 4x4x16 slice. The times are simulated.
512 devices in a mesh: replica: 4 (over z_hi, core), fsdp: 32 (over x, z_lo), tensor: 4 (over y).
Axes of the slice: x: 4, y: 4, z: 16 (z_hi: 2, z_lo: 8; z = z_hi * 8 + z_lo), core: 2. Of those that a mesh axis runs over, the one named last changes fastest.
Arguments:
- tokens: bfloat16 [65536, 8192], P(('replica', 'fsdp', 'tensor')), may hold values from -6 to 6
- cotangent: bfloat16 [65536, 2, 512], P(('replica', 'fsdp'), None, 'tensor'), may hold values from -0.125 to 0.125
- weights: bfloat16 [4, 8192, 2, 512], P('replica', 'fsdp', None, 'tensor'), may hold values from -0.0625 to 0.0625
- first_moment: float32 [4, 8192, 2, 512], P('replica', 'fsdp', None, 'tensor'), may hold values from -6 to 6
- second_moment: float32 [4, 8192, 2, 512], P('replica', 'fsdp', None, 'tensor'), may hold values from 0.5 to 2
- frag_global: float32 [8192, 2, 512], P('fsdp', None, 'tensor'), may hold values from -6 to 6
- frag_moment: float32 [8192, 2, 512], P('fsdp', None, 'tensor'), may hold values from -6 to 6
- frag_local: bfloat16 [4, 8192, 2, 512], P('replica', 'fsdp', None, 'tensor'), may hold values from -6 to 6
Outputs:
- keys_values: bfloat16 [65536, 2, 512], P(('replica', 'fsdp'), None, 'tensor')
- weights_next: bfloat16 [4, 8192, 2, 512], P('replica', 'fsdp', None, 'tensor')
- first_next: float32 [4, 8192, 2, 512], P('replica', 'fsdp', None, 'tensor')
- second_next: float32 [4, 8192, 2, 512], P('replica', 'fsdp', None, 'tensor')
- global_next: float32 [8192, 2, 512], P('fsdp', None, 'tensor')
- moment_next: float32 [8192, 2, 512], P('fsdp', None, 'tensor')
- local_next: bfloat16 [4, 8192, 2, 512], P('replica', 'fsdp', None, 'tensor')
All inputs are finite; a program needn't handle non-finite values.
Results may differ from a plain program's by a relative error of at most 0.009.
Values may be sent and summed in bfloat16 or wider, within the bound.
No kernel may reach another device: no remote copies, remote signals or barrier semaphores. Data moves between devices by JAX's collectives and lax.ppermute only.
A program may use at most 128 MiB of HBM per device.

v0:
```python
import jax
import jax.numpy as jnp
from jax import lax
from jax.sharding import PartitionSpec as P


def body(
    tokens, cotangent, weights, first_moment, second_moment, frag_global, frag_moment, frag_local
):
    local_float = frag_local[0].astype(jnp.float32)
    summed = lax.psum(local_float.astype(jnp.bfloat16), "replica").astype(jnp.float32)
    outer_step = frag_global - summed / lax.axis_size("replica")
    moment_next = 0.9 * frag_moment + outer_step
    global_next = frag_global - 0.7 * (outer_step + 0.9 * moment_next)
    local_next = (0.5 * local_float + 0.5 * global_next).astype(jnp.bfloat16)
    global_next, moment_next, local_next = (global_next, moment_next, local_next[None])
    gathered = lax.all_gather(tokens, "tensor", axis=0, tiled=True)
    columns = gathered
    projected = jnp.einsum(
        "td,dkc->tkc",
        columns,
        lax.all_gather(weights[0], "fsdp", axis=0, tiled=True),
        preferred_element_type=jnp.float32,
    )
    keys_values = projected.astype(jnp.bfloat16)
    columns = gathered
    gradient = lax.psum_scatter(
        jnp.einsum("td,tkc->dkc", columns, cotangent, preferred_element_type=jnp.float32).astype(
            jnp.bfloat16
        ),
        "fsdp",
        scatter_dimension=0,
        tiled=True,
    ).astype(jnp.float32)
    gradient = gradient[None]
    first_next = 0.9 * first_moment + 0.1 * gradient
    second_next = 0.95 * second_moment + 0.05 * gradient * gradient
    weight_float = weights.astype(jnp.float32)
    update = first_next / (1.0 - 0.9**10) / (jnp.sqrt(second_next / (1.0 - 0.95**10)) + 1e-08)
    weights_next = (weight_float - 0.001 * (update + 0.1 * weight_float)).astype(jnp.bfloat16)
    return (
        keys_values,
        weights_next,
        first_next,
        second_next,
        global_next,
        moment_next,
        local_next,
    )


def solution(mesh):
    return jax.shard_map(
        body,
        mesh=mesh,
        in_specs=(
            P(("replica", "fsdp", "tensor"), None),
            P(("replica", "fsdp"), None, "tensor"),
            P("replica", "fsdp", None, "tensor"),
            P("replica", "fsdp", None, "tensor"),
            P("replica", "fsdp", None, "tensor"),
            P("fsdp", None, "tensor"),
            P("fsdp", None, "tensor"),
            P("replica", "fsdp", None, "tensor"),
        ),
        out_specs=(
            P(("replica", "fsdp"), None, "tensor"),
            P("replica", "fsdp", None, "tensor"),
            P("replica", "fsdp", None, "tensor"),
            P("replica", "fsdp", None, "tensor"),
            P("fsdp", None, "tensor"),
            P("fsdp", None, "tensor"),
            P("replica", "fsdp", None, "tensor"),
        ),
        check_vma=False,
    )
```

profile of v0, /device:TPU:16, one launch (start us, length us, event | category | flops | bytes accessed | tf_op | source)
XLA Modules:
  0.0 615.0 jit_solution(9813667823967061453)
XLA Ops:
  8.0 0.0 copy-start
  8.0 0.0 all-gather.4.cloned.1.call-start
  8.1 0.7 all-gather.4.cloned.1.call-update
  8.7 0.0 all-reduce.2.cloned.1.call-start
  8.8 0.5 all-reduce.2.cloned.1.call-update
  9.3 0.0 all-gather.6.cloned.1.call-start
  9.4 1.6 copy.15
  11.0 0.0 all-gather.6.cloned.1.call-update
  11.0 0.0 copy-start.1
  11.0 0.0 copy-start.3
  11.0 0.0 copy-start.4
  11.0 0.0 reduce-scatter.2.cloned.1.call-start
  11.1 94.7 %all-gather.4.cloned.1.call-done = bf16[512,8192]{1,0:T(8,128)(2,1)} async-done(((bf16[128,8192]{1,0:T(8,128)(2,1)}), bf16[512,8192]{1,0:T(8,128)(2,1)}) %all-gather.4.cloned.1.call-update) | async-done | bytes 8388624 | tf_op jit(solution)/shard_map/all_gather | solution.py:17
  105.8 0.0 copy-done
  105.8 7.7 %convolution_convert_fusion = bf16[8192,2,128]{2,0,1:T(8,128)(2,1)} fusion(bf16[512,8192]{1,0:T(8,128)(2,1)} %all-gather.4.cloned.1.call-done, bf16[512,2,128]{2,1,0:T(2,128)(2,1)S(1)} %copy-done), kind=kOutput, calls=%fused_computation | convolution fusion | flops 2149580800 | bytes 12845056 | tf_op jit(solution)/shard_map/td,tkc->dkc/dot_general | solution.py:28
  113.5 0.0 reduce-scatter.2.cloned.1.call-update
  113.5 0.0 all-reduce.2.cloned.1.call-done
  113.6 0.0 copy-done.1
  113.6 0.0 copy-done.3
  113.6 0.0 copy-done.4
  113.6 2.2 fusion.17
  115.8 0.0 copy-start.2
  115.8 0.0 copy-start.5
  115.8 0.0 copy-start.6
  115.8 231.2 %all-gather.6.cloned.1.call-done = bf16[1,8192,2,128]{3,1,2,0:T(8,128)(2,1)} async-done(((bf16[1,256,2,128]{3,1,2,0:T(8,128)(2,1)}), bf16[1,8192,2,128]{3,1,2,0:T(8,128)(2,1)}) %all-gather.6.cloned.1.call-update) | async-done | bytes 4194320 | tf_op jit(solution)/shard_map/all_gather | solution.py:22
  347.0 6.9 %fusion.4 = bf16[512,2,128]{2,0,1:T(8,128)(2,1)S(1)} fusion(bf16[1,8192,2,128]{3,1,2,0:T(8,128)(2,1)} %all-gather.6.cloned.1.call-done, bf16[512,8192]{1,0:T(8,128)(2,1)} %all-gather.4.cloned.1.call-done), kind=kOutput, calls=%fused_computation.5 | convolution fusion | flops 2147614720 | bytes 12845056 | tf_op jit(solution)/shard_map/td,dkc->tkc/dot_general | solution.py:19
  353.9 1.0 copy.21
  354.9 249.2 %reduce-scatter.2.cloned.1.call-done = bf16[256,2,128]{2,0,1:T(8,128)(2,1)} async-done(((bf16[8192,2,128]{2,0,1:T(8,128)(2,1)}), bf16[256,2,128]{2,0,1:T(8,128)(2,1)}) %reduce-scatter.2.cloned.1.call-update) | async-done | bytes 131088 | tf_op jit(solution)/shard_map/reduce_scatter | solution.py:27
  604.1 0.0 copy-done.2
  604.1 0.0 copy-done.5
  604.1 0.0 copy-done.6
  604.1 1.1 fusion.11
  605.2 0.8 copy.22
  606.0 0.9 copy.23
  606.9 0.9 copy.24
Async XLA Ops:
  8.0 97.8 %copy-start = (bf16[512,2,128]{2,1,0:T(2,128)(2,1)S(1)}, bf16[512,2,128]{2,1,0:T(2,128)(2,1)}, u32[]{:S(2)}) copy-start(bf16[512,2,128]{2,1,0:T(2,128)(2,1)} %param.9) | copy-start | bytes 786436
  8.0 97.8 %all-gather.4.cloned.1.call-start = ((), (), s32[]{:S(2)}) async-start(), calls=%async_computation.1 | async-start | bytes 10485760 | tf_op jit(solution)/shard_map/all_gather | solution.py:17
  8.7 104.8 %all-reduce.2.cloned.1.call-start = ((), (), s32[]{:S(2)}) async-start(), calls=%async_computation.3 | async-start | bytes 262144 | tf_op jit(solution)/shard_map/psum | solution.py:11
  9.3 337.6 %all-gather.6.cloned.1.call-start = ((), (), s32[]{:S(2)}) async-start(), calls=%async_computation.4 | async-start | bytes 4325376 | tf_op jit(solution)/shard_map/all_gather | solution.py:22
  11.0 102.6 %copy-start.1 = (bf16[1,256,2,128]{3,2,1,0:T(2,128)(2,1)S(1)}, bf16[1,256,2,128]{3,2,1,0:T(2,128)(2,1)}, u32[]{:S(2)}) copy-start(bf16[1,256,2,128]{3,2,1,0:T(2,128)(2,1)} %param.15) | copy-start | bytes 393220
  11.0 102.6 %copy-start.3 = (f32[256,2,128]{2,1,0:T(2,128)S(1)}, f32[256,2,128]{2,1,0:T(2,128)}, u32[]{:S(2)}) copy-start(f32[256,2,128]{2,1,0:T(2,128)} %param.13) | copy-start | bytes 786436
  11.0 102.6 %copy-start.4 = (f32[256,2,128]{2,1,0:T(2,128)S(1)}, f32[256,2,128]{2,1,0:T(2,128)}, u32[]{:S(2)}) copy-start(f32[256,2,128]{2,1,0:T(2,128)} %param.14) | copy-start | bytes 786436
  11.0 593.1 %reduce-scatter.2.cloned.1.call-start = ((), (), s32[]{:S(2)}) async-start(), calls=%async_computation.2 | async-start | bytes 4325376 | tf_op jit(solution)/shard_map/reduce_scatter | solution.py:27
  115.8 488.3 %copy-start.2 = (bf16[1,256,2,128]{3,2,1,0:T(2,128)(2,1)S(1)}, bf16[1,256,2,128]{3,2,1,0:T(2,128)(2,1)}, u32[]{:S(2)}) copy-start(bf16[1,256,2,128]{3,2,1,0:T(2,128)(2,1)} %param.10) | copy-start | bytes 393220
  115.8 488.3 %copy-start.5 = (f32[1,256,2,128]{3,2,1,0:T(2,128)S(1)}, f32[1,256,2,128]{3,2,1,0:T(2,128)}, u32[]{:S(2)}) copy-start(f32[1,256,2,128]{3,2,1,0:T(2,128)} %param.11) | copy-start | bytes 786436
  115.8 488.3 %copy-start.6 = (f32[1,256,2,128]{3,2,1,0:T(2,128)S(1)}, f32[1,256,2,128]{3,2,1,0:T(2,128)}, u32[]{:S(2)}) copy-start(f32[1,256,2,128]{3,2,1,0:T(2,128)} %param.12) | copy-start | bytes 786436
Sparse Core Ops, SparseCore 0:
  10.9 94.7 all-gather.3
  108.4 238.4 all-gather.5
  349.8 254.2 reduce-scatter.1
Sparse Core Ops, SparseCore 1:
  12.1 83.0 all-reduce.1
where the time goes:
time: 615 us
  waiting for transfers between devices  576 us (94%)
  between operations  15.3 us (2%)
  matrix products  14.6 us (2%)
    reduce_scatter x1, waiting for transfers between devices, body(): lax.psum_scatter(jnp.einsum('td,tkc->dkc', columns, cotangent, preferred_...  249 us
    all_gather x1, waiting for transfers between devices, body(): lax.all_gather(weights[0], 'fsdp', axis=0, tiled=True)  231 us
    all_gather x1, waiting for transfers between devices, body(): gathered = lax.all_gather(tokens, 'tensor', axis=0, tiled=True)  94.7 us
  transfers between devices with their start and end apart: 4, of which 3 were waited for; matrix products, arithmetic and copies ran while one was open for 3% of the time, Pallas kernels for 0%

commit v1 on v0

--- a/solution.py
+++ b/solution.py
@@ -3,36 +3,96 @@
 from jax import lax
 from jax.sharding import PartitionSpec as P
 
+NX, NZ, NY = 4, 8, 4
+
+
+def move_x(value, shift):
+    pairs = [(NZ * x + z, NZ * ((x + shift) % NX) + z) for x in range(NX) for z in range(NZ)]
+    return lax.ppermute(value, "fsdp", pairs)
+
+
+def move_z(value, shift):
+    pairs = [(NZ * x + z, NZ * x + (z + shift) % NZ) for x in range(NX) for z in range(NZ)]
+    return lax.ppermute(value, "fsdp", pairs)
+
+
+def move_y(value, shift):
+    return lax.ppermute(value, "tensor", [(y, (y + shift) % NY) for y in range(NY)])
+
 
 def body(
     tokens, cotangent, weights, first_moment, second_moment, frag_global, frag_moment, frag_local
 ):
+    rows, width = tokens.shape
+    depth = weights.shape[1]
+    columns = weights.shape[2] * weights.shape[3]
+    chunk = width // NX
+    x = lax.axis_index("fsdp") // NZ
+    z = lax.axis_index("fsdp") % NZ
+    y = lax.axis_index("tensor")
+
     local_float = frag_local[0].astype(jnp.float32)
-    summed = lax.psum(local_float.astype(jnp.bfloat16), "replica").astype(jnp.float32)
+    summed = lax.psum(frag_local[0], "replica").astype(jnp.float32)
     outer_step = frag_global - summed / lax.axis_size("replica")
     moment_next = 0.9 * frag_moment + outer_step
     global_next = frag_global - 0.7 * (outer_step + 0.9 * moment_next)
-    local_next = (0.5 * local_float + 0.5 * global_next).astype(jnp.bfloat16)
-    global_next, moment_next, local_next = (global_next, moment_next, local_next[None])
-    gathered = lax.all_gather(tokens, "tensor", axis=0, tiled=True)
-    columns = gathered
-    projected = jnp.einsum(
-        "td,dkc->tkc",
-        columns,
-        lax.all_gather(weights[0], "fsdp", axis=0, tiled=True),
-        preferred_element_type=jnp.float32,
+    local_next = (0.5 * local_float + 0.5 * global_next).astype(jnp.bfloat16)[None]
+
+    def gather_rows(j):
+        own = lax.dynamic_slice_in_dim(tokens, (x + j) % NX * chunk, chunk, axis=1)
+        before = move_y(own, 1)
+        after = move_y(own, -1)
+        first = move_y(before[: rows // 2], 1)
+        second = move_y(after[rows // 2 :], -1)
+        return jnp.concatenate([own, before, after, first, second], axis=0)
+
+    held = {j: gather_rows(j) for j in (2, 1, 3, 0)}
+    order = jnp.stack([y, (y + 3) % NY, (y + 1) % NY, (y + 2) % NY])
+    cot = cotangent.reshape(NY, rows, columns)[order].reshape(NY * rows, columns)
+
+    own = weights[0].reshape(depth, columns)
+    blocks = [own] + [move_z(own, -s) for s in range(1, NZ)]
+    blocks = jnp.concatenate(blocks + blocks, axis=0)
+    plane = lax.dynamic_slice_in_dim(blocks, (NZ - z) * depth, NZ * depth, axis=0)
+    plane_before = move_x(plane, 1)
+    plane_after = move_x(plane, -1)
+    half = NZ * depth // 2
+    plane_far = jnp.concatenate(
+        [move_x(plane_before[:half], 1), move_x(plane_after[half:], -1)], axis=0
     )
-    keys_values = projected.astype(jnp.bfloat16)
-    columns = gathered
-    gradient = lax.psum_scatter(
-        jnp.einsum("td,tkc->dkc", columns, cotangent, preferred_element_type=jnp.float32).astype(
-            jnp.bfloat16
-        ),
-        "fsdp",
-        scatter_dimension=0,
-        tiled=True,
-    ).astype(jnp.float32)
-    gradient = gradient[None]
+    planes = {0: plane, 1: plane_after, 2: plane_far, 3: plane_before}
+
+    def term(j):
+        return lax.dot_general(
+            held[j], cot, (((0,), (0,)), ((), ())), preferred_element_type=jnp.float32
+        ).astype(jnp.bfloat16)
+
+    far = term(2)
+    far_first = move_x(far[:half], 1)
+    far_second = move_x(far[half:], -1)
+    up = term(1)
+    up = jnp.concatenate([up[:half] + far_first, up[half:]], axis=0)
+    from_before = move_x(up, 1)
+    down = term(3)
+    down = jnp.concatenate([down[:half], down[half:] + far_second], axis=0)
+    from_after = move_x(down, -1)
+    mine = term(0).astype(jnp.float32)
+    mine = mine + from_before.astype(jnp.float32) + from_after.astype(jnp.float32)
+    sent = mine.astype(jnp.bfloat16)
+    gradient = lax.dynamic_slice_in_dim(mine, z * depth, depth, axis=0)
+    for s in range(1, NZ):
+        block = lax.dynamic_slice_in_dim(sent, (z + s) % NZ * depth, depth, axis=0)
+        gradient = gradient + move_z(block, s).astype(jnp.float32)
+
+    projected = sum(
+        jnp.dot(held[j], planes[j], preferred_element_type=jnp.float32) for j in (2, 1, 3, 0)
+    )
+    back = jnp.stack([(p - y) % NY for p in range(NY)])
+    place = jnp.array([0, 2, 3, 1])[back]
+    keys_values = projected.astype(jnp.bfloat16).reshape(NY, rows, columns)[place]
+    keys_values = keys_values.reshape(cotangent.shape)
+
+    gradient = gradient.reshape(first_moment.shape)
     first_next = 0.9 * first_moment + 0.1 * gradient
     second_next = 0.95 * second_moment + 0.05 * gradient * gradient
     weight_float = weights.astype(jnp.float32)

time: 615 us -> 303 us (0.49)
  the two profiles are of different devices: /device:TPU:16 before, /device:TPU:102 now
where the time goes in v1:
time: 303 us; the launch traced here: 301 us
  starting transfers between devices  154 us (51%)
  waiting for transfers between devices  81.4 us (27%)
  local copies, waits for them, and re-layouts  37.2 us (12%)
  between operations  15.3 us (5%)
  matrix products  7.42 us (2%)
  other arithmetic  5.79 us (2%)
    ppermute x14, starting transfers between devices, move_z(): return lax.ppermute(value, 'fsdp', pairs)  75.8 us
    ppermute x16, starting transfers between devices, move_y(): lax.ppermute(value, 'tensor', [(y, (y + shift) % NY) for y in range(NY)])  55.8 us
    ppermute x8, waiting for transfers between devices, move_x(): return lax.ppermute(value, 'fsdp', pairs)  38.1 us
    psum x1, waiting for transfers between devices, body(): summed = lax.psum(frag_local[0], 'replica').astype(jnp.float32)  32.4 us
    unnamed x49, local copies, waits for them, and re-layouts  26.3 us
    ppermute x8, starting transfers between devices, move_x(): return lax.ppermute(value, 'fsdp', pairs)  22.5 us
    ppermute x14, waiting for transfers between devices, move_z(): return lax.ppermute(value, 'fsdp', pairs)  10.8 us
  transfers between devices with their start and end apart: 39, of which 8 were waited for; matrix products, arithmetic and copies ran while one was open for 15% of the time, Pallas kernels for 0%

profile of v1, /device:TPU:102, one launch (start us, length us, event | category | flops | bytes accessed | tf_op | source)
XLA Modules:
  0.0 301.3 jit_solution(5730867594577048936)
XLA Ops:
  7.3 3.5 %constant_dynamic-update-slice_fusion.4 = (bf16[512,2048]{1,0:T(8,128)(2,1)}, bf16[128,2048]{1,0:T(8,128)(2,1)}, bf16[512,2048]{1,0:T(8,128)(2,1)}, bf16[128,204...) fusion(bf16[128,8192]{1,0:T(8,128)(2,1)} %param.9, ...), kind=kLoop, calls=%fused_computation.40 | loop fusion | bytes 6291472
  10.8 3.5 %collective-permute-start = (bf16[128,2048]{1,0:T(8,128)(2,1)}, bf16[128,2048]{1,0:T(8,128)(2,1)S(1)}, u32[]{:S(2)}, u32[]{:S(2)}) collective-permute-start(bf16[128,2048]{1,0:T(8,128)(2,1)} %get-tuple-element.14), channel_id=1, source_target_pairs={{0,1},{1,2},{2,3},{3,0},{4,5},{5,6},{6,7},{7,4},{8,9},{9,10},{10,1... | collective-permute-start | bytes 1572872 | tf_op jit(solution)/shard_map/ppermute | solution.py:20
  14.3 3.6 %collective-permute-start.1 = (bf16[128,2048]{1,0:T(8,128)(2,1)}, bf16[128,2048]{1,0:T(8,128)(2,1)S(1)}, u32[]{:S(2)}, u32[]{:S(2)}) collective-permute-start(bf16[128,2048]{1,0:T(8,128)(2,1)} %get-tuple-element.14), channel_id=1, source_target_pairs={{0,3},{1,0},{2,1},{3,2},{4,7},{5,4},{6,5},{7,6},{8,11},{9,8},{10,9... | collective-permute-start | bytes 1572872 | tf_op jit(solution)/shard_map/ppermute | solution.py:20
  18.6 2.0 collective-permute-start.4
  20.6 1.9 collective-permute-start.5
  22.5 12.3 %collective-permute-start.6 = (bf16[256,256]{1,0:T(8,128)(2,1)}, bf16[256,256]{1,0:T(8,128)(2,1)}, u32[]{:S(2)}, u32[]{:S(2)}) collective-permute-start(bf16[256,256]{1,0:T(8,128)(2,1)} %bitcast.46), channel_id=1, source_target_pairs={{0,20},{4,24},{8,28},{12,0},{16,4},{20,8},{24,12},{28,16},{32,52},... | collective-permute-start | bytes 393224 | tf_op jit(solution)/shard_map/ppermute | solution.py:16
  37.3 1.5 gather_fusion.2
  38.9 3.6 %collective-permute-start.7 = (bf16[256,256]{1,0:T(8,128)(2,1)}, bf16[256,256]{1,0:T(8,128)(2,1)S(1)}, u32[]{:S(2)}, u32[]{:S(2)}) collective-permute-start(bf16[256,256]{1,0:T(8,128)(2,1)} %bitcast.46), channel_id=1, source_target_pairs={{0,16},{4,20},{8,24},{12,28},{16,0},{20,4},{24,8},{28,12},{32,48},... | collective-permute-start | bytes 393224 | tf_op jit(solution)/shard_map/ppermute | solution.py:16
  42.5 1.6 constant_dynamic-update-slice_fusion.19
  44.1 5.2 %collective-permute-start.8 = (bf16[256,256]{1,0:T(8,128)(2,1)}, bf16[256,256]{1,0:T(8,128)(2,1)S(1)}, u32[]{:S(2)}, u32[]{:S(2)}) collective-permute-start(bf16[256,256]{1,0:T(8,128)(2,1)} %bitcast.46), channel_id=1, source_target_pairs={{0,12},{4,16},{8,20},{12,24},{16,28},{20,0},{24,4},{28,8},{32,44},... | collective-permute-start | bytes 393224 | tf_op jit(solution)/shard_map/ppermute | solution.py:16
  49.4 1.6 constant_dynamic-update-slice_fusion.18
  50.9 5.6 %collective-permute-start.9 = (bf16[256,256]{1,0:T(8,128)(2,1)}, bf16[256,256]{1,0:T(8,128)(2,1)S(1)}, u32[]{:S(2)}, u32[]{:S(2)}) collective-permute-start(bf16[256,256]{1,0:T(8,128)(2,1)} %bitcast.46), channel_id=1, source_target_pairs={{0,8},{4,12},{8,16},{12,20},{16,24},{20,28},{24,0},{28,4},{32,40},... | collective-permute-start | bytes 393224 | tf_op jit(solution)/shard_map/ppermute | solution.py:16
  56.5 1.6 constant_dynamic-update-slice_fusion.17
  58.1 14.7 %collective-permute-start.10 = (bf16[256,256]{1,0:T(8,128)(2,1)}, bf16[256,256]{1,0:T(8,128)(2,1)S(1)}, u32[]{:S(2)}, u32[]{:S(2)}) collective-permute-start(bf16[256,256]{1,0:T(8,128)(2,1)} %bitcast.46), channel_id=1, source_target_pairs={{0,4},{4,8},{8,12},{12,16},{16,20},{20,24},{24,28},{28,0},{32,36},... | collective-permute-start | bytes 393224 | tf_op jit(solution)/shard_map/ppermute | solution.py:16
  73.5 1.9 collective-permute-start.15
  76.1 5.1 %collective-permute-start.16 = (bf16[128,2048]{1,0:T(8,128)(2,1)}, bf16[128,2048]{1,0:T(8,128)(2,1)}, u32[]{:S(2)}, u32[]{:S(2)}) collective-permute-start(bf16[128,2048]{1,0:T(8,128)(2,1)} %get-tuple-element.22), channel_id=1, source_target_pairs={{0,3},{1,0},{2,1},{3,2},{4,7},{5,4},{6,5},{7,6},{8,11},{9,8},{10,9... | collective-permute-start | bytes 1572872 | tf_op jit(solution)/shard_map/ppermute | solution.py:20
  81.8 1.9 collective-permute-start.19
  85.1 1.6 constant_dynamic-update-slice_fusion.11
  86.6 1.6 constant_dynamic-update-slice_fusion.10
  88.2 1.6 constant_dynamic-update-slice_fusion.9
  92.4 2.3 constant_dynamic-slice_fusion.10
  94.7 32.4 %all-reduce.2.cloned.1.call-done = bf16[256,2,128]{2,1,0:T(2,128)(2,1)} async-done(((bf16[256,2,128]{2,1,0:T(2,128)(2,1)}), bf16[256,2,128]{2,1,0:T(2,128)(2,1)}) %all-reduce.2.cloned.1.call-update) | async-done | bytes 131088 | tf_op jit(solution)/shard_map/psum | solution.py:35
  127.1 2.5 fusion.13
  129.6 4.6 %collective-permute-start.20 = (bf16[128,2048]{1,0:T(8,128)(2,1)}, bf16[128,2048]{1,0:T(8,128)(2,1)S(1)}, u32[]{:S(2)}, u32[]{:S(2)}) collective-permute-start(bf16[128,2048]{1,0:T(8,128)(2,1)} %get-tuple-element.26), channel_id=1, source_target_pairs={{0,3},{1,0},{2,1},{3,2},{4,7},{5,4},{6,5},{7,6},{8,11},{9,8},{10,9... | collective-permute-start | bytes 1572872 | tf_op jit(solution)/shard_map/ppermute | solution.py:20
  135.1 1.9 collective-permute-start.23
  137.9 5.1 %collective-permute-start.24 = (bf16[128,2048]{1,0:T(8,128)(2,1)S(1)}, bf16[128,2048]{1,0:T(8,128)(2,1)S(1)}, u32[]{:S(2)}, u32[]{:S(2)}) collective-permute-start(bf16[128,2048]{1,0:T(8,128)(2,1)S(1)} %copy-done.3), channel_id=1, source_target_pairs={{0,3},{1,0},{2,1},{3,2},{4,7},{5,4},{6,5},{7,6},{8,11},{9,8},{10,9... | collective-permute-start | bytes 1572872 | tf_op jit(solution)/shard_map/ppermute | solution.py:20
  143.0 1.9 constant_dynamic-update-slice_fusion.24
  144.9 2.7 collective-permute-start.13
  147.7 1.9 constant_dynamic-update-slice_fusion.23
  149.5 4.3 %collective-permute-start.11 = (bf16[2048,256]{1,0:T(8,128)(2,1)S(1)}, bf16[2048,256]{1,0:T(8,128)(2,1)S(1)}, u32[]{:S(2)}, u32[]{:S(2)}) collective-permute-start(bf16[2048,256]{1,0:T(8,128)(2,1)S(1)} %copy-done.2), channel_id=1, source_target_pairs={{0,32},{4,36},{8,40},{12,44},{16,48},{20,52},{24,56},{28,60},{32,6... | collective-permute-start | bytes 3145736 | tf_op jit(solution)/shard_map/ppermute | solution.py:11
  153.8 1.1 constant_dynamic-update-slice_fusion.29
  155.0 1.9 collective-permute-start.2
  157.0 5.1 %collective-permute-start.3 = (bf16[64,2048]{1,0:T(8,128)(2,1)S(1)}, bf16[64,2048]{1,0:T(8,128)(2,1)S(1)}, u32[]{:S(2)}, u32[]{:S(2)}) collective-permute-start(bf16[64,2048]{1,0:T(8,128)(2,1)S(1)} %slice.71), channel_id=1, source_target_pairs={{0,3},{1,0},{2,1},{3,2},{4,7},{5,4},{6,5},{7,6},{8,11},{9,8},{10,9... | collective-permute-start | bytes 786440 | tf_op jit(solution)/shard_map/ppermute | solution.py:20
  162.2 1.1 slice.74
  163.3 1.9 collective-permute-start.17
  165.3 1.0 slice.75
  167.3 5.1 %collective-permute-start.18 = (bf16[64,2048]{1,0:T(8,128)(2,1)S(1)}, bf16[64,2048]{1,0:T(8,128)(2,1)S(1)}, u32[]{:S(2)}, u32[]{:S(2)}) collective-permute-start(bf16[64,2048]{1,0:T(8,128)(2,1)S(1)} %slice.75), channel_id=1, source_target_pairs={{0,3},{1,0},{2,1},{3,2},{4,7},{5,4},{6,5},{7,6},{8,11},{9,8},{10,9... | collective-permute-start | bytes 786440 | tf_op jit(solution)/shard_map/ppermute | solution.py:20
  172.5 1.9 collective-permute-start.21
  175.2 5.1 %collective-permute-start.22 = (bf16[64,2048]{1,0:T(8,128)(2,1)S(1)}, bf16[64,2048]{1,0:T(8,128)(2,1)S(1)}, u32[]{:S(2)}, u32[]{:S(2)}) collective-permute-start(bf16[64,2048]{1,0:T(8,128)(2,1)S(1)} %slice.77), channel_id=1, source_target_pairs={{0,3},{1,0},{2,1},{3,2},{4,7},{5,4},{6,5},{7,6},{8,11},{9,8},{10,9... | collective-permute-start | bytes 786440 | tf_op jit(solution)/shard_map/ppermute | solution.py:20
  180.4 1.9 collective-permute-start.25
  183.2 5.1 %collective-permute-start.26 = (bf16[64,2048]{1,0:T(8,128)(2,1)S(1)}, bf16[64,2048]{1,0:T(8,128)(2,1)S(1)}, u32[]{:S(2)}, u32[]{:S(2)}) collective-permute-start(bf16[64,2048]{1,0:T(8,128)(2,1)S(1)} %slice.79), channel_id=1, source_target_pairs={{0,3},{1,0},{2,1},{3,2},{4,7},{5,4},{6,5},{7,6},{8,11},{9,8},{10,9... | collective-permute-start | bytes 786440 | tf_op jit(solution)/shard_map/ppermute | solution.py:20
  188.4 1.9 collective-permute-start.27
  191.2 9.7 %collective-permute-done.27 = bf16[1024,256]{0,1:T(8,128)(2,1)S(1)} collective-permute-done((bf16[1024,256]{0,1:T(8,128)(2,1)S(1)}, bf16[1024,256]{0,1:T(8,128)(2,1)S(1)}, u32[]{:S(2)}, u32[]{:S(2)}) %collective-permute-start.27) | collective-permute-done | bytes 524320 | tf_op jit(solution)/shard_map/ppermute | solution.py:11
  200.9 1.9 collective-permute-start.29
  203.0 10.6 %collective-permute-done.29 = bf16[1024,256]{0,1:T(8,128)(2,1)S(1)} collective-permute-done((bf16[1024,256]{0,1:T(8,128)(2,1)S(1)}, bf16[1024,256]{0,1:T(8,128)(2,1)S(1)}, u32[]{:S(2)}, u32[]{:S(2)}) %collective-permute-start.29) | collective-permute-done | bytes 524320 | tf_op jit(solution)/shard_map/ppermute | solution.py:11
  213.6 2.5 collective-permute-start.28
  216.2 3.4 %collective-permute-start.30 = (bf16[2048,256]{0,1:T(8,128)(2,1)S(1)}, bf16[2048,256]{0,1:T(8,128)(2,1)S(1)}, u32[]{:S(2)}, u32[]{:S(2)}) collective-permute-start(bf16[2048,256]{0,1:T(8,128)(2,1)S(1)} %pad_maximum_fusion.1), channel_id=1, source_target_pairs={{0,96},{4,100},{8,104},{12,108},{16,112},{20,116},{24,120},{28,124... | collective-permute-start | bytes 3145736 | tf_op jit(solution)/shard_map/ppermute | solution.py:11
  220.5 3.7 %collective-permute-start.12 = (bf16[1024,256]{1,0:T(8,128)(2,1)S(1)}, bf16[1024,256]{1,0:T(8,128)(2,1)S(1)}, u32[]{:S(2)}, u32[]{:S(2)}) collective-permute-start(bf16[1024,256]{1,0:T(8,128)(2,1)S(1)} %slice.72), channel_id=1, source_target_pairs={{0,32},{4,36},{8,40},{12,44},{16,48},{20,52},{24,56},{28,60},{32,6... | collective-permute-start | bytes 1572872 | tf_op jit(solution)/shard_map/ppermute | solution.py:11
  224.2 2.2 collective-permute-start.14
  227.1 13.9 %collective-permute-done.28 = bf16[2048,256]{0,1:T(8,128)(2,1)S(1)} collective-permute-done((bf16[2048,256]{0,1:T(8,128)(2,1)S(1)}, bf16[2048,256]{0,1:T(8,128)(2,1)S(1)}, u32[]{:S(2)}, u32[]{:S(2)}) %collective-permute-start.28) | collective-permute-done | bytes 1048608 | tf_op jit(solution)/shard_map/ppermute | solution.py:11
  241.0 3.9 %collective-permute-done.30 = bf16[2048,256]{0,1:T(8,128)(2,1)S(1)} collective-permute-done((bf16[2048,256]{0,1:T(8,128)(2,1)S(1)}, bf16[2048,256]{0,1:T(8,128)(2,1)S(1)}, u32[]{:S(2)}, u32[]{:S(2)}) %collective-permute-start.30) | collective-permute-done | bytes 1048608 | tf_op jit(solution)/shard_map/ppermute | solution.py:11
  244.9 2.3 fusion.21
  247.3 2.5 collective-permute-start.31
  249.8 2.7 collective-permute-start.32
  253.2 8.6 %collective-permute-start.33 = (bf16[256,256]{0,1:T(8,128)(2,1)S(1)}, bf16[256,256]{0,1:T(8,128)(2,1)S(1)}, u32[]{:S(2)}, u32[]{:S(2)}) collective-permute-start(bf16[256,256]{0,1:T(8,128)(2,1)S(1)} %get-tuple-element.32), channel_id=1, source_target_pairs={{0,12},{4,16},{8,20},{12,24},{16,28},{20,0},{24,4},{28,8},{32,44},... | collective-permute-start | bytes 393224 | tf_op jit(solution)/shard_map/ppermute | solution.py:16
  261.8 2.2 collective-permute-start.34
  264.0 5.7 %collective-permute-start.35 = (bf16[256,256]{0,1:T(8,128)(2,1)S(1)}, bf16[256,256]{0,1:T(8,128)(2,1)S(1)}, u32[]{:S(2)}, u32[]{:S(2)}) collective-permute-start(bf16[256,256]{0,1:T(8,128)(2,1)S(1)} %get-tuple-element.30), channel_id=1, source_target_pairs={{0,20},{4,24},{8,28},{12,0},{16,4},{20,8},{24,12},{28,16},{32,52},... | collective-permute-start | bytes 393224 | tf_op jit(solution)/shard_map/ppermute | solution.py:16
  269.7 6.9 %collective-permute-start.36 = (bf16[256,256]{0,1:T(8,128)(2,1)S(1)}, bf16[256,256]{0,1:T(8,128)(2,1)S(1)}, u32[]{:S(2)}, u32[]{:S(2)}) collective-permute-start(bf16[256,256]{0,1:T(8,128)(2,1)S(1)} %get-tuple-element.29), channel_id=1, source_target_pairs={{0,24},{4,28},{8,0},{12,4},{16,8},{20,12},{24,16},{28,20},{32,56},... | collective-permute-start | bytes 393224 | tf_op jit(solution)/shard_map/ppermute | solution.py:16
  276.7 1.9 collective-permute-start.37
  280.7 6.9 %collective-permute-done.33 = bf16[256,256]{0,1:T(8,128)(2,1)S(1)} collective-permute-done((bf16[256,256]{0,1:T(8,128)(2,1)S(1)}, bf16[256,256]{0,1:T(8,128)(2,1)S(1)}, u32[]{:S(2)}, u32[]{:S(2)}) %collective-permute-start.33) | collective-permute-done | bytes 131104 | tf_op jit(solution)/shard_map/ppermute | solution.py:16
  287.5 1.4 collective-permute-done.34
  288.9 2.5 collective-permute-done.37
  291.4 1.1 convert_add_fusion
  292.7 1.7 fusion.12
  (108 shorter events, 19.4 us)
Async XLA Ops:
  7.2 119.9 %all-reduce.2.cloned.1.call-start = ((), (), s32[]{:S(2)}) async-start(), calls=%async_computation | async-start | bytes 262144 | tf_op jit(solution)/shard_map/psum | solution.py:35
  7.3 10.6 %copy-start.1 = (bf16[1,256,2,128]{3,2,1,0:T(2,128)(2,1)S(1)}, bf16[1,256,2,128]{3,2,1,0:T(2,128)(2,1)}, u32[]{:S(2)}) copy-start(bf16[1,256,2,128]{3,2,1,0:T(2,128)(2,1)} %param.11) | copy-start | bytes 393220
  7.3 28.3 %copy-start = (s32[4]{0:T(128)S(1)}, s32[4]{0:T(128)}, u32[]{:S(2)}) copy-start(s32[4]{0:T(128)} %constant.160.clone) | copy-start | bytes 52
  7.3 29.1 %copy-start.4 = (bf16[512,2,128]{2,1,0:T(2,128)(2,1)S(1)}, bf16[512,2,128]{2,1,0:T(2,128)(2,1)}, u32[]{:S(2)}) copy-start(bf16[512,2,128]{2,1,0:T(2,128)(2,1)} %param.10) | copy-start | bytes 786436
  10.8 118.8 %collective-permute-start = (bf16[128,2048]{1,0:T(8,128)(2,1)}, bf16[128,2048]{1,0:T(8,128)(2,1)S(1)}, u32[]{:S(2)}, u32[]{:S(2)}) collective-permute-start(bf16[128,2048]{1,0:T(8,128)(2,1)} %get-tuple-element.14), channel_id=1, source_target_pairs={{0,1},{1,2},{2,3},{3,0},{4,5},{5,6},{6,7},{7,4},{8,9},{9,10},{10,1... | collective-permute-start | bytes 1572872 | tf_op jit(solution)/shard_map/ppermute | solution.py:20
  14.3 120.8 %collective-permute-start.1 = (bf16[128,2048]{1,0:T(8,128)(2,1)}, bf16[128,2048]{1,0:T(8,128)(2,1)S(1)}, u32[]{:S(2)}, u32[]{:S(2)}) collective-permute-start(bf16[128,2048]{1,0:T(8,128)(2,1)} %get-tuple-element.14), channel_id=1, source_target_pairs={{0,3},{1,0},{2,1},{3,2},{4,7},{5,4},{6,5},{7,6},{8,11},{9,8},{10,9... | collective-permute-start | bytes 1572872 | tf_op jit(solution)/shard_map/ppermute | solution.py:20
  18.6 20.3 %collective-permute-start.4 = (bf16[256,256]{1,0:T(8,128)(2,1)}, bf16[256,256]{1,0:T(8,128)(2,1)}, u32[]{:S(2)}, u32[]{:S(2)}) collective-permute-start(bf16[256,256]{1,0:T(8,128)(2,1)} %bitcast.46), channel_id=1, source_target_pairs={{0,28},{4,0},{8,4},{12,8},{16,12},{20,16},{24,20},{28,24},{32,60},... | collective-permute-start | bytes 393224 | tf_op jit(solution)/shard_map/ppermute | solution.py:16
  20.6 23.5 %collective-permute-start.5 = (bf16[256,256]{1,0:T(8,128)(2,1)}, bf16[256,256]{1,0:T(8,128)(2,1)}, u32[]{:S(2)}, u32[]{:S(2)}) collective-permute-start(bf16[256,256]{1,0:T(8,128)(2,1)} %bitcast.46), channel_id=1, source_target_pairs={{0,24},{4,28},{8,0},{12,4},{16,8},{20,12},{24,16},{28,20},{32,56},... | collective-permute-start | bytes 393224 | tf_op jit(solution)/shard_map/ppermute | solution.py:16
  22.5 28.4 %collective-permute-start.6 = (bf16[256,256]{1,0:T(8,128)(2,1)}, bf16[256,256]{1,0:T(8,128)(2,1)}, u32[]{:S(2)}, u32[]{:S(2)}) collective-permute-start(bf16[256,256]{1,0:T(8,128)(2,1)} %bitcast.46), channel_id=1, source_target_pairs={{0,20},{4,24},{8,28},{12,0},{16,4},{20,8},{24,12},{28,16},{32,52},... | collective-permute-start | bytes 393224 | tf_op jit(solution)/shard_map/ppermute | solution.py:16
  38.9 19.1 %collective-permute-start.7 = (bf16[256,256]{1,0:T(8,128)(2,1)}, bf16[256,256]{1,0:T(8,128)(2,1)S(1)}, u32[]{:S(2)}, u32[]{:S(2)}) collective-permute-start(bf16[256,256]{1,0:T(8,128)(2,1)} %bitcast.46), channel_id=1, source_target_pairs={{0,16},{4,20},{8,24},{12,28},{16,0},{20,4},{24,8},{28,12},{32,48},... | collective-permute-start | bytes 393224 | tf_op jit(solution)/shard_map/ppermute | solution.py:16
  44.1 29.3 %collective-permute-start.8 = (bf16[256,256]{1,0:T(8,128)(2,1)}, bf16[256,256]{1,0:T(8,128)(2,1)S(1)}, u32[]{:S(2)}, u32[]{:S(2)}) collective-permute-start(bf16[256,256]{1,0:T(8,128)(2,1)} %bitcast.46), channel_id=1, source_target_pairs={{0,12},{4,16},{8,20},{12,24},{16,28},{20,0},{24,4},{28,8},{32,44},... | collective-permute-start | bytes 393224 | tf_op jit(solution)/shard_map/ppermute | solution.py:16
  50.9 25.1 %collective-permute-start.9 = (bf16[256,256]{1,0:T(8,128)(2,1)}, bf16[256,256]{1,0:T(8,128)(2,1)S(1)}, u32[]{:S(2)}, u32[]{:S(2)}) collective-permute-start(bf16[256,256]{1,0:T(8,128)(2,1)} %bitcast.46), channel_id=1, source_target_pairs={{0,8},{4,12},{8,16},{12,20},{16,24},{20,28},{24,0},{28,4},{32,40},... | collective-permute-start | bytes 393224 | tf_op jit(solution)/shard_map/ppermute | solution.py:16
  58.1 23.8 %collective-permute-start.10 = (bf16[256,256]{1,0:T(8,128)(2,1)}, bf16[256,256]{1,0:T(8,128)(2,1)S(1)}, u32[]{:S(2)}, u32[]{:S(2)}) collective-permute-start(bf16[256,256]{1,0:T(8,128)(2,1)} %bitcast.46), channel_id=1, source_target_pairs={{0,4},{4,8},{8,12},{12,16},{16,20},{20,24},{24,28},{28,0},{32,36},... | collective-permute-start | bytes 393224 | tf_op jit(solution)/shard_map/ppermute | solution.py:16
  73.5 64.5 %collective-permute-start.15 = (bf16[128,2048]{1,0:T(8,128)(2,1)}, bf16[128,2048]{1,0:T(8,128)(2,1)}, u32[]{:S(2)}, u32[]{:S(2)}) collective-permute-start(bf16[128,2048]{1,0:T(8,128)(2,1)} %get-tuple-element.22), channel_id=1, source_target_pairs={{0,1},{1,2},{2,3},{3,0},{4,5},{5,6},{6,7},{7,4},{8,9},{9,10},{10,1... | collective-permute-start | bytes 1572872 | tf_op jit(solution)/shard_map/ppermute | solution.py:20
  76.1 68.9 %collective-permute-start.16 = (bf16[128,2048]{1,0:T(8,128)(2,1)}, bf16[128,2048]{1,0:T(8,128)(2,1)}, u32[]{:S(2)}, u32[]{:S(2)}) collective-permute-start(bf16[128,2048]{1,0:T(8,128)(2,1)} %get-tuple-element.22), channel_id=1, source_target_pairs={{0,3},{1,0},{2,1},{3,2},{4,7},{5,4},{6,5},{7,6},{8,11},{9,8},{10,9... | collective-permute-start | bytes 1572872 | tf_op jit(solution)/shard_map/ppermute | solution.py:20
  81.8 67.7 %collective-permute-start.19 = (bf16[128,2048]{1,0:T(8,128)(2,1)}, bf16[128,2048]{1,0:T(8,128)(2,1)}, u32[]{:S(2)}, u32[]{:S(2)}) collective-permute-start(bf16[128,2048]{1,0:T(8,128)(2,1)} %get-tuple-element.26), channel_id=1, source_target_pairs={{0,1},{1,2},{2,3},{3,0},{4,5},{5,6},{6,7},{7,4},{8,9},{9,10},{10,1... | collective-permute-start | bytes 1572872 | tf_op jit(solution)/shard_map/ppermute | solution.py:20
  127.1 8.1 %copy-start.3 = (bf16[128,2048]{1,0:T(8,128)(2,1)S(1)}, bf16[128,2048]{1,0:T(8,128)(2,1)}, u32[]{:S(2)}) copy-start(bf16[128,2048]{1,0:T(8,128)(2,1)} %get-tuple-element.24) | copy-start | bytes 1572868
  127.1 17.8 %copy-start.2 = (bf16[2048,256]{1,0:T(8,128)(2,1)S(1)}, bf16[2048,256]{1,0:T(8,128)(2,1)}, u32[]{:S(2)}) copy-start(bf16[2048,256]{1,0:T(8,128)(2,1)} %constant_dynamic-slice_fusion.10) | copy-start | bytes 3145732
  129.6 25.4 %collective-permute-start.20 = (bf16[128,2048]{1,0:T(8,128)(2,1)}, bf16[128,2048]{1,0:T(8,128)(2,1)S(1)}, u32[]{:S(2)}, u32[]{:S(2)}) collective-permute-start(bf16[128,2048]{1,0:T(8,128)(2,1)} %get-tuple-element.26), channel_id=1, source_target_pairs={{0,3},{1,0},{2,1},{3,2},{4,7},{5,4},{6,5},{7,6},{8,11},{9,8},{10,9... | collective-permute-start | bytes 1572872 | tf_op jit(solution)/shard_map/ppermute | solution.py:20
  134.3 19.6 %copy-start.7 = (bf16[512,2048]{1,0:T(8,128)(2,1)S(1)}, bf16[512,2048]{1,0:T(8,128)(2,1)}, u32[]{:S(2)}) copy-start(bf16[512,2048]{1,0:T(8,128)(2,1)} %get-tuple-element.25) | copy-start | bytes 6291460
  135.1 21.9 %collective-permute-start.23 = (bf16[128,2048]{1,0:T(8,128)(2,1)S(1)}, bf16[128,2048]{1,0:T(8,128)(2,1)S(1)}, u32[]{:S(2)}, u32[]{:S(2)}) collective-permute-start(bf16[128,2048]{1,0:T(8,128)(2,1)S(1)} %copy-done.3), channel_id=1, source_target_pairs={{0,1},{1,2},{2,3},{3,0},{4,5},{5,6},{6,7},{7,4},{8,9},{9,10},{10,1... | collective-permute-start | bytes 1572872 | tf_op jit(solution)/shard_map/ppermute | solution.py:20
  137.9 25.4 %collective-permute-start.24 = (bf16[128,2048]{1,0:T(8,128)(2,1)S(1)}, bf16[128,2048]{1,0:T(8,128)(2,1)S(1)}, u32[]{:S(2)}, u32[]{:S(2)}) collective-permute-start(bf16[128,2048]{1,0:T(8,128)(2,1)S(1)} %copy-done.3), channel_id=1, source_target_pairs={{0,3},{1,0},{2,1},{3,2},{4,7},{5,4},{6,5},{7,6},{8,11},{9,8},{10,9... | collective-permute-start | bytes 1572872 | tf_op jit(solution)/shard_map/ppermute | solution.py:20
  144.9 79.2 %collective-permute-start.13 = (bf16[2048,256]{1,0:T(8,128)(2,1)S(1)}, bf16[2048,256]{1,0:T(8,128)(2,1)S(1)}, u32[]{:S(2)}, u32[]{:S(2)}) collective-permute-start(bf16[2048,256]{1,0:T(8,128)(2,1)S(1)} %copy-done.2), channel_id=1, source_target_pairs={{0,96},{4,100},{8,104},{12,108},{16,112},{20,116},{24,120},{28,124... | collective-permute-start | bytes 3145736 | tf_op jit(solution)/shard_map/ppermute | solution.py:11
  149.5 70.9 %collective-permute-start.11 = (bf16[2048,256]{1,0:T(8,128)(2,1)S(1)}, bf16[2048,256]{1,0:T(8,128)(2,1)S(1)}, u32[]{:S(2)}, u32[]{:S(2)}) collective-permute-start(bf16[2048,256]{1,0:T(8,128)(2,1)S(1)} %copy-done.2), channel_id=1, source_target_pairs={{0,32},{4,36},{8,40},{12,44},{16,48},{20,52},{24,56},{28,60},{32,6... | collective-permute-start | bytes 3145736 | tf_op jit(solution)/shard_map/ppermute | solution.py:11
  155.0 12.3 %collective-permute-start.2 = (bf16[64,2048]{1,0:T(8,128)(2,1)S(1)}, bf16[64,2048]{1,0:T(8,128)(2,1)S(1)}, u32[]{:S(2)}, u32[]{:S(2)}) collective-permute-start(bf16[64,2048]{1,0:T(8,128)(2,1)S(1)} %slice.70), channel_id=1, source_target_pairs={{0,1},{1,2},{2,3},{3,0},{4,5},{5,6},{6,7},{7,4},{8,9},{9,10},{10,1... | collective-permute-start | bytes 786440 | tf_op jit(solution)/shard_map/ppermute | solution.py:20
  157.0 15.5 %collective-permute-start.3 = (bf16[64,2048]{1,0:T(8,128)(2,1)S(1)}, bf16[64,2048]{1,0:T(8,128)(2,1)S(1)}, u32[]{:S(2)}, u32[]{:S(2)}) collective-permute-start(bf16[64,2048]{1,0:T(8,128)(2,1)S(1)} %slice.71), channel_id=1, source_target_pairs={{0,3},{1,0},{2,1},{3,2},{4,7},{5,4},{6,5},{7,6},{8,11},{9,8},{10,9... | collective-permute-start | bytes 786440 | tf_op jit(solution)/shard_map/ppermute | solution.py:20
  162.2 10.3 %copy-start.9 = (bf16[512,2048]{1,0:T(8,128)(2,1)S(1)}, bf16[512,2048]{1,0:T(8,128)(2,1)}, u32[]{:S(2)}) copy-start(bf16[512,2048]{1,0:T(8,128)(2,1)} %constant_dynamic-update-slice_fusion.2) | copy-start | bytes 6291460
  163.3 11.9 %collective-permute-start.17 = (bf16[64,2048]{1,0:T(8,128)(2,1)S(1)}, bf16[64,2048]{1,0:T(8,128)(2,1)S(1)}, u32[]{:S(2)}, u32[]{:S(2)}) collective-permute-start(bf16[64,2048]{1,0:T(8,128)(2,1)S(1)} %slice.74), channel_id=1, source_target_pairs={{0,1},{1,2},{2,3},{3,0},{4,5},{5,6},{6,7},{7,4},{8,9},{9,10},{10,1... | collective-permute-start | bytes 786440 | tf_op jit(solution)/shard_map/ppermute | solution.py:20
  167.3 13.1 %collective-permute-start.18 = (bf16[64,2048]{1,0:T(8,128)(2,1)S(1)}, bf16[64,2048]{1,0:T(8,128)(2,1)S(1)}, u32[]{:S(2)}, u32[]{:S(2)}) collective-permute-start(bf16[64,2048]{1,0:T(8,128)(2,1)S(1)} %slice.75), channel_id=1, source_target_pairs={{0,3},{1,0},{2,1},{3,2},{4,7},{5,4},{6,5},{7,6},{8,11},{9,8},{10,9... | collective-permute-start | bytes 786440 | tf_op jit(solution)/shard_map/ppermute | solution.py:20
  172.5 10.7 %collective-permute-start.21 = (bf16[64,2048]{1,0:T(8,128)(2,1)S(1)}, bf16[64,2048]{1,0:T(8,128)(2,1)S(1)}, u32[]{:S(2)}, u32[]{:S(2)}) collective-permute-start(bf16[64,2048]{1,0:T(8,128)(2,1)S(1)} %slice.76), channel_id=1, source_target_pairs={{0,1},{1,2},{2,3},{3,0},{4,5},{5,6},{6,7},{7,4},{8,9},{9,10},{10,1... | collective-permute-start | bytes 786440 | tf_op jit(solution)/shard_map/ppermute | solution.py:20
  174.5 5.9 %copy-start.8 = (bf16[512,2048]{1,0:T(8,128)(2,1)S(1)}, bf16[512,2048]{1,0:T(8,128)(2,1)}, u32[]{:S(2)}) copy-start(bf16[512,2048]{1,0:T(8,128)(2,1)} %constant_dynamic-update-slice_fusion.23) | copy-start | bytes 6291460
  175.2 13.2 %collective-permute-start.22 = (bf16[64,2048]{1,0:T(8,128)(2,1)S(1)}, bf16[64,2048]{1,0:T(8,128)(2,1)S(1)}, u32[]{:S(2)}, u32[]{:S(2)}) collective-permute-start(bf16[64,2048]{1,0:T(8,128)(2,1)S(1)} %slice.77), channel_id=1, source_target_pairs={{0,3},{1,0},{2,1},{3,2},{4,7},{5,4},{6,5},{7,6},{8,11},{9,8},{10,9... | collective-permute-start | bytes 786440 | tf_op jit(solution)/shard_map/ppermute | solution.py:20
  180.4 35.8 %collective-permute-start.25 = (bf16[64,2048]{1,0:T(8,128)(2,1)S(1)}, bf16[64,2048]{1,0:T(8,128)(2,1)S(1)}, u32[]{:S(2)}, u32[]{:S(2)}) collective-permute-start(bf16[64,2048]{1,0:T(8,128)(2,1)S(1)} %slice.78), channel_id=1, source_target_pairs={{0,1},{1,2},{2,3},{3,0},{4,5},{5,6},{6,7},{7,4},{8,9},{9,10},{10,1... | collective-permute-start | bytes 786440 | tf_op jit(solution)/shard_map/ppermute | solution.py:20
  183.2 36.5 %collective-permute-start.26 = (bf16[64,2048]{1,0:T(8,128)(2,1)S(1)}, bf16[64,2048]{1,0:T(8,128)(2,1)S(1)}, u32[]{:S(2)}, u32[]{:S(2)}) collective-permute-start(bf16[64,2048]{1,0:T(8,128)(2,1)S(1)} %slice.79), channel_id=1, source_target_pairs={{0,3},{1,0},{2,1},{3,2},{4,7},{5,4},{6,5},{7,6},{8,11},{9,8},{10,9... | collective-permute-start | bytes 786440 | tf_op jit(solution)/shard_map/ppermute | solution.py:20
  188.4 12.4 %collective-permute-start.27 = (bf16[1024,256]{0,1:T(8,128)(2,1)S(1)}, bf16[1024,256]{0,1:T(8,128)(2,1)S(1)}, u32[]{:S(2)}, u32[]{:S(2)}) collective-permute-start(bf16[1024,256]{0,1:T(8,128)(2,1)S(1)} %get-tuple-element.36), channel_id=1, source_target_pairs={{0,32},{4,36},{8,40},{12,44},{16,48},{20,52},{24,56},{28,60},{32,6... | collective-permute-start | bytes 1572872 | tf_op jit(solution)/shard_map/ppermute | solution.py:11
  200.9 12.7 %collective-permute-start.29 = (bf16[1024,256]{0,1:T(8,128)(2,1)S(1)}, bf16[1024,256]{0,1:T(8,128)(2,1)S(1)}, u32[]{:S(2)}, u32[]{:S(2)}) collective-permute-start(bf16[1024,256]{0,1:T(8,128)(2,1)S(1)} %get-tuple-element.37), channel_id=1, source_target_pairs={{0,96},{4,100},{8,104},{12,108},{16,112},{20,116},{24,120},{28,124... | collective-permute-start | bytes 1572872 | tf_op jit(solution)/shard_map/ppermute | solution.py:11
  213.6 27.4 %collective-permute-start.28 = (bf16[2048,256]{0,1:T(8,128)(2,1)S(1)}, bf16[2048,256]{0,1:T(8,128)(2,1)S(1)}, u32[]{:S(2)}, u32[]{:S(2)}) collective-permute-start(bf16[2048,256]{0,1:T(8,128)(2,1)S(1)} %pad_maximum_fusion), channel_id=1, source_target_pairs={{0,32},{4,36},{8,40},{12,44},{16,48},{20,52},{24,56},{28,60},{32,6... | collective-permute-start | bytes 3145736 | tf_op jit(solution)/shard_map/ppermute | solution.py:11
  216.2 28.7 %collective-permute-start.30 = (bf16[2048,256]{0,1:T(8,128)(2,1)S(1)}, bf16[2048,256]{0,1:T(8,128)(2,1)S(1)}, u32[]{:S(2)}, u32[]{:S(2)}) collective-permute-start(bf16[2048,256]{0,1:T(8,128)(2,1)S(1)} %pad_maximum_fusion.1), channel_id=1, source_target_pairs={{0,96},{4,100},{8,104},{12,108},{16,112},{20,116},{24,120},{28,124... | collective-permute-start | bytes 3145736 | tf_op jit(solution)/shard_map/ppermute | solution.py:11
  220.5 41.3 %collective-permute-start.12 = (bf16[1024,256]{1,0:T(8,128)(2,1)S(1)}, bf16[1024,256]{1,0:T(8,128)(2,1)S(1)}, u32[]{:S(2)}, u32[]{:S(2)}) collective-permute-start(bf16[1024,256]{1,0:T(8,128)(2,1)S(1)} %slice.72), channel_id=1, source_target_pairs={{0,32},{4,36},{8,40},{12,44},{16,48},{20,52},{24,56},{28,60},{32,6... | collective-permute-start | bytes 1572872 | tf_op jit(solution)/shard_map/ppermute | solution.py:11
  224.2 39.8 %collective-permute-start.14 = (bf16[1024,256]{1,0:T(8,128)(2,1)S(1)}, bf16[1024,256]{1,0:T(8,128)(2,1)S(1)}, u32[]{:S(2)}, u32[]{:S(2)}) collective-permute-start(bf16[1024,256]{1,0:T(8,128)(2,1)S(1)} %slice.73), channel_id=1, source_target_pairs={{0,96},{4,100},{8,104},{12,108},{16,112},{20,116},{24,120},{28,124... | collective-permute-start | bytes 1572872 | tf_op jit(solution)/shard_map/ppermute | solution.py:11
  247.3 22.4 %collective-permute-start.31 = (bf16[256,256]{0,1:T(8,128)(2,1)S(1)}, bf16[256,256]{0,1:T(8,128)(2,1)S(1)}, u32[]{:S(2)}, u32[]{:S(2)}) collective-permute-start(bf16[256,256]{0,1:T(8,128)(2,1)S(1)} %get-tuple-element.27), channel_id=1, source_target_pairs={{0,4},{4,8},{8,12},{12,16},{16,20},{20,24},{24,28},{28,0},{32,36},... | collective-permute-start | bytes 393224 | tf_op jit(solution)/shard_map/ppermute | solution.py:16
  249.8 26.9 %collective-permute-start.32 = (bf16[256,256]{0,1:T(8,128)(2,1)S(1)}, bf16[256,256]{0,1:T(8,128)(2,1)S(1)}, u32[]{:S(2)}, u32[]{:S(2)}) collective-permute-start(bf16[256,256]{0,1:T(8,128)(2,1)S(1)} %get-tuple-element.33), channel_id=1, source_target_pairs={{0,8},{4,12},{8,16},{12,20},{16,24},{20,28},{24,0},{28,4},{32,40},... | collective-permute-start | bytes 393224 | tf_op jit(solution)/shard_map/ppermute | solution.py:16
  253.2 34.4 %collective-permute-start.33 = (bf16[256,256]{0,1:T(8,128)(2,1)S(1)}, bf16[256,256]{0,1:T(8,128)(2,1)S(1)}, u32[]{:S(2)}, u32[]{:S(2)}) collective-permute-start(bf16[256,256]{0,1:T(8,128)(2,1)S(1)} %get-tuple-element.32), channel_id=1, source_target_pairs={{0,12},{4,16},{8,20},{12,24},{16,28},{20,0},{24,4},{28,8},{32,44},... | collective-permute-start | bytes 393224 | tf_op jit(solution)/shard_map/ppermute | solution.py:16
  261.8 27.1 %collective-permute-start.34 = (bf16[256,256]{0,1:T(8,128)(2,1)S(1)}, bf16[256,256]{0,1:T(8,128)(2,1)S(1)}, u32[]{:S(2)}, u32[]{:S(2)}) collective-permute-start(bf16[256,256]{0,1:T(8,128)(2,1)S(1)} %get-tuple-element.31), channel_id=1, source_target_pairs={{0,16},{4,20},{8,24},{12,28},{16,0},{20,4},{24,8},{28,12},{32,48},... | collective-permute-start | bytes 393224 | tf_op jit(solution)/shard_map/ppermute | solution.py:16
  264.0 25.0 %collective-permute-start.35 = (bf16[256,256]{0,1:T(8,128)(2,1)S(1)}, bf16[256,256]{0,1:T(8,128)(2,1)S(1)}, u32[]{:S(2)}, u32[]{:S(2)}) collective-permute-start(bf16[256,256]{0,1:T(8,128)(2,1)S(1)} %get-tuple-element.30), channel_id=1, source_target_pairs={{0,20},{4,24},{8,28},{12,0},{16,4},{20,8},{24,12},{28,16},{32,52},... | collective-permute-start | bytes 393224 | tf_op jit(solution)/shard_map/ppermute | solution.py:16
  269.7 19.2 %collective-permute-start.36 = (bf16[256,256]{0,1:T(8,128)(2,1)S(1)}, bf16[256,256]{0,1:T(8,128)(2,1)S(1)}, u32[]{:S(2)}, u32[]{:S(2)}) collective-permute-start(bf16[256,256]{0,1:T(8,128)(2,1)S(1)} %get-tuple-element.29), channel_id=1, source_target_pairs={{0,24},{4,28},{8,0},{12,4},{16,8},{20,12},{24,16},{28,20},{32,56},... | collective-permute-start | bytes 393224 | tf_op jit(solution)/shard_map/ppermute | solution.py:16
  276.7 14.8 %collective-permute-start.37 = (bf16[256,256]{0,1:T(8,128)(2,1)S(1)}, bf16[256,256]{0,1:T(8,128)(2,1)S(1)}, u32[]{:S(2)}, u32[]{:S(2)}) collective-permute-start(bf16[256,256]{0,1:T(8,128)(2,1)S(1)} %get-tuple-element.28), channel_id=1, source_target_pairs={{0,28},{4,0},{8,4},{12,8},{16,12},{20,16},{24,20},{28,24},{32,60},... | collective-permute-start | bytes 393224 | tf_op jit(solution)/shard_map/ppermute | solution.py:16
  279.3 13.4 %copy-start.5 = (f32[1,256,2,128]{3,2,1,0:T(2,128)S(1)}, f32[1,256,2,128]{3,2,1,0:T(2,128)}, u32[]{:S(2)}) copy-start(f32[1,256,2,128]{3,2,1,0:T(2,128)} %param.12) | copy-start | bytes 786436
  279.3 13.3 %copy-start.6 = (f32[1,256,2,128]{3,2,1,0:T(2,128)S(1)}, f32[1,256,2,128]{3,2,1,0:T(2,128)}, u32[]{:S(2)}) copy-start(f32[1,256,2,128]{3,2,1,0:T(2,128)} %param.13) | copy-start | bytes 786436
Sparse Core Ops, SparseCore 0:
  34.9 92.0 all-reduce.1

commit v2 on v0

v2 whole, which is shorter than its diff:
```python
import jax
import jax.numpy as jnp
from jax import lax
from jax.sharding import PartitionSpec as P

NX, NZ, NY = 4, 8, 4
HALF = NZ // 2
BF16, F32 = jnp.bfloat16, jnp.float32


def move(value, target):
    pairs = []
    for x in range(NX):
        for z in range(NZ):
            to_x, to_z = target(x, z)
            pairs.append((NZ * x + z, NZ * (to_x % NX) + to_z))
    return lax.ppermute(value, "fsdp", pairs)


def move_x(value, shift):
    return move(value, lambda x, z: (x + shift, z))


def move_y(value, shift):
    return lax.ppermute(value, "tensor", [(y, (y + shift) % NY) for y in range(NY)])


def swap_z(value, bit):
    return move(value, lambda x, z: (x, z ^ bit))


def swap_replica(value, bit):
    return lax.ppermute(value, "replica", [(r, r ^ bit) for r in range(lax.axis_size("replica"))])


def after(value, *others):
    return lax.optimization_barrier((value, *others))[0]


def body(
    tokens, cotangent, weights, first_moment, second_moment, frag_global, frag_moment, frag_local
):
    rows, width = tokens.shape
    depth = weights.shape[1]
    columns = weights.shape[2] * weights.shape[3]
    part = HALF * depth
    x = lax.axis_index("fsdp") // NZ
    z = lax.axis_index("fsdp") % NZ
    side = z // HALF
    y = lax.axis_index("tensor")

    def chunk(j, other):
        start = (x + j) % NX * (NZ * depth) + (side ^ other) * part
        return lax.dynamic_slice_in_dim(tokens, start, part, axis=1)

    held = []
    ready = ()
    for other in (1, 0):
        sent = jnp.concatenate([chunk(j, other) for j in (2, 1, 3, 0)], axis=1)
        sent = after(sent, *ready)
        before, behind = move_y(sent, 1), move_y(sent, -1)
        front, back = lax.optimization_barrier((before[: rows // 2], behind[rows // 2 :]))
        if other:
            arrived = front
        first, second = move_y(front, 1), move_y(back, -1)
        rest = jnp.concatenate([sent, before, behind], axis=0)
        rest = lax.optimization_barrier(jnp.pad(rest, ((0, rows), (0, 0))))
        ready = (rest,)
        rest = lax.dynamic_update_slice(rest, first, (3 * rows, 0))
        held.append(lax.dynamic_update_slice(rest, second, (3 * rows + rows // 2, 0)))
    far_held, near_held = held
    cot = cotangent.reshape(NY, rows, columns)
    cot = jnp.concatenate(
        [lax.dynamic_slice_in_dim(cot, (y + k) % NY, 1, axis=0) for k in (0, 3, 1, 2)], axis=0
    ).reshape(NY * rows, columns)

    own = weights[0].reshape(1, depth, columns)
    two = jnp.stack([own, swap_z(own, 4)])
    four = jnp.stack([two, swap_z(two, 2)])
    four = after(four, arrived)
    eight = jnp.stack([four, swap_z(four, 1)])
    eight = eight.reshape(2, 2, 2, depth, columns)
    eight = jnp.where((z & 1) == 0, eight, eight[::-1])
    eight = jnp.where((z & 2) == 0, eight, eight[:, ::-1])
    eight = jnp.where((z & 4) == 0, eight, eight[:, :, ::-1])
    plane = eight.transpose(2, 1, 0, 3, 4).reshape(2 * part, columns)
    def terms(held):
        product = lax.dot_general(held, cot, (((0,), (0,)), ((), ())), preferred_element_type=F32)
        return product.astype(BF16).reshape(NX, part, columns)

    def send_x(opposite, up, down, sign):
        if sign < 0:
            up, down = down, up
        passed = move_x(opposite, sign)
        reverse = move_x(down, -sign)
        return (up.astype(F32) + passed.astype(F32)).astype(BF16), reverse

    def block(value, index, count=1):
        return lax.dynamic_slice_in_dim(value, index * depth, count * depth, axis=0)

    opposite, up, down, here = terms(far_held)
    up, reverse = send_x(opposite, up, down, 1)
    forward = move_x(up, 1)
    far = here.astype(F32) + reverse.astype(F32) + forward.astype(F32)
    far = far.astype(BF16)
    crossing = swap_z(far, 4)

    plane = after(plane, far)
    low = move_x(plane, 1)
    high = move_x(plane, -1)
    planes = {0: plane, 1: high, 2: move_x(low, 1), 3: low}

    opposite, up, down, here = terms(near_held)
    down, reverse = send_x(opposite, up, down, -1)
    forward = move_x(down, -1)
    near = here.astype(F32) + reverse.astype(F32) + forward.astype(F32) + crossing.astype(F32)
    sent = near.astype(BF16)
    quarter = z % HALF
    pieces = [swap_z(block(sent, quarter ^ k), k) for k in range(1, HALF)]
    def half_plane(j, other):
        return lax.dynamic_slice_in_dim(planes[j], (side ^ other) * part, part, axis=0)

    def project(held, other):
        matrix = jnp.concatenate([half_plane(j, other) for j in (2, 1, 3, 0)], axis=0)
        return jnp.dot(held, matrix, preferred_element_type=F32)

    projected = (project(far_held, 1) + project(near_held, 0)).astype(BF16)
    projected = projected.reshape(NY, rows, columns)
    ordered = []
    for row in range(NY):
        k = (row - y) % NY
        place = jnp.where(k == 0, 0, k % 3 + 1)
        ordered.append(lax.dynamic_slice_in_dim(projected, place, 1, axis=0))
    keys_values = jnp.concatenate(ordered, axis=0).reshape(cotangent.shape)

    pieces = after(pieces, keys_values)
    gradient = block(near, quarter)
    for piece in pieces:
        gradient = gradient + piece.astype(F32)

    gradient = gradient.reshape(first_moment.shape)
    first_next = 0.9 * first_moment + 0.1 * gradient
    second_next = 0.95 * second_moment + 0.05 * gradient * gradient
    weight_float = weights.astype(F32)
    update = first_next / (1.0 - 0.9**10) / (jnp.sqrt(second_next / (1.0 - 0.95**10)) + 1e-08)
    weights_next = (weight_float - 0.001 * (update + 0.1 * weight_float)).astype(BF16)

    local_float = frag_local[0].astype(F32)
    pair = (local_float + swap_replica(frag_local[0], 1).astype(F32)).astype(BF16)
    summed = pair.astype(F32) + swap_replica(after(pair, far), 2).astype(F32)
    outer_step = frag_global - summed / lax.axis_size("replica")
    moment_next = 0.9 * frag_moment + outer_step
    global_next = frag_global - 0.7 * (outer_step + 0.9 * moment_next)
    local_next = (0.5 * local_float + 0.5 * global_next).astype(BF16)[None]
    return (
        keys_values,
        weights_next,
        first_next,
        second_next,
        global_next,
        moment_next,
        local_next,
    )


def solution(mesh):
    return jax.shard_map(
        body,
        mesh=mesh,
        in_specs=(
            P(("replica", "fsdp", "tensor"), None),
            P(("replica", "fsdp"), None, "tensor"),
            P("replica", "fsdp", None, "tensor"),
            P("replica", "fsdp", None, "tensor"),
            P("replica", "fsdp", None, "tensor"),
            P("fsdp", None, "tensor"),
            P("fsdp", None, "tensor"),
            P("replica", "fsdp", None, "tensor"),
        ),
        out_specs=(
            P(("replica", "fsdp"), None, "tensor"),
            P("replica", "fsdp", None, "tensor"),
            P("replica", "fsdp", None, "tensor"),
            P("replica", "fsdp", None, "tensor"),
            P("fsdp", None, "tensor"),
            P("fsdp", None, "tensor"),
            P("replica", "fsdp", None, "tensor"),
        ),
        check_vma=False,
    )
```

time: 615 us -> 214 us (0.35)
  the two profiles are of different devices: /device:TPU:16 before, /device:TPU:88 now
where the time goes in v2:
time: 214 us; the launch traced here: 213 us
  starting transfers between devices  98.2 us (46%)
  waiting for transfers between devices  73.7 us (34%)
  other arithmetic  18.8 us (9%)
  local copies, waits for them, and re-layouts  15.4 us (7%)
  matrix products  5.11 us (2%)
    ppermute x16, starting transfers between devices, move(): return lax.ppermute(value, 'fsdp', pairs)  59.9 us
    ppermute x2, waiting for transfers between devices, swap_replica(): lax.ppermute(value, 'replica', [(r, r ^ bit) for r in range(lax.axis_size...  37.3 us
    ppermute x8, starting transfers between devices, move_y(): lax.ppermute(value, 'tensor', [(y, (y + shift) % NY) for y in range(NY)])  24.6 us
    ppermute x16, waiting for transfers between devices, move(): return lax.ppermute(value, 'fsdp', pairs)  20.9 us
    ppermute x8, waiting for transfers between devices, move_y(): lax.ppermute(value, 'tensor', [(y, (y + shift) % NY) for y in range(NY)])  15.4 us
    ppermute x2, starting transfers between devices, swap_replica(): lax.ppermute(value, 'replica', [(r, r ^ bit) for r in range(lax.axis_size...  13.7 us
    concatenate x2, other arithmetic, body(): rest = jnp.concatenate([sent, before, behind], axis=0)  4.99 us
  transfers between devices with their start and end apart: 26, of which 12 were waited for; matrix products, arithmetic and copies ran while one was open for 15% of the time, Pallas kernels for 0%

profile of v2, /device:TPU:88, one launch (start us, length us, event | category | flops | bytes accessed | tf_op | source)
XLA Modules:
  0.0 212.7 jit_solution(6090997405943861723)
XLA Ops:
  0.6 1.1 reshape_squeeze.3
  1.7 9.1 %collective-permute-start.4 = (bf16[1,256,256]{2,1,0:T(8,128)(2,1)S(1)}, bf16[1,256,256]{2,1,0:T(8,128)(2,1)S(1)}, u32[]{:S(2)}, u32[]{:S(2)}) collective-permute-start(bf16[1,256,256]{2,1,0:T(8,128)(2,1)S(1)} %reshape_squeeze.3), channel_id=1, source_target_pairs={{0,16},{4,20},{8,24},{12,28},{16,0},{20,4},{24,8},{28,12},{32,48},... | collective-permute-start | bytes 393224 | tf_op jit(solution)/shard_map/ppermute | solution.py:17
  11.0 2.6 %constant_dynamic-slice_fusion.26 = (bf16[128,1024]{1,0:T(8,128)(2,1)S(1)}, bf16[128,1024]{1,0:T(8,128)(2,1)}, bf16[128,1024]{1,0:T(8,128)(2,1)}, bf16[128,1024]...) fusion(bf16[128,8192]{1,0:T(8,128)(2,1)} %param.8, ...), kind=kLoop, calls=%fused_computation.93 | loop fusion | bytes 4194336 | tf_op jit(solution)/shard_map/dynamic_slice | solution.py:54
  13.6 2.1 %collective-permute-start = (bf16[128,4096]{1,0:T(8,128)(2,1)S(1)}, bf16[128,4096]{1,0:T(8,128)(2,1)S(1)}, u32[]{:S(2)}, u32[]{:S(2)}) collective-permute-start(bf16[128,4096]{1,0:T(8,128)(2,1)S(1)} %pad_maximum_fusion), channel_id=1, source_target_pairs={{0,1},{1,2},{2,3},{3,0},{4,5},{5,6},{6,7},{7,4},{8,9},{9,10},{10,1... | collective-permute-start | bytes 3145736 | tf_op jit(solution)/shard_map/ppermute | solution.py:25
  15.8 3.7 %collective-permute-start.1 = (bf16[128,4096]{1,0:T(8,128)(2,1)S(1)}, bf16[128,4096]{1,0:T(8,128)(2,1)}, u32[]{:S(2)}, u32[]{:S(2)}) collective-permute-start(bf16[128,4096]{1,0:T(8,128)(2,1)S(1)} %pad_maximum_fusion), channel_id=1, source_target_pairs={{0,3},{1,0},{2,1},{3,2},{4,7},{5,4},{6,5},{7,6},{8,11},{9,8},{10,9... | collective-permute-start | bytes 3145736 | tf_op jit(solution)/shard_map/ppermute | solution.py:25
  19.6 0.7 fusion.42
  20.4 4.6 %collective-permute-start.5 = (bf16[2,1,256,256]{3,2,0,1:T(8,128)(2,1)}, bf16[2,1,256,256]{3,2,0,1:T(8,128)(2,1)}, u32[]{:S(2)}, u32[]{:S(2)}) collective-permute-start(bf16[2,1,256,256]{3,2,0,1:T(8,128)(2,1)} %get-tuple-element.69), channel_id=1, source_target_pairs={{0,8},{4,12},{8,0},{12,4},{16,24},{20,28},{24,16},{28,20},{32,40},... | collective-permute-start | bytes 786440 | tf_op jit(solution)/shard_map/ppermute | solution.py:17
  25.0 1.3 pad_maximum_fusion.1
  26.3 1.8 reshape.91
  28.2 1.0 constant_dynamic-slice_fusion.22
  29.2 6.8 %collective-permute-done.5 = bf16[2,1,256,256]{3,2,0,1:T(8,128)(2,1)} collective-permute-done((bf16[2,1,256,256]{3,2,0,1:T(8,128)(2,1)}, bf16[2,1,256,256]{3,2,0,1:T(8,128)(2,1)}, u32[]{:S(2)}, u32[]{:S(2)}) %collective-permute-start.5) | collective-permute-done | bytes 262176 | tf_op jit(solution)/shard_map/ppermute | solution.py:17
  35.9 1.0 pad_maximum_fusion.2
  36.9 3.2 %collective-permute-done = bf16[128,4096]{1,0:T(8,128)(2,1)S(1)} collective-permute-done((bf16[128,4096]{1,0:T(8,128)(2,1)S(1)}, bf16[128,4096]{1,0:T(8,128)(2,1)S(1)}, u32[]{:S(2)}, u32[]{:S(2)}) %collective-permute-start) | collective-permute-done | bytes 1048608 | tf_op jit(solution)/shard_map/ppermute | solution.py:25
  40.2 3.2 %collective-permute-done.1 = bf16[128,4096]{1,0:T(8,128)(2,1)} collective-permute-done((bf16[128,4096]{1,0:T(8,128)(2,1)S(1)}, bf16[128,4096]{1,0:T(8,128)(2,1)}, u32[]{:S(2)}, u32[]{:S(2)}) %collective-permute-start.1) | collective-permute-done | bytes 1048608 | tf_op jit(solution)/shard_map/ppermute | solution.py:25
  43.4 1.1 slice.25
  44.5 2.2 %collective-permute-start.2 = (bf16[64,4096]{1,0:T(8,128)(2,1)S(1)}, bf16[64,4096]{1,0:T(8,128)(2,1)S(1)}, u32[]{:S(2)}, u32[]{:S(2)}) collective-permute-start(bf16[64,4096]{1,0:T(8,128)(2,1)S(1)} %slice.24), channel_id=1, source_target_pairs={{0,1},{1,2},{2,3},{3,0},{4,5},{5,6},{6,7},{7,4},{8,9},{9,10},{10,1... | collective-permute-start | bytes 1572872 | tf_op jit(solution)/shard_map/ppermute | solution.py:25
  46.7 3.6 %collective-permute-start.3 = (bf16[64,4096]{1,0:T(8,128)(2,1)S(1)}, bf16[64,4096]{1,0:T(8,128)(2,1)S(1)}, u32[]{:S(2)}, u32[]{:S(2)}) collective-permute-start(bf16[64,4096]{1,0:T(8,128)(2,1)S(1)} %slice.25), channel_id=1, source_target_pairs={{0,3},{1,0},{2,1},{3,2},{4,7},{5,4},{6,5},{7,6},{8,11},{9,8},{10,9... | collective-permute-start | bytes 1572872 | tf_op jit(solution)/shard_map/ppermute | solution.py:25
  50.3 4.4 %fusion.7 = bf16[512,4096]{1,0:T(8,128)(2,1)S(1)} fusion(bf16[128,4096]{1,0:T(8,128)(2,1)} %collective-permute-done.1, bf16[128,4096]{1,0:T(8,128)(2,1)S(1)} %collective-permute-done, bf16[128,4096]{1,0:T(8,128)(2,1)S(1)} %pad_maximum_fusion), kind=kLoop, calls=%fused_computation.10 | loop fusion | flops 20971520 | bytes 7340032 | tf_op jit(solution)/shard_map/concatenate | solution.py:66
  54.8 2.4 %collective-permute-start.14 = (bf16[128,4096]{1,0:T(8,128)(2,1)S(1)}, bf16[128,4096]{1,0:T(8,128)(2,1)S(1)}, u32[]{:S(2)}, u32[]{:S(2)}) collective-permute-start(bf16[128,4096]{1,0:T(8,128)(2,1)S(1)} %pad_maximum_fusion.1), channel_id=1, source_target_pairs={{0,3},{1,0},{2,1},{3,2},{4,7},{5,4},{6,5},{7,6},{8,11},{9,8},{10,9... | collective-permute-start | bytes 3145736 | tf_op jit(solution)/shard_map/ppermute | solution.py:25
  57.2 4.6 %collective-permute-start.13 = (bf16[128,4096]{1,0:T(8,128)(2,1)S(1)}, bf16[128,4096]{1,0:T(8,128)(2,1)S(1)}, u32[]{:S(2)}, u32[]{:S(2)}) collective-permute-start(bf16[128,4096]{1,0:T(8,128)(2,1)S(1)} %pad_maximum_fusion.1), channel_id=1, source_target_pairs={{0,1},{1,2},{2,3},{3,0},{4,5},{5,6},{6,7},{7,4},{8,9},{9,10},{10,1... | collective-permute-start | bytes 3145736 | tf_op jit(solution)/shard_map/ppermute | solution.py:25
  61.8 3.8 %collective-permute-start.6 = (bf16[2,2,1,256,256]{4,3,0,1,2:T(8,128)(2,1)S(1)}, bf16[2,2,1,256,256]{4,3,0,1,2:T(8,128)(2,1)S(1)}, u32[]{:S(2)}, u32[]{:S(2)}) collective-permute-start(bf16[2,2,1,256,256]{4,3,0,1,2:T(8,128)(2,1)S(1)} %pad_maximum_fusion.2), channel_id=1, source_target_pairs={{0,4},{4,0},{8,12},{12,8},{16,20},{20,16},{24,28},{28,24},{32,36},... | collective-permute-start | bytes 1572872 | tf_op jit(solution)/shard_map/ppermute | solution.py:17
  65.8 1.3 convolution_convert_fusion.1
  67.1 0.6 copy-done.2
  67.8 3.4 %collective-permute-start.8 = (bf16[1024,256]{1,0:T(8,128)(2,1)S(1)}, bf16[1024,256]{1,0:T(8,128)(2,1)S(1)}, u32[]{:S(2)}, u32[]{:S(2)}) collective-permute-start(bf16[1024,256]{1,0:T(8,128)(2,1)S(1)} %get-tuple-element.40), channel_id=1, source_target_pairs={{0,32},{4,36},{8,40},{12,44},{16,48},{20,52},{24,56},{28,60},{32,6... | collective-permute-start | bytes 1572872 | tf_op jit(solution)/shard_map/ppermute | solution.py:17
  71.2 3.7 %collective-permute-start.7 = (bf16[1024,256]{1,0:T(8,128)(2,1)S(1)}, bf16[1024,256]{1,0:T(8,128)(2,1)S(1)}, u32[]{:S(2)}, u32[]{:S(2)}) collective-permute-start(bf16[1024,256]{1,0:T(8,128)(2,1)S(1)} %get-tuple-element.39), channel_id=1, source_target_pairs={{0,96},{4,100},{8,104},{12,108},{16,112},{20,116},{24,120},{28,124... | collective-permute-start | bytes 1572872 | tf_op jit(solution)/shard_map/ppermute | solution.py:17
  75.7 6.2 %collective-permute-done.13 = bf16[128,4096]{1,0:T(8,128)(2,1)S(1)} collective-permute-done((bf16[128,4096]{1,0:T(8,128)(2,1)S(1)}, bf16[128,4096]{1,0:T(8,128)(2,1)S(1)}, u32[]{:S(2)}, u32[]{:S(2)}) %collective-permute-start.13) | collective-permute-done | bytes 1048608 | tf_op jit(solution)/shard_map/ppermute | solution.py:25
  82.0 2.2 %collective-permute-done.14 = bf16[128,4096]{1,0:T(8,128)(2,1)S(1)} collective-permute-done((bf16[128,4096]{1,0:T(8,128)(2,1)S(1)}, bf16[128,4096]{1,0:T(8,128)(2,1)S(1)}, u32[]{:S(2)}, u32[]{:S(2)}) %collective-permute-start.14) | collective-permute-done | bytes 1048608 | tf_op jit(solution)/shard_map/ppermute | solution.py:25
  84.3 3.4 %collective-permute-start.15 = (bf16[64,4096]{1,0:T(8,128)(2,1)S(1)}, bf16[64,4096]{1,0:T(8,128)(2,1)S(1)}, u32[]{:S(2)}, u32[]{:S(2)}) collective-permute-start(bf16[64,4096]{1,0:T(8,128)(2,1)S(1)} %slice.26), channel_id=1, source_target_pairs={{0,1},{1,2},{2,3},{3,0},{4,5},{5,6},{6,7},{7,4},{8,9},{9,10},{10,1... | collective-permute-start | bytes 1572872 | tf_op jit(solution)/shard_map/ppermute | solution.py:25
  87.8 3.4 %collective-permute-start.9 = (bf16[1024,256]{1,0:T(8,128)(2,1)S(1)}, bf16[1024,256]{1,0:T(8,128)(2,1)S(1)}, u32[]{:S(2)}, u32[]{:S(2)}) collective-permute-start(bf16[1024,256]{1,0:T(8,128)(2,1)S(1)} %add_convert_fusion.2), channel_id=1, source_target_pairs={{0,32},{4,36},{8,40},{12,44},{16,48},{20,52},{24,56},{28,60},{32,6... | collective-permute-start | bytes 1572872 | tf_op jit(solution)/shard_map/ppermute | solution.py:17
  91.2 0.6 fusion.9
  91.8 2.5 %collective-permute-start.16 = (bf16[64,4096]{1,0:T(8,128)(2,1)S(1)}, bf16[64,4096]{1,0:T(8,128)(2,1)S(1)}, u32[]{:S(2)}, u32[]{:S(2)}) collective-permute-start(bf16[64,4096]{1,0:T(8,128)(2,1)S(1)} %slice.27), channel_id=1, source_target_pairs={{0,3},{1,0},{2,1},{3,2},{4,7},{5,4},{6,5},{7,6},{8,11},{9,8},{10,9... | collective-permute-start | bytes 1572872 | tf_op jit(solution)/shard_map/ppermute | solution.py:25
  94.3 6.8 %collective-permute-done.9 = bf16[1024,256]{1,0:T(8,128)(2,1)S(1)} collective-permute-done((bf16[1024,256]{1,0:T(8,128)(2,1)S(1)}, bf16[1024,256]{1,0:T(8,128)(2,1)S(1)}, u32[]{:S(2)}, u32[]{:S(2)}) %collective-permute-start.9) | collective-permute-done | bytes 524320 | tf_op jit(solution)/shard_map/ppermute | solution.py:17
  101.1 1.0 add_convert_fusion.1
  102.1 2.2 %collective-permute-start.10 = (bf16[2048,256]{1,0:T(8,128)(2,1)S(1)}, bf16[2048,256]{1,0:T(8,128)(2,1)}, u32[]{:S(2)}, u32[]{:S(2)}) collective-permute-start(bf16[2048,256]{1,0:T(8,128)(2,1)S(1)} %bitcast.28), channel_id=1, source_target_pairs={{0,32},{4,36},{8,40},{12,44},{16,48},{20,52},{24,56},{28,60},{32,6... | collective-permute-start | bytes 3145736 | tf_op jit(solution)/shard_map/ppermute | solution.py:17
  104.9 1.3 convolution_convert_fusion
  106.2 0.7 copy-done
  106.9 0.9 fusion.45
  107.8 4.4 %collective-permute-start.18 = (bf16[1024,256]{1,0:T(8,128)(2,1)S(1)}, bf16[1024,256]{1,0:T(8,128)(2,1)S(1)}, u32[]{:S(2)}, u32[]{:S(2)}) collective-permute-start(bf16[1024,256]{1,0:T(8,128)(2,1)S(1)} %get-tuple-element.38), channel_id=1, source_target_pairs={{0,96},{4,100},{8,104},{12,108},{16,112},{20,116},{24,120},{28,124... | collective-permute-start | bytes 1572872 | tf_op jit(solution)/shard_map/ppermute | solution.py:17
  112.2 1.9 collective-permute-start.24
  114.1 1.3 collective-permute-done.24
  115.6 2.8 %collective-permute-start.20 = (bf16[1024,256]{1,0:T(8,128)(2,1)}, bf16[1024,256]{1,0:T(8,128)(2,1)}, u32[]{:S(2)}, u32[]{:S(2)}) collective-permute-start(bf16[1024,256]{1,0:T(8,128)(2,1)} %add_convert_fusion.1), channel_id=1, source_target_pairs={{0,16},{4,20},{8,24},{12,28},{16,0},{20,4},{24,8},{28,12},{32,48},... | collective-permute-start | bytes 1572872 | tf_op jit(solution)/shard_map/ppermute | solution.py:17
  118.4 1.9 collective-permute-start.17
  120.3 11.8 %collective-permute-start.25 = (bf16[256,2,128]{2,1,0:T(2,128)(2,1)S(1)}, bf16[256,2,128]{2,1,0:T(2,128)(2,1)S(1)}, u32[]{:S(2)}, u32[]{:S(2)}) collective-permute-start(bf16[256,2,128]{2,1,0:T(2,128)(2,1)S(1)} %fusion.34), channel_id=1, source_target_pairs={{0,256},{128,384},{256,0},{384,128},{1,257},{129,385},{257,1},{385... | collective-permute-start | bytes 393224 | tf_op jit(solution)/shard_map/ppermute | solution.py:33
  132.1 0.9 add_convert_fusion
  133.1 5.1 %collective-permute-start.19 = (bf16[1024,256]{1,0:T(8,128)(2,1)}, bf16[1024,256]{1,0:T(8,128)(2,1)}, u32[]{:S(2)}, u32[]{:S(2)}) collective-permute-start(bf16[1024,256]{1,0:T(8,128)(2,1)} %add_convert_fusion), channel_id=1, source_target_pairs={{0,96},{4,100},{8,104},{12,108},{16,112},{20,116},{24,120},{28,124... | collective-permute-start | bytes 1572872 | tf_op jit(solution)/shard_map/ppermute | solution.py:17
  138.2 36.0 %collective-permute-done.25 = bf16[256,2,128]{2,1,0:T(2,128)(2,1)S(1)} collective-permute-done((bf16[256,2,128]{2,1,0:T(2,128)(2,1)S(1)}, bf16[256,2,128]{2,1,0:T(2,128)(2,1)S(1)}, u32[]{:S(2)}, u32[]{:S(2)}) %collective-permute-start.25) | collective-permute-done | bytes 131104 | tf_op jit(solution)/shard_map/ppermute | solution.py:33
  174.2 0.7 copy-done.8
  174.9 2.7 %collective-permute-start.12 = (bf16[2048,256]{1,0:T(8,128)(2,1)S(1)}, bf16[2048,256]{1,0:T(8,128)(2,1)}, u32[]{:S(2)}, u32[]{:S(2)}) collective-permute-start(bf16[2048,256]{1,0:T(8,128)(2,1)S(1)} %bitcast.29), channel_id=1, source_target_pairs={{0,96},{4,100},{8,104},{12,108},{16,112},{20,116},{24,120},{28,124... | collective-permute-start | bytes 3145736 | tf_op jit(solution)/shard_map/ppermute | solution.py:17
  177.8 3.3 %collective-permute-start.11 = (bf16[2048,256]{1,0:T(8,128)(2,1)}, bf16[2048,256]{1,0:T(8,128)(2,1)S(1)}, u32[]{:S(2)}, u32[]{:S(2)}) collective-permute-start(bf16[2048,256]{1,0:T(8,128)(2,1)} %collective-permute-done.10), channel_id=1, source_target_pairs={{0,32},{4,36},{8,40},{12,44},{16,48},{20,52},{24,56},{28,60},{32,6... | collective-permute-start | bytes 3145736 | tf_op jit(solution)/shard_map/ppermute | solution.py:17
  181.2 2.4 %fusion.39 = (bf16[1,256,2,128]{3,2,1,0:T(2,128)(2,1)}, f32[256,2,128]{2,1,0:T(2,128)}, f32[256,2,128]{2,1,0:T(2,128)}) fusion(bf16[1,256,2,128]{3,2,1,0:T(2,128)(2,1)S(1)} %copy-done.5, f32[256,2,128]{2,1,0:T(2,128)} %param.13, bf16[256,2,128]{2,1,0:T(2,128)(2,1)} %copy-done.8, bf16[256,2,128]{2,1,0:T(2,128)(2,1)S(1)} %fusion.34, f32[256,2,128]{2,1,0:T(2,128)} %param.14), kind=kLoop, calls=%fused_computation.62 | loop fusion | flops 983040 | bytes 1572864 | tf_op jit(solution)/shard_map/broadcast_in_dim | solution.py:154
  183.6 2.6 %fusion.44 = (bf16[1024,256]{1,0:T(8,128)(2,1)S(1)}, f32[1024,256]{1,0:T(8,128)}) fusion(bf16[1024,256]{1,0:T(8,128)(2,1)} %collective-permute-done.20, bf16[1024,256]{1,0:T(8,128)(2,1)} %collective-permute-done.19, bf16[1024,256]{1,0:T(8,128)(2,1)} %collective-permute-done.17, bf16[4096,256]{1,0:T(8,128)(2,1)S(1)} %convolution_convert_fusion), kind=kLoop, calls=%fused_computation.97 | loop fusion | flops 2097152 | bytes 3670016 | tf_op jit(solution)/shard_map/convert_element_type | solution.py:117
  186.2 2.2 %collective-permute-start.21 = (bf16[256,256]{1,0:T(8,128)(2,1)S(1)}, bf16[256,256]{1,0:T(8,128)(2,1)S(1)}, u32[]{:S(2)}, u32[]{:S(2)}) collective-permute-start(bf16[256,256]{1,0:T(8,128)(2,1)S(1)} %get-tuple-element.59), channel_id=1, source_target_pairs={{0,4},{4,0},{8,12},{12,8},{16,20},{20,16},{24,28},{28,24},{32,36},... | collective-permute-start | bytes 393224 | tf_op jit(solution)/shard_map/ppermute | solution.py:17
  188.4 1.9 collective-permute-start.22
  190.4 5.4 %collective-permute-start.23 = (bf16[256,256]{1,0:T(8,128)(2,1)S(1)}, bf16[256,256]{1,0:T(8,128)(2,1)S(1)}, u32[]{:S(2)}, u32[]{:S(2)}) collective-permute-start(bf16[256,256]{1,0:T(8,128)(2,1)S(1)} %get-tuple-element.57), channel_id=1, source_target_pairs={{0,12},{4,8},{8,4},{12,0},{16,28},{20,24},{24,20},{28,16},{32,44},... | collective-permute-start | bytes 393224 | tf_op jit(solution)/shard_map/ppermute | solution.py:17
  195.7 1.3 constant_dynamic-slice_fusion.16
  197.0 4.4 %collective-permute-done.12 = bf16[2048,256]{1,0:T(8,128)(2,1)} collective-permute-done((bf16[2048,256]{1,0:T(8,128)(2,1)S(1)}, bf16[2048,256]{1,0:T(8,128)(2,1)}, u32[]{:S(2)}, u32[]{:S(2)}) %collective-permute-start.12) | collective-permute-done | bytes 1048608 | tf_op jit(solution)/shard_map/ppermute | solution.py:17
  201.5 1.3 constant_dynamic-slice_fusion.17
  202.7 2.7 %collective-permute-done.11 = bf16[2048,256]{1,0:T(8,128)(2,1)S(1)} collective-permute-done((bf16[2048,256]{1,0:T(8,128)(2,1)}, bf16[2048,256]{1,0:T(8,128)(2,1)S(1)}, u32[]{:S(2)}, u32[]{:S(2)}) %collective-permute-start.11) | collective-permute-done | bytes 1048608 | tf_op jit(solution)/shard_map/ppermute | solution.py:17
  205.5 1.3 fusion.18
  206.8 0.9 copy-done.3
  207.7 1.2 fusion.29
  209.0 0.8 reshape.94
  209.8 1.0 convert_add_fusion.3
  211.0 1.7 fusion.38
  (53 shorter events, 2.5 us)
Async XLA Ops:
  0.6 18.9 %copy-start.4 = (bf16[1,256,2,128]{3,2,1,0:T(2,128)(2,1)S(1)}, bf16[1,256,2,128]{3,2,1,0:T(2,128)(2,1)}, u32[]{:S(2)}) copy-start(bf16[1,256,2,128]{3,2,1,0:T(2,128)(2,1)} %param.10) | copy-start | bytes 393220
  1.7 17.9 %collective-permute-start.4 = (bf16[1,256,256]{2,1,0:T(8,128)(2,1)S(1)}, bf16[1,256,256]{2,1,0:T(8,128)(2,1)S(1)}, u32[]{:S(2)}, u32[]{:S(2)}) collective-permute-start(bf16[1,256,256]{2,1,0:T(8,128)(2,1)S(1)} %reshape_squeeze.3), channel_id=1, source_target_pairs={{0,16},{4,20},{8,24},{12,28},{16,0},{20,4},{24,8},{28,12},{32,48},... | collective-permute-start | bytes 393224 | tf_op jit(solution)/shard_map/ppermute | solution.py:17
  13.6 26.5 %collective-permute-start = (bf16[128,4096]{1,0:T(8,128)(2,1)S(1)}, bf16[128,4096]{1,0:T(8,128)(2,1)S(1)}, u32[]{:S(2)}, u32[]{:S(2)}) collective-permute-start(bf16[128,4096]{1,0:T(8,128)(2,1)S(1)} %pad_maximum_fusion), channel_id=1, source_target_pairs={{0,1},{1,2},{2,3},{3,0},{4,5},{5,6},{6,7},{7,4},{8,9},{9,10},{10,1... | collective-permute-start | bytes 3145736 | tf_op jit(solution)/shard_map/ppermute | solution.py:25
  15.8 27.6 %collective-permute-start.1 = (bf16[128,4096]{1,0:T(8,128)(2,1)S(1)}, bf16[128,4096]{1,0:T(8,128)(2,1)}, u32[]{:S(2)}, u32[]{:S(2)}) collective-permute-start(bf16[128,4096]{1,0:T(8,128)(2,1)S(1)} %pad_maximum_fusion), channel_id=1, source_target_pairs={{0,3},{1,0},{2,1},{3,2},{4,7},{5,4},{6,5},{7,6},{8,11},{9,8},{10,9... | collective-permute-start | bytes 3145736 | tf_op jit(solution)/shard_map/ppermute | solution.py:25
  20.4 15.6 %collective-permute-start.5 = (bf16[2,1,256,256]{3,2,0,1:T(8,128)(2,1)}, bf16[2,1,256,256]{3,2,0,1:T(8,128)(2,1)}, u32[]{:S(2)}, u32[]{:S(2)}) collective-permute-start(bf16[2,1,256,256]{3,2,0,1:T(8,128)(2,1)} %get-tuple-element.69), channel_id=1, source_target_pairs={{0,8},{4,12},{8,0},{12,4},{16,24},{20,28},{24,16},{28,20},{32,40},... | collective-permute-start | bytes 786440 | tf_op jit(solution)/shard_map/ppermute | solution.py:17
  44.5 21.2 %collective-permute-start.2 = (bf16[64,4096]{1,0:T(8,128)(2,1)S(1)}, bf16[64,4096]{1,0:T(8,128)(2,1)S(1)}, u32[]{:S(2)}, u32[]{:S(2)}) collective-permute-start(bf16[64,4096]{1,0:T(8,128)(2,1)S(1)} %slice.24), channel_id=1, source_target_pairs={{0,1},{1,2},{2,3},{3,0},{4,5},{5,6},{6,7},{7,4},{8,9},{9,10},{10,1... | collective-permute-start | bytes 1572872 | tf_op jit(solution)/shard_map/ppermute | solution.py:25
  46.7 19.0 %collective-permute-start.3 = (bf16[64,4096]{1,0:T(8,128)(2,1)S(1)}, bf16[64,4096]{1,0:T(8,128)(2,1)S(1)}, u32[]{:S(2)}, u32[]{:S(2)}) collective-permute-start(bf16[64,4096]{1,0:T(8,128)(2,1)S(1)} %slice.25), channel_id=1, source_target_pairs={{0,3},{1,0},{2,1},{3,2},{4,7},{5,4},{6,5},{7,6},{8,11},{9,8},{10,9... | collective-permute-start | bytes 1572872 | tf_op jit(solution)/shard_map/ppermute | solution.py:25
  54.8 29.5 %collective-permute-start.14 = (bf16[128,4096]{1,0:T(8,128)(2,1)S(1)}, bf16[128,4096]{1,0:T(8,128)(2,1)S(1)}, u32[]{:S(2)}, u32[]{:S(2)}) collective-permute-start(bf16[128,4096]{1,0:T(8,128)(2,1)S(1)} %pad_maximum_fusion.1), channel_id=1, source_target_pairs={{0,3},{1,0},{2,1},{3,2},{4,7},{5,4},{6,5},{7,6},{8,11},{9,8},{10,9... | collective-permute-start | bytes 3145736 | tf_op jit(solution)/shard_map/ppermute | solution.py:25
  57.2 24.8 %collective-permute-start.13 = (bf16[128,4096]{1,0:T(8,128)(2,1)S(1)}, bf16[128,4096]{1,0:T(8,128)(2,1)S(1)}, u32[]{:S(2)}, u32[]{:S(2)}) collective-permute-start(bf16[128,4096]{1,0:T(8,128)(2,1)S(1)} %pad_maximum_fusion.1), channel_id=1, source_target_pairs={{0,1},{1,2},{2,3},{3,0},{4,5},{5,6},{6,7},{7,4},{8,9},{9,10},{10,1... | collective-permute-start | bytes 3145736 | tf_op jit(solution)/shard_map/ppermute | solution.py:25
  61.8 13.2 %collective-permute-start.6 = (bf16[2,2,1,256,256]{4,3,0,1,2:T(8,128)(2,1)S(1)}, bf16[2,2,1,256,256]{4,3,0,1,2:T(8,128)(2,1)S(1)}, u32[]{:S(2)}, u32[]{:S(2)}) collective-permute-start(bf16[2,2,1,256,256]{4,3,0,1,2:T(8,128)(2,1)S(1)} %pad_maximum_fusion.2), channel_id=1, source_target_pairs={{0,4},{4,0},{8,12},{12,8},{16,20},{20,16},{24,28},{28,24},{32,36},... | collective-permute-start | bytes 1572872 | tf_op jit(solution)/shard_map/ppermute | solution.py:17
  65.8 2.0 copy-start.2
  67.8 19.9 %collective-permute-start.8 = (bf16[1024,256]{1,0:T(8,128)(2,1)S(1)}, bf16[1024,256]{1,0:T(8,128)(2,1)S(1)}, u32[]{:S(2)}, u32[]{:S(2)}) collective-permute-start(bf16[1024,256]{1,0:T(8,128)(2,1)S(1)} %get-tuple-element.40), channel_id=1, source_target_pairs={{0,32},{4,36},{8,40},{12,44},{16,48},{20,52},{24,56},{28,60},{32,6... | collective-permute-start | bytes 1572872 | tf_op jit(solution)/shard_map/ppermute | solution.py:17
  71.2 23.1 %collective-permute-start.7 = (bf16[1024,256]{1,0:T(8,128)(2,1)S(1)}, bf16[1024,256]{1,0:T(8,128)(2,1)S(1)}, u32[]{:S(2)}, u32[]{:S(2)}) collective-permute-start(bf16[1024,256]{1,0:T(8,128)(2,1)S(1)} %get-tuple-element.39), channel_id=1, source_target_pairs={{0,96},{4,100},{8,104},{12,108},{16,112},{20,116},{24,120},{28,124... | collective-permute-start | bytes 1572872 | tf_op jit(solution)/shard_map/ppermute | solution.py:17
  84.3 20.1 %collective-permute-start.15 = (bf16[64,4096]{1,0:T(8,128)(2,1)S(1)}, bf16[64,4096]{1,0:T(8,128)(2,1)S(1)}, u32[]{:S(2)}, u32[]{:S(2)}) collective-permute-start(bf16[64,4096]{1,0:T(8,128)(2,1)S(1)} %slice.26), channel_id=1, source_target_pairs={{0,1},{1,2},{2,3},{3,0},{4,5},{5,6},{6,7},{7,4},{8,9},{9,10},{10,1... | collective-permute-start | bytes 1572872 | tf_op jit(solution)/shard_map/ppermute | solution.py:25
  87.8 13.3 %collective-permute-start.9 = (bf16[1024,256]{1,0:T(8,128)(2,1)S(1)}, bf16[1024,256]{1,0:T(8,128)(2,1)S(1)}, u32[]{:S(2)}, u32[]{:S(2)}) collective-permute-start(bf16[1024,256]{1,0:T(8,128)(2,1)S(1)} %add_convert_fusion.2), channel_id=1, source_target_pairs={{0,32},{4,36},{8,40},{12,44},{16,48},{20,52},{24,56},{28,60},{32,6... | collective-permute-start | bytes 1572872 | tf_op jit(solution)/shard_map/ppermute | solution.py:17
  91.8 13.0 %collective-permute-start.16 = (bf16[64,4096]{1,0:T(8,128)(2,1)S(1)}, bf16[64,4096]{1,0:T(8,128)(2,1)S(1)}, u32[]{:S(2)}, u32[]{:S(2)}) collective-permute-start(bf16[64,4096]{1,0:T(8,128)(2,1)S(1)} %slice.27), channel_id=1, source_target_pairs={{0,3},{1,0},{2,1},{3,2},{4,7},{5,4},{6,5},{7,6},{8,11},{9,8},{10,9... | collective-permute-start | bytes 1572872 | tf_op jit(solution)/shard_map/ppermute | solution.py:25
  102.1 75.6 %collective-permute-start.10 = (bf16[2048,256]{1,0:T(8,128)(2,1)S(1)}, bf16[2048,256]{1,0:T(8,128)(2,1)}, u32[]{:S(2)}, u32[]{:S(2)}) collective-permute-start(bf16[2048,256]{1,0:T(8,128)(2,1)S(1)} %bitcast.28), channel_id=1, source_target_pairs={{0,32},{4,36},{8,40},{12,44},{16,48},{20,52},{24,56},{28,60},{32,6... | collective-permute-start | bytes 3145736 | tf_op jit(solution)/shard_map/ppermute | solution.py:17
  104.9 2.0 copy-start
  104.9 7.3 %copy-start.5 = (bf16[1,256,2,128]{3,2,1,0:T(2,128)(2,1)S(1)}, bf16[1,256,2,128]{3,2,1,0:T(2,128)(2,1)}, u32[]{:S(2)}) copy-start(bf16[1,256,2,128]{3,2,1,0:T(2,128)(2,1)} %param.15) | copy-start | bytes 393220
  107.8 24.3 %collective-permute-start.18 = (bf16[1024,256]{1,0:T(8,128)(2,1)S(1)}, bf16[1024,256]{1,0:T(8,128)(2,1)S(1)}, u32[]{:S(2)}, u32[]{:S(2)}) collective-permute-start(bf16[1024,256]{1,0:T(8,128)(2,1)S(1)} %get-tuple-element.38), channel_id=1, source_target_pairs={{0,96},{4,100},{8,104},{12,108},{16,112},{20,116},{24,120},{28,124... | collective-permute-start | bytes 1572872 | tf_op jit(solution)/shard_map/ppermute | solution.py:17
  112.2 3.2 %collective-permute-start.24 = (bf16[256,2,128]{2,1,0:T(2,128)(2,1)S(1)}, bf16[256,2,128]{2,1,0:T(2,128)(2,1)S(1)}, u32[]{:S(2)}, u32[]{:S(2)}) collective-permute-start(bf16[256,2,128]{2,1,0:T(2,128)(2,1)S(1)} %bitcast.32), channel_id=1, source_target_pairs={{0,128},{128,0},{256,384},{384,256},{1,129},{129,1},{257,385},{385... | collective-permute-start | bytes 393224 | tf_op jit(solution)/shard_map/ppermute | solution.py:33
  115.6 68.0 %collective-permute-start.20 = (bf16[1024,256]{1,0:T(8,128)(2,1)}, bf16[1024,256]{1,0:T(8,128)(2,1)}, u32[]{:S(2)}, u32[]{:S(2)}) collective-permute-start(bf16[1024,256]{1,0:T(8,128)(2,1)} %add_convert_fusion.1), channel_id=1, source_target_pairs={{0,16},{4,20},{8,24},{12,28},{16,0},{20,4},{24,8},{28,12},{32,48},... | collective-permute-start | bytes 1572872 | tf_op jit(solution)/shard_map/ppermute | solution.py:17
  118.4 65.2 %collective-permute-start.17 = (bf16[1024,256]{1,0:T(8,128)(2,1)}, bf16[1024,256]{1,0:T(8,128)(2,1)}, u32[]{:S(2)}, u32[]{:S(2)}) collective-permute-start(bf16[1024,256]{1,0:T(8,128)(2,1)} %get-tuple-element.37), channel_id=1, source_target_pairs={{0,32},{4,36},{8,40},{12,44},{16,48},{20,52},{24,56},{28,60},{32,6... | collective-permute-start | bytes 1572872 | tf_op jit(solution)/shard_map/ppermute | solution.py:17
  120.3 53.9 %collective-permute-start.25 = (bf16[256,2,128]{2,1,0:T(2,128)(2,1)S(1)}, bf16[256,2,128]{2,1,0:T(2,128)(2,1)S(1)}, u32[]{:S(2)}, u32[]{:S(2)}) collective-permute-start(bf16[256,2,128]{2,1,0:T(2,128)(2,1)S(1)} %fusion.34), channel_id=1, source_target_pairs={{0,256},{128,384},{256,0},{384,128},{1,257},{129,385},{257,1},{385... | collective-permute-start | bytes 393224 | tf_op jit(solution)/shard_map/ppermute | solution.py:33
  133.1 50.6 %collective-permute-start.19 = (bf16[1024,256]{1,0:T(8,128)(2,1)}, bf16[1024,256]{1,0:T(8,128)(2,1)}, u32[]{:S(2)}, u32[]{:S(2)}) collective-permute-start(bf16[1024,256]{1,0:T(8,128)(2,1)} %add_convert_fusion), channel_id=1, source_target_pairs={{0,96},{4,100},{8,104},{12,108},{16,112},{20,116},{24,120},{28,124... | collective-permute-start | bytes 1572872 | tf_op jit(solution)/shard_map/ppermute | solution.py:17
  174.2 0.7 copy-start.8
  174.9 26.6 %collective-permute-start.12 = (bf16[2048,256]{1,0:T(8,128)(2,1)S(1)}, bf16[2048,256]{1,0:T(8,128)(2,1)}, u32[]{:S(2)}, u32[]{:S(2)}) collective-permute-start(bf16[2048,256]{1,0:T(8,128)(2,1)S(1)} %bitcast.29), channel_id=1, source_target_pairs={{0,96},{4,100},{8,104},{12,108},{16,112},{20,116},{24,120},{28,124... | collective-permute-start | bytes 3145736 | tf_op jit(solution)/shard_map/ppermute | solution.py:17
  177.8 27.6 %collective-permute-start.11 = (bf16[2048,256]{1,0:T(8,128)(2,1)}, bf16[2048,256]{1,0:T(8,128)(2,1)S(1)}, u32[]{:S(2)}, u32[]{:S(2)}) collective-permute-start(bf16[2048,256]{1,0:T(8,128)(2,1)} %collective-permute-done.10), channel_id=1, source_target_pairs={{0,32},{4,36},{8,40},{12,44},{16,48},{20,52},{24,56},{28,60},{32,6... | collective-permute-start | bytes 3145736 | tf_op jit(solution)/shard_map/ppermute | solution.py:17
  186.2 19.3 %copy-start.1 = (bf16[512,4096]{1,0:T(8,128)(2,1)S(1)}, bf16[512,4096]{1,0:T(8,128)(2,1)}, u32[]{:S(2)}) copy-start(bf16[512,4096]{1,0:T(8,128)(2,1)} %copy-done) | copy-start | bytes 12582916
  186.2 23.6 %collective-permute-start.21 = (bf16[256,256]{1,0:T(8,128)(2,1)S(1)}, bf16[256,256]{1,0:T(8,128)(2,1)S(1)}, u32[]{:S(2)}, u32[]{:S(2)}) collective-permute-start(bf16[256,256]{1,0:T(8,128)(2,1)S(1)} %get-tuple-element.59), channel_id=1, source_target_pairs={{0,4},{4,0},{8,12},{12,8},{16,20},{20,16},{24,28},{28,24},{32,36},... | collective-permute-start | bytes 393224 | tf_op jit(solution)/shard_map/ppermute | solution.py:17
  188.4 21.4 %collective-permute-start.22 = (bf16[256,256]{1,0:T(8,128)(2,1)S(1)}, bf16[256,256]{1,0:T(8,128)(2,1)S(1)}, u32[]{:S(2)}, u32[]{:S(2)}) collective-permute-start(bf16[256,256]{1,0:T(8,128)(2,1)S(1)} %get-tuple-element.58), channel_id=1, source_target_pairs={{0,8},{4,12},{8,0},{12,4},{16,24},{20,28},{24,16},{28,20},{32,40},... | collective-permute-start | bytes 393224 | tf_op jit(solution)/shard_map/ppermute | solution.py:17
  190.4 19.5 %collective-permute-start.23 = (bf16[256,256]{1,0:T(8,128)(2,1)S(1)}, bf16[256,256]{1,0:T(8,128)(2,1)S(1)}, u32[]{:S(2)}, u32[]{:S(2)}) collective-permute-start(bf16[256,256]{1,0:T(8,128)(2,1)S(1)} %get-tuple-element.57), channel_id=1, source_target_pairs={{0,12},{4,8},{8,4},{12,0},{16,28},{20,24},{24,20},{28,16},{32,44},... | collective-permute-start | bytes 393224 | tf_op jit(solution)/shard_map/ppermute | solution.py:17
  205.5 2.2 %copy-start.3 = (bf16[512,4096]{1,0:T(8,128)(2,1)S(1)}, bf16[512,4096]{1,0:T(8,128)(2,1)}, u32[]{:S(2)}) copy-start(bf16[512,4096]{1,0:T(8,128)(2,1)} %copy-done.2) | copy-start | bytes 12582916
  207.7 3.3 %copy-start.6 = (f32[1,256,2,128]{3,2,1,0:T(2,128)S(1)}, f32[1,256,2,128]{3,2,1,0:T(2,128)}, u32[]{:S(2)}) copy-start(f32[1,256,2,128]{3,2,1,0:T(2,128)} %param.11) | copy-start | bytes 786436
  207.7 3.3 %copy-start.7 = (f32[1,256,2,128]{3,2,1,0:T(2,128)S(1)}, f32[1,256,2,128]{3,2,1,0:T(2,128)}, u32[]{:S(2)}) copy-start(f32[1,256,2,128]{3,2,1,0:T(2,128)} %param.12) | copy-start | bytes 786436

commit v3 on v2

--- a/solution.py
+++ b/solution.py
@@ -49,41 +49,43 @@
     side = z // HALF
     y = lax.axis_index("tensor")
 
-    def chunk(j, other):
-        start = (x + j) % NX * (NZ * depth) + (side ^ other) * part
-        return lax.dynamic_slice_in_dim(tokens, start, part, axis=1)
+    def lot(half):
+        starts = [(x + j) % NX * (NZ * depth) + half * part for j in (2, 1, 3, 0)]
+        return jnp.concatenate(
+            [lax.dynamic_slice_in_dim(tokens, start, part, axis=1) for start in starts], axis=1
+        )
 
-    held = []
-    ready = ()
-    for other in (1, 0):
-        sent = jnp.concatenate([chunk(j, other) for j in (2, 1, 3, 0)], axis=1)
-        sent = after(sent, *ready)
-        before, behind = move_y(sent, 1), move_y(sent, -1)
-        front, back = lax.optimization_barrier((before[: rows // 2], behind[rows // 2 :]))
-        if other:
-            arrived = front
-        first, second = move_y(front, 1), move_y(back, -1)
-        rest = jnp.concatenate([sent, before, behind], axis=0)
-        rest = lax.optimization_barrier(jnp.pad(rest, ((0, rows), (0, 0))))
-        ready = (rest,)
-        rest = lax.dynamic_update_slice(rest, first, (3 * rows, 0))
-        held.append(lax.dynamic_update_slice(rest, second, (3 * rows + rows // 2, 0)))
-    far_held, near_held = held
+    far_own, near_own = lot(1 - side), lot(side)
+
+    own = after(weights[0], far_own).reshape(1, depth, columns)
+    two = jnp.stack([own, swap_z(own, 4)])
+    four = jnp.stack([two, swap_z(two, 2)])
+
+    far_before, far_behind = move_y(far_own, 1), move_y(far_own, -1)
+    far_before, far_behind, four = lax.optimization_barrier((far_before, far_behind, four))
+    far_opposite = move_y(far_before, 1)
+    near_own, far_behind = lax.optimization_barrier((near_own, far_behind))
+    near_behind = move_y(near_own, -1)
+
+    eight = jnp.stack([four, swap_z(four, 1)])
+    eight = eight.reshape(2, 2, 2, depth, columns)
+    near_behind, far_opposite, eight = lax.optimization_barrier((near_behind, far_opposite, eight))
+    near_opposite = move_y(near_behind, -1)
+    near_own, far_opposite = lax.optimization_barrier((near_own, far_opposite))
+    near_before = move_y(near_own, 1)
+    far_held = jnp.concatenate([far_own, far_before, far_behind, far_opposite], axis=0)
+    near_held = jnp.concatenate([near_own, near_before, near_behind, near_opposite], axis=0)
+
+    eight = jnp.where((z & 1) == 0, eight, eight[::-1])
+    eight = jnp.where((z & 2) == 0, eight, eight[:, ::-1])
+    eight = jnp.where((z & 4) == 0, eight, eight[:, :, ::-1])
+    plane = eight.transpose(2, 1, 0, 3, 4).reshape(2 * part, columns)
+
     cot = cotangent.reshape(NY, rows, columns)
     cot = jnp.concatenate(
         [lax.dynamic_slice_in_dim(cot, (y + k) % NY, 1, axis=0) for k in (0, 3, 1, 2)], axis=0
     ).reshape(NY * rows, columns)
 
-    own = weights[0].reshape(1, depth, columns)
-    two = jnp.stack([own, swap_z(own, 4)])
-    four = jnp.stack([two, swap_z(two, 2)])
-    four = after(four, arrived)
-    eight = jnp.stack([four, swap_z(four, 1)])
-    eight = eight.reshape(2, 2, 2, depth, columns)
-    eight = jnp.where((z & 1) == 0, eight, eight[::-1])
-    eight = jnp.where((z & 2) == 0, eight, eight[:, ::-1])
-    eight = jnp.where((z & 4) == 0, eight, eight[:, :, ::-1])
-    plane = eight.transpose(2, 1, 0, 3, 4).reshape(2 * part, columns)
     def terms(held):
         product = lax.dot_general(held, cot, (((0,), (0,)), ((), ())), preferred_element_type=F32)
         return product.astype(BF16).reshape(NX, part, columns)
@@ -95,17 +97,20 @@
         reverse = move_x(down, -sign)
         return (up.astype(F32) + passed.astype(F32)).astype(BF16), reverse
 
-    def block(value, index, count=1):
-        return lax.dynamic_slice_in_dim(value, index * depth, count * depth, axis=0)
-
     opposite, up, down, here = terms(far_held)
     up, reverse = send_x(opposite, up, down, 1)
+    up, plane = lax.optimization_barrier((up, plane))
     forward = move_x(up, 1)
     far = here.astype(F32) + reverse.astype(F32) + forward.astype(F32)
-    far = far.astype(BF16)
-    crossing = swap_z(far, 4)
+    def halve(value, bit):
+        value = value.reshape(-1, 2, depth, columns)
+        low = (z & bit) == 0
+        kept = jnp.where(low, value[:, 0], value[:, 1])
+        given = jnp.where(low, value[:, 1], value[:, 0])
+        return kept + swap_z(given.astype(BF16), bit).astype(F32)
 
-    plane = after(plane, far)
+    crossing = swap_z(halve(halve(far, 1), 2)[0].astype(BF16), 4).astype(F32)
+
     low = move_x(plane, 1)
     high = move_x(plane, -1)
     planes = {0: plane, 1: high, 2: move_x(low, 1), 3: low}
@@ -113,10 +118,12 @@
     opposite, up, down, here = terms(near_held)
     down, reverse = send_x(opposite, up, down, -1)
     forward = move_x(down, -1)
-    near = here.astype(F32) + reverse.astype(F32) + forward.astype(F32) + crossing.astype(F32)
-    sent = near.astype(BF16)
-    quarter = z % HALF
-    pieces = [swap_z(block(sent, quarter ^ k), k) for k in range(1, HALF)]
+    near = here.astype(F32) + reverse.astype(F32) + forward.astype(F32)
+    groups = [[NZ * i + HALF * h + k for k in range(HALF)] for i in range(NX) for h in range(2)]
+    pieces = lax.all_to_all(
+        near.astype(BF16).reshape(HALF, depth, columns), "fsdp", 0, 0, axis_index_groups=groups
+    )
+
     def half_plane(j, other):
         return lax.dynamic_slice_in_dim(planes[j], (side ^ other) * part, part, axis=0)
 
@@ -133,10 +140,7 @@
         ordered.append(lax.dynamic_slice_in_dim(projected, place, 1, axis=0))
     keys_values = jnp.concatenate(ordered, axis=0).reshape(cotangent.shape)
 
-    pieces = after(pieces, keys_values)
-    gradient = block(near, quarter)
-    for piece in pieces:
-        gradient = gradient + piece.astype(F32)
+    gradient = pieces.astype(F32).sum(axis=0) + crossing
 
     gradient = gradient.reshape(first_moment.shape)
     first_next = 0.9 * first_moment + 0.1 * gradient
@@ -147,7 +151,7 @@
 
     local_float = frag_local[0].astype(F32)
     pair = (local_float + swap_replica(frag_local[0], 1).astype(F32)).astype(BF16)
-    summed = pair.astype(F32) + swap_replica(after(pair, far), 2).astype(F32)
+    summed = pair.astype(F32) + swap_replica(after(pair, eight), 2).astype(F32)
     outer_step = frag_global - summed / lax.axis_size("replica")
     moment_next = 0.9 * frag_moment + outer_step
     global_next = frag_global - 0.7 * (outer_step + 0.9 * moment_next)

time: 214 us -> 207 us (0.967)
  the two profiles are of different devices: /device:TPU:88 before, /device:TPU:6 now
where the time goes in v3:
time: 207 us; the launch traced here: 206 us
  starting transfers between devices  95.9 us (46%)
  waiting for transfers between devices  58.7 us (28%)
  matrix products  29.6 us (14%)
  other arithmetic  10 us (5%)
  local copies, waits for them, and re-layouts  9.86 us (5%)
    ppermute x15, waiting for transfers between devices, move(): return lax.ppermute(value, 'fsdp', pairs)  56.6 us
    ppermute x15, starting transfers between devices, move(): return lax.ppermute(value, 'fsdp', pairs)  46.8 us
    ppermute x2, starting transfers between devices, swap_replica(): lax.ppermute(value, 'replica', [(r, r ^ bit) for r in range(lax.axis_size...  25.5 us
    dot_general x2, matrix products, project(): return jnp.dot(held, matrix, preferred_element_type=F32)  23 us
    ppermute x6, starting transfers between devices, move_y(): lax.ppermute(value, 'tensor', [(y, (y + shift) % NY) for y in range(NY)])  20 us
    dot_general x2, matrix products, terms(): lax.dot_general(held, cot, (((0,), (0,)), ((), ())), preferred_element_ty...  6.56 us
  transfers between devices with their start and end apart: 24, of which 9 were waited for; matrix products, arithmetic and copies ran while one was open for 19% of the time, Pallas kernels for 0%

profile of v3, /device:TPU:6, one launch (start us, length us, event | category | flops | bytes accessed | tf_op | source)
XLA Modules:
  0.0 205.7 jit_solution(13212109069512159301)
XLA Ops:
  0.8 2.5 %constant_dynamic-slice_fusion.23 = (bf16[128,1024]{1,0:T(8,128)(2,1)S(1)}, bf16[128,1024]{1,0:T(8,128)(2,1)S(1)}, bf16[128,1024]{1,0:T(8,128)(2,1)S(1)}, bf16[1...) fusion(bf16[128,8192]{1,0:T(8,128)(2,1)} %param.8, ...), kind=kLoop, calls=%fused_computation.92 | loop fusion | bytes 4194336 | tf_op jit(solution)/shard_map/dynamic_slice | solution.py:55
  3.3 3.5 %collective-permute-start = (bf16[128,4096]{1,0:T(8,128)(2,1)S(1)}, bf16[128,4096]{1,0:T(8,128)(2,1)}, u32[]{:S(2)}, u32[]{:S(2)}) collective-permute-start(bf16[128,4096]{1,0:T(8,128)(2,1)S(1)} %pad_maximum_fusion.1), channel_id=1, source_target_pairs={{0,1},{1,2},{2,3},{3,0},{4,5},{5,6},{6,7},{7,4},{8,9},{9,10},{10,1... | collective-permute-start | bytes 3145736 | tf_op jit(solution)/shard_map/ppermute | solution.py:25
  6.8 3.6 %collective-permute-start.1 = (bf16[128,4096]{1,0:T(8,128)(2,1)S(1)}, bf16[128,4096]{1,0:T(8,128)(2,1)}, u32[]{:S(2)}, u32[]{:S(2)}) collective-permute-start(bf16[128,4096]{1,0:T(8,128)(2,1)S(1)} %pad_maximum_fusion.1), channel_id=1, source_target_pairs={{0,3},{1,0},{2,1},{3,2},{4,7},{5,4},{6,5},{7,6},{8,11},{9,8},{10,9... | collective-permute-start | bytes 3145736 | tf_op jit(solution)/shard_map/ppermute | solution.py:25
  10.4 0.1 reshape.156
  10.5 9.1 %collective-permute-start.2 = (bf16[1,256,256]{2,1,0:T(8,128)(2,1)S(1)}, bf16[1,256,256]{2,1,0:T(8,128)(2,1)S(1)}, u32[]{:S(2)}, u32[]{:S(2)}) collective-permute-start(bf16[1,256,256]{2,1,0:T(8,128)(2,1)S(1)} %reshape.156), channel_id=1, source_target_pairs={{0,16},{4,20},{8,24},{12,28},{16,0},{20,4},{24,8},{28,12},{32,48},... | collective-permute-start | bytes 393224 | tf_op jit(solution)/shard_map/ppermute | solution.py:17
  19.7 0.1 stack_reshape.3
  19.7 11.3 %collective-permute-done.2 = bf16[1,256,256]{2,1,0:T(8,128)(2,1)S(1)} collective-permute-done((bf16[1,256,256]{2,1,0:T(8,128)(2,1)S(1)}, bf16[1,256,256]{2,1,0:T(8,128)(2,1)S(1)}, u32[]{:S(2)}, u32[]{:S(2)}) %collective-permute-start.2) | collective-permute-done | bytes 131104 | tf_op jit(solution)/shard_map/ppermute | solution.py:17
  31.1 1.9 collective-permute-start.3
  33.0 1.0 pad_maximum_fusion.2
  34.1 10.8 %collective-permute-done.3 = bf16[2,1,256,256]{3,2,0,1:T(8,128)(2,1)S(1)} collective-permute-done((bf16[2,1,256,256]{3,2,0,1:T(8,128)(2,1)S(1)}, bf16[2,1,256,256]{3,2,0,1:T(8,128)(2,1)S(1)}, u32[]{:S(2)}, u32[]{:S(2)}) %collective-permute-start.3) | collective-permute-done | bytes 262176 | tf_op jit(solution)/shard_map/ppermute | solution.py:17
  44.9 3.6 %collective-permute-start.4 = (bf16[128,4096]{1,0:T(8,128)(2,1)S(1)}, bf16[128,4096]{1,0:T(8,128)(2,1)S(1)}, u32[]{:S(2)}, u32[]{:S(2)}) collective-permute-start(bf16[128,4096]{1,0:T(8,128)(2,1)S(1)} %pad_maximum_fusion.2), channel_id=1, source_target_pairs={{0,3},{1,0},{2,1},{3,2},{4,7},{5,4},{6,5},{7,6},{8,11},{9,8},{10,9... | collective-permute-start | bytes 3145736 | tf_op jit(solution)/shard_map/ppermute | solution.py:25
  48.5 2.2 %collective-permute-start.5 = (bf16[128,4096]{1,0:T(8,128)(2,1)}, bf16[128,4096]{1,0:T(8,128)(2,1)}, u32[]{:S(2)}, u32[]{:S(2)}) collective-permute-start(bf16[128,4096]{1,0:T(8,128)(2,1)} %collective-permute-done), channel_id=1, source_target_pairs={{0,1},{1,2},{2,3},{3,0},{4,5},{5,6},{6,7},{7,4},{8,9},{9,10},{10,1... | collective-permute-start | bytes 3145736 | tf_op jit(solution)/shard_map/ppermute | solution.py:25
  50.8 1.9 collective-permute-start.6
  52.7 1.9 collective-permute-start.21
  54.7 1.1 reshape.158
  55.8 0.7 constant_dynamic-slice_fusion.15
  56.5 1.0 pad_maximum_fusion.5
  57.5 1.1 fusion.27
  58.6 5.6 %collective-permute-done.6 = bf16[2,2,1,256,256]{4,3,0,1,2:T(8,128)(2,1)} collective-permute-done((bf16[2,2,1,256,256]{4,3,0,1,2:T(8,128)(2,1)S(1)}, bf16[2,2,1,256,256]{4,3,0,1,2:T(8,128)(2,1)}, u32[]{:S(2)}, u32[]{:S(2)}) %collective-permute-start.6) | collective-permute-done | bytes 524320 | tf_op jit(solution)/shard_map/ppermute | solution.py:17
  64.2 1.1 maximum_bitcast_fusion
  65.3 2.1 %collective-permute-done.5 = bf16[128,4096]{1,0:T(8,128)(2,1)} collective-permute-done((bf16[128,4096]{1,0:T(8,128)(2,1)}, bf16[128,4096]{1,0:T(8,128)(2,1)}, u32[]{:S(2)}, u32[]{:S(2)}) %collective-permute-start.5) | collective-permute-done | bytes 1048608 | tf_op jit(solution)/shard_map/ppermute | solution.py:25
  67.5 5.2 %convolution_convert_fusion.1 = bf16[4096,256]{1,0:T(8,128)(2,1)S(1)} fusion(bf16[512,256]{1,0:T(8,128)(2,1)S(1)} %bitcast.74, bf16[128,4096]{1,0:T(8,128)(2,1)} %collective-permute-done.5, bf16[128,4096]{1,0:T(8,128)(2,1)} %collective-permute-done.1, bf16[128,4096]{1,0:T(8,128)(2,1)} %collective-permute-done, bf16[128,1024]{1,0:T(8,128)(2,1)S(1)} %get-tuple-element.48, ...), kind=kOutput, calls=%fused_computation.1 | convolution fusion | flops 1104150528 | bytes 6553600 | tf_op jit(solution)/shard_map/dot_general | solution.py:90
  72.8 2.4 %collective-permute-start.7 = (bf16[1024,256]{1,0:T(8,128)(2,1)S(1)}, bf16[1024,256]{1,0:T(8,128)(2,1)S(1)}, u32[]{:S(2)}, u32[]{:S(2)}) collective-permute-start(bf16[1024,256]{1,0:T(8,128)(2,1)S(1)} %get-tuple-element.42), channel_id=1, source_target_pairs={{0,32},{4,36},{8,40},{12,44},{16,48},{20,52},{24,56},{28,60},{32,6... | collective-permute-start | bytes 1572872 | tf_op jit(solution)/shard_map/ppermute | solution.py:17
  75.2 3.5 %collective-permute-start.16 = (bf16[1024,256]{1,0:T(8,128)(2,1)S(1)}, bf16[1024,256]{1,0:T(8,128)(2,1)S(1)}, u32[]{:S(2)}, u32[]{:S(2)}) collective-permute-start(bf16[1024,256]{1,0:T(8,128)(2,1)S(1)} %get-tuple-element.41), channel_id=1, source_target_pairs={{0,96},{4,100},{8,104},{12,108},{16,112},{20,116},{24,120},{28,124... | collective-permute-start | bytes 1572872 | tf_op jit(solution)/shard_map/ppermute | solution.py:17
  78.7 1.9 collective-permute-start.11
  80.6 5.1 %collective-permute-start.12 = (bf16[128,4096]{1,0:T(8,128)(2,1)S(1)}, bf16[128,4096]{1,0:T(8,128)(2,1)S(1)}, u32[]{:S(2)}, u32[]{:S(2)}) collective-permute-start(bf16[128,4096]{1,0:T(8,128)(2,1)S(1)} %collective-permute-done.4), channel_id=1, source_target_pairs={{0,3},{1,0},{2,1},{3,2},{4,7},{5,4},{6,5},{7,6},{8,11},{9,8},{10,9... | collective-permute-start | bytes 3145736 | tf_op jit(solution)/shard_map/ppermute | solution.py:25
  85.7 0.2 reverse_select_fusion.2
  85.9 0.2 reverse_select_fusion.1
  86.2 0.2 reverse_select_fusion
  86.4 23.6 %collective-permute-start.22 = (bf16[256,2,128]{2,1,0:T(2,128)(2,1)S(1)}, bf16[256,2,128]{2,1,0:T(2,128)(2,1)S(1)}, u32[]{:S(2)}, u32[]{:S(2)}) collective-permute-start(bf16[256,2,128]{2,1,0:T(2,128)(2,1)S(1)} %fusion.27), channel_id=1, source_target_pairs={{0,256},{128,384},{256,0},{384,128},{1,257},{129,385},{257,1},{385... | collective-permute-start | bytes 393224 | tf_op jit(solution)/shard_map/ppermute | solution.py:33
  110.1 0.2 add_convert_fusion.2
  110.2 3.6 %collective-permute-start.17 = (bf16[1024,256]{1,0:T(8,128)(2,1)S(1)}, bf16[1024,256]{1,0:T(8,128)(2,1)S(1)}, u32[]{:S(2)}, u32[]{:S(2)}) collective-permute-start(bf16[1024,256]{1,0:T(8,128)(2,1)S(1)} %add_convert_fusion.2), channel_id=1, source_target_pairs={{0,32},{4,36},{8,40},{12,44},{16,48},{20,52},{24,56},{28,60},{32,6... | collective-permute-start | bytes 1572872 | tf_op jit(solution)/shard_map/ppermute | solution.py:17
  113.8 2.2 %collective-permute-start.8 = (bf16[2048,256]{1,0:T(8,128)(2,1)S(1)}, bf16[2048,256]{1,0:T(8,128)(2,1)S(1)}, u32[]{:S(2)}, u32[]{:S(2)}) collective-permute-start(bf16[2048,256]{1,0:T(8,128)(2,1)S(1)} %bitcast.67), channel_id=1, source_target_pairs={{0,32},{4,36},{8,40},{12,44},{16,48},{20,52},{24,56},{28,60},{32,6... | collective-permute-start | bytes 3145736 | tf_op jit(solution)/shard_map/ppermute | solution.py:17
  116.0 0.1 constant_dynamic-update-slice_fusion.2
  116.2 0.1 constant_dynamic-update-slice_fusion
  116.3 1.3 convolution_convert_fusion
  117.6 0.6 copy-done.9
  118.3 8.7 %collective-permute-done.17 = bf16[1024,256]{1,0:T(8,128)(2,1)S(1)} collective-permute-done((bf16[1024,256]{1,0:T(8,128)(2,1)S(1)}, bf16[1024,256]{1,0:T(8,128)(2,1)S(1)}, u32[]{:S(2)}, u32[]{:S(2)}) %collective-permute-start.17) | collective-permute-done | bytes 524320 | tf_op jit(solution)/shard_map/ppermute | solution.py:17
  127.0 0.2 convert_add_fusion
  127.3 1.9 collective-permute-start.18
  129.3 2.7 %collective-permute-start.14 = (bf16[1024,256]{1,0:T(8,128)(2,1)S(1)}, bf16[1024,256]{1,0:T(8,128)(2,1)S(1)}, u32[]{:S(2)}, u32[]{:S(2)}) collective-permute-start(bf16[1024,256]{1,0:T(8,128)(2,1)S(1)} %get-tuple-element.44), channel_id=1, source_target_pairs={{0,96},{4,100},{8,104},{12,108},{16,112},{20,116},{24,120},{28,124... | collective-permute-start | bytes 1572872 | tf_op jit(solution)/shard_map/ppermute | solution.py:17
  132.1 1.3 fusion.36
  133.4 2.4 %collective-permute-start.10 = (bf16[2048,256]{1,0:T(8,128)(2,1)S(1)}, bf16[2048,256]{1,0:T(8,128)(2,1)S(1)}, u32[]{:S(2)}, u32[]{:S(2)}) collective-permute-start(bf16[2048,256]{1,0:T(8,128)(2,1)S(1)} %bitcast.68), channel_id=1, source_target_pairs={{0,96},{4,100},{8,104},{12,108},{16,112},{20,116},{24,120},{28,124... | collective-permute-start | bytes 3145736 | tf_op jit(solution)/shard_map/ppermute | solution.py:17
  135.8 4.6 %collective-permute-start.13 = (bf16[1024,256]{1,0:T(8,128)(2,1)S(1)}, bf16[1024,256]{1,0:T(8,128)(2,1)S(1)}, u32[]{:S(2)}, u32[]{:S(2)}) collective-permute-start(bf16[1024,256]{1,0:T(8,128)(2,1)S(1)} %get-tuple-element.43), channel_id=1, source_target_pairs={{0,32},{4,36},{8,40},{12,44},{16,48},{20,52},{24,56},{28,60},{32,6... | collective-permute-start | bytes 1572872 | tf_op jit(solution)/shard_map/ppermute | solution.py:17
  140.4 0.1 fusion.24
  140.6 1.9 collective-permute-start.19
  142.5 6.9 %collective-permute-done.8 = bf16[2048,256]{1,0:T(8,128)(2,1)S(1)} collective-permute-done((bf16[2048,256]{1,0:T(8,128)(2,1)S(1)}, bf16[2048,256]{1,0:T(8,128)(2,1)S(1)}, u32[]{:S(2)}, u32[]{:S(2)}) %collective-permute-start.8) | collective-permute-done | bytes 1048608 | tf_op jit(solution)/shard_map/ppermute | solution.py:17
  149.4 4.8 %collective-permute-start.9 = (bf16[2048,256]{1,0:T(8,128)(2,1)S(1)}, bf16[2048,256]{1,0:T(8,128)(2,1)S(1)}, u32[]{:S(2)}, u32[]{:S(2)}) collective-permute-start(bf16[2048,256]{1,0:T(8,128)(2,1)S(1)} %collective-permute-done.8), channel_id=1, source_target_pairs={{0,32},{4,36},{8,40},{12,44},{16,48},{20,52},{24,56},{28,60},{32,6... | collective-permute-start | bytes 3145736 | tf_op jit(solution)/shard_map/ppermute | solution.py:17
  154.3 0.1 add_convert_fusion.1
  154.4 1.9 collective-permute-start.15
  156.3 1.1 constant_dynamic-slice_fusion.8
  157.5 1.9 collective-permute-start.20
  159.4 1.1 constant_dynamic-slice_fusion.9
  160.5 6.8 %collective-permute-done.10 = bf16[2048,256]{1,0:T(8,128)(2,1)S(1)} collective-permute-done((bf16[2048,256]{1,0:T(8,128)(2,1)S(1)}, bf16[2048,256]{1,0:T(8,128)(2,1)S(1)}, u32[]{:S(2)}, u32[]{:S(2)}) %collective-permute-start.10) | collective-permute-done | bytes 1048608 | tf_op jit(solution)/shard_map/ppermute | solution.py:17
  167.2 1.0 constant_dynamic-slice_fusion.10
  168.3 4.6 %collective-permute-done.15 = bf16[1024,256]{1,0:T(8,128)(2,1)S(1)} collective-permute-done((bf16[1024,256]{1,0:T(8,128)(2,1)S(1)}, bf16[1024,256]{1,0:T(8,128)(2,1)S(1)}, u32[]{:S(2)}, u32[]{:S(2)}) %collective-permute-start.15) | collective-permute-done | bytes 524320 | tf_op jit(solution)/shard_map/ppermute | solution.py:17
  172.9 1.1 add_convert_fusion
  174.0 3.6 %all-to-all-start = ((bf16[4,256,256]{2,1,0:T(8,128)(2,1)}), bf16[4,256,256]{2,1,0:T(8,128)(2,1)S(1)}, u32[]{:S(2)}, u32[]{:S(2)}) async-start(bf16[4,256,256]{2,1,0:T(8,128)(2,1)} %bitcast.13), calls=%async_computation | async-start | bytes 1048576 | tf_op jit(solution)/shard_map/all_to_all | solution.py:123
  177.6 2.0 collective-permute-done.9
  179.7 4.0 %fusion.8 = f32[512,256]{1,0:T(8,128)S(1)} fusion(bf16[512,4096]{1,0:T(8,128)(2,1)} %copy-done.9, bf16[1024,256]{1,0:T(8,128)(2,1)} %get-tuple-element.60, bf16[1024,256]{1,0:T(8,128)(2,1)} %get-tuple-element.58, bf16[1024,256]{1,0:T(8,128)(2,1)} %get-tuple-element.56, bf16[1024,256]{1,0:T(8,128)(2,1)S(1)} %get-tuple-element.54), kind=kOutput, calls=%fused_computation.11 | convolution fusion | flops 1082130432 | bytes 6815744 | tf_op jit(solution)/shard_map/dot_general | solution.py:132
  183.8 19.0 %fusion.19 = bf16[512,256]{1,0:T(8,128)(2,1)S(1)} fusion(f32[512,256]{1,0:T(8,128)S(1)} %fusion.8, bf16[1024,256]{1,0:T(8,128)(2,1)S(1)} %copy-done.6, bf16[1024,256]{1,0:T(8,128)(2,1)S(1)} %copy-done.7, bf16[1024,256]{1,0:T(8,128)(2,1)S(1)} %copy-done.8, bf16[1024,256]{1,0:T(8,128)(2,1)S(1)} %get-tuple-element.53, ...), kind=kOutput, calls=%fused_computation.23 | convolution fusion | flops 1111752704 | bytes 7077888 | tf_op jit(solution)/shard_map/dot_general | solution.py:132
  202.9 0.8 reshape.162
  203.8 0.1 reshape.166
  204.0 1.7 fusion.33
  (57 shorter events, 0.9 us)
Async XLA Ops:
  0.6 9.8 %copy-start = (bf16[1,256,2,128]{3,2,1,0:T(2,128)(2,1)S(1)}, bf16[1,256,2,128]{3,2,1,0:T(2,128)(2,1)}, u32[]{:S(2)}) copy-start(bf16[1,256,2,128]{3,2,1,0:T(2,128)(2,1)} %param.10) | copy-start | bytes 393220
  3.3 7.2 %copy-start.1 = (bf16[128,1024]{1,0:T(8,128)(2,1)}, bf16[128,1024]{1,0:T(8,128)(2,1)S(1)}, u32[]{:S(2)}) copy-start(bf16[128,1024]{1,0:T(8,128)(2,1)S(1)} %get-tuple-element.49) | copy-start | bytes 786436
  3.3 7.2 %copy-start.3 = (bf16[128,1024]{1,0:T(8,128)(2,1)}, bf16[128,1024]{1,0:T(8,128)(2,1)S(1)}, u32[]{:S(2)}) copy-start(bf16[128,1024]{1,0:T(8,128)(2,1)S(1)} %get-tuple-element.50) | copy-start | bytes 786436
  3.3 41.5 %collective-permute-start = (bf16[128,4096]{1,0:T(8,128)(2,1)S(1)}, bf16[128,4096]{1,0:T(8,128)(2,1)}, u32[]{:S(2)}, u32[]{:S(2)}) collective-permute-start(bf16[128,4096]{1,0:T(8,128)(2,1)S(1)} %pad_maximum_fusion.1), channel_id=1, source_target_pairs={{0,1},{1,2},{2,3},{3,0},{4,5},{5,6},{6,7},{7,4},{8,9},{9,10},{10,1... | collective-permute-start | bytes 3145736 | tf_op jit(solution)/shard_map/ppermute | solution.py:25
  6.8 38.0 %collective-permute-start.1 = (bf16[128,4096]{1,0:T(8,128)(2,1)S(1)}, bf16[128,4096]{1,0:T(8,128)(2,1)}, u32[]{:S(2)}, u32[]{:S(2)}) collective-permute-start(bf16[128,4096]{1,0:T(8,128)(2,1)S(1)} %pad_maximum_fusion.1), channel_id=1, source_target_pairs={{0,3},{1,0},{2,1},{3,2},{4,7},{5,4},{6,5},{7,6},{8,11},{9,8},{10,9... | collective-permute-start | bytes 3145736 | tf_op jit(solution)/shard_map/ppermute | solution.py:25
  10.5 20.5 %collective-permute-start.2 = (bf16[1,256,256]{2,1,0:T(8,128)(2,1)S(1)}, bf16[1,256,256]{2,1,0:T(8,128)(2,1)S(1)}, u32[]{:S(2)}, u32[]{:S(2)}) collective-permute-start(bf16[1,256,256]{2,1,0:T(8,128)(2,1)S(1)} %reshape.156), channel_id=1, source_target_pairs={{0,16},{4,20},{8,24},{12,28},{16,0},{20,4},{24,8},{28,12},{32,48},... | collective-permute-start | bytes 393224 | tf_op jit(solution)/shard_map/ppermute | solution.py:17
  31.1 13.7 %collective-permute-start.3 = (bf16[2,1,256,256]{3,2,0,1:T(8,128)(2,1)S(1)}, bf16[2,1,256,256]{3,2,0,1:T(8,128)(2,1)S(1)}, u32[]{:S(2)}, u32[]{:S(2)}) collective-permute-start(bf16[2,1,256,256]{3,2,0,1:T(8,128)(2,1)S(1)} %get-tuple-element.70), channel_id=1, source_target_pairs={{0,8},{4,12},{8,0},{12,4},{16,24},{20,28},{24,16},{28,20},{32,40},... | collective-permute-start | bytes 786440 | tf_op jit(solution)/shard_map/ppermute | solution.py:17
  44.9 20.4 %collective-permute-start.4 = (bf16[128,4096]{1,0:T(8,128)(2,1)S(1)}, bf16[128,4096]{1,0:T(8,128)(2,1)S(1)}, u32[]{:S(2)}, u32[]{:S(2)}) collective-permute-start(bf16[128,4096]{1,0:T(8,128)(2,1)S(1)} %pad_maximum_fusion.2), channel_id=1, source_target_pairs={{0,3},{1,0},{2,1},{3,2},{4,7},{5,4},{6,5},{7,6},{8,11},{9,8},{10,9... | collective-permute-start | bytes 3145736 | tf_op jit(solution)/shard_map/ppermute | solution.py:25
  48.5 18.9 %collective-permute-start.5 = (bf16[128,4096]{1,0:T(8,128)(2,1)}, bf16[128,4096]{1,0:T(8,128)(2,1)}, u32[]{:S(2)}, u32[]{:S(2)}) collective-permute-start(bf16[128,4096]{1,0:T(8,128)(2,1)} %collective-permute-done), channel_id=1, source_target_pairs={{0,1},{1,2},{2,3},{3,0},{4,5},{5,6},{6,7},{7,4},{8,9},{9,10},{10,1... | collective-permute-start | bytes 3145736 | tf_op jit(solution)/shard_map/ppermute | solution.py:25
  50.8 13.4 %collective-permute-start.6 = (bf16[2,2,1,256,256]{4,3,0,1,2:T(8,128)(2,1)S(1)}, bf16[2,2,1,256,256]{4,3,0,1,2:T(8,128)(2,1)}, u32[]{:S(2)}, u32[]{:S(2)}) collective-permute-start(bf16[2,2,1,256,256]{4,3,0,1,2:T(8,128)(2,1)S(1)} %pad_maximum_fusion.3), channel_id=1, source_target_pairs={{0,4},{4,0},{8,12},{12,8},{16,20},{20,16},{24,28},{28,24},{32,36},... | collective-permute-start | bytes 1572872 | tf_op jit(solution)/shard_map/ppermute | solution.py:17
  52.7 4.8 %collective-permute-start.21 = (bf16[256,2,128]{2,1,0:T(2,128)(2,1)}, bf16[256,2,128]{2,1,0:T(2,128)(2,1)}, u32[]{:S(2)}, u32[]{:S(2)}) collective-permute-start(bf16[256,2,128]{2,1,0:T(2,128)(2,1)} %bitcast.73), channel_id=1, source_target_pairs={{0,128},{128,0},{256,384},{384,256},{1,129},{129,1},{257,385},{385... | collective-permute-start | bytes 393224 | tf_op jit(solution)/shard_map/ppermute | solution.py:33
  72.8 37.3 %collective-permute-start.7 = (bf16[1024,256]{1,0:T(8,128)(2,1)S(1)}, bf16[1024,256]{1,0:T(8,128)(2,1)S(1)}, u32[]{:S(2)}, u32[]{:S(2)}) collective-permute-start(bf16[1024,256]{1,0:T(8,128)(2,1)S(1)} %get-tuple-element.42), channel_id=1, source_target_pairs={{0,32},{4,36},{8,40},{12,44},{16,48},{20,52},{24,56},{28,60},{32,6... | collective-permute-start | bytes 1572872 | tf_op jit(solution)/shard_map/ppermute | solution.py:17
  75.2 43.1 %collective-permute-start.16 = (bf16[1024,256]{1,0:T(8,128)(2,1)S(1)}, bf16[1024,256]{1,0:T(8,128)(2,1)S(1)}, u32[]{:S(2)}, u32[]{:S(2)}) collective-permute-start(bf16[1024,256]{1,0:T(8,128)(2,1)S(1)} %get-tuple-element.41), channel_id=1, source_target_pairs={{0,96},{4,100},{8,104},{12,108},{16,112},{20,116},{24,120},{28,124... | collective-permute-start | bytes 1572872 | tf_op jit(solution)/shard_map/ppermute | solution.py:17
  78.7 35.2 %collective-permute-start.11 = (bf16[128,4096]{1,0:T(8,128)(2,1)S(1)}, bf16[128,4096]{1,0:T(8,128)(2,1)S(1)}, u32[]{:S(2)}, u32[]{:S(2)}) collective-permute-start(bf16[128,4096]{1,0:T(8,128)(2,1)S(1)} %pad_maximum_fusion.2), channel_id=1, source_target_pairs={{0,1},{1,2},{2,3},{3,0},{4,5},{5,6},{6,7},{7,4},{8,9},{9,10},{10,1... | collective-permute-start | bytes 3145736 | tf_op jit(solution)/shard_map/ppermute | solution.py:25
  80.6 35.6 %collective-permute-start.12 = (bf16[128,4096]{1,0:T(8,128)(2,1)S(1)}, bf16[128,4096]{1,0:T(8,128)(2,1)S(1)}, u32[]{:S(2)}, u32[]{:S(2)}) collective-permute-start(bf16[128,4096]{1,0:T(8,128)(2,1)S(1)} %collective-permute-done.4), channel_id=1, source_target_pairs={{0,3},{1,0},{2,1},{3,2},{4,7},{5,4},{6,5},{7,6},{8,11},{9,8},{10,9... | collective-permute-start | bytes 3145736 | tf_op jit(solution)/shard_map/ppermute | solution.py:25
  86.4 45.6 %collective-permute-start.22 = (bf16[256,2,128]{2,1,0:T(2,128)(2,1)S(1)}, bf16[256,2,128]{2,1,0:T(2,128)(2,1)S(1)}, u32[]{:S(2)}, u32[]{:S(2)}) collective-permute-start(bf16[256,2,128]{2,1,0:T(2,128)(2,1)S(1)} %fusion.27), channel_id=1, source_target_pairs={{0,256},{128,384},{256,0},{384,128},{1,257},{129,385},{257,1},{385... | collective-permute-start | bytes 393224 | tf_op jit(solution)/shard_map/ppermute | solution.py:33
  110.2 16.8 %collective-permute-start.17 = (bf16[1024,256]{1,0:T(8,128)(2,1)S(1)}, bf16[1024,256]{1,0:T(8,128)(2,1)S(1)}, u32[]{:S(2)}, u32[]{:S(2)}) collective-permute-start(bf16[1024,256]{1,0:T(8,128)(2,1)S(1)} %add_convert_fusion.2), channel_id=1, source_target_pairs={{0,32},{4,36},{8,40},{12,44},{16,48},{20,52},{24,56},{28,60},{32,6... | collective-permute-start | bytes 1572872 | tf_op jit(solution)/shard_map/ppermute | solution.py:17
  113.8 35.6 %collective-permute-start.8 = (bf16[2048,256]{1,0:T(8,128)(2,1)S(1)}, bf16[2048,256]{1,0:T(8,128)(2,1)S(1)}, u32[]{:S(2)}, u32[]{:S(2)}) collective-permute-start(bf16[2048,256]{1,0:T(8,128)(2,1)S(1)} %bitcast.67), channel_id=1, source_target_pairs={{0,32},{4,36},{8,40},{12,44},{16,48},{20,52},{24,56},{28,60},{32,6... | collective-permute-start | bytes 3145736 | tf_op jit(solution)/shard_map/ppermute | solution.py:17
  116.3 2.0 copy-start.9
  118.3 13.7 %copy-start.5 = (bf16[1,256,2,128]{3,2,1,0:T(2,128)(2,1)S(1)}, bf16[1,256,2,128]{3,2,1,0:T(2,128)(2,1)}, u32[]{:S(2)}) copy-start(bf16[1,256,2,128]{3,2,1,0:T(2,128)(2,1)} %param.15) | copy-start | bytes 393220
  118.3 13.8 %copy-start.10 = (f32[256,2,128]{2,1,0:T(2,128)S(1)}, f32[256,2,128]{2,1,0:T(2,128)}, u32[]{:S(2)}) copy-start(f32[256,2,128]{2,1,0:T(2,128)} %param.13) | copy-start | bytes 786436
  118.3 13.8 %copy-start.11 = (f32[256,2,128]{2,1,0:T(2,128)S(1)}, f32[256,2,128]{2,1,0:T(2,128)}, u32[]{:S(2)}) copy-start(f32[256,2,128]{2,1,0:T(2,128)} %param.14) | copy-start | bytes 786436
  127.3 13.2 %collective-permute-start.18 = (bf16[2,256,256]{2,1,0:T(8,128)(2,1)S(1)}, bf16[2,256,256]{2,1,0:T(8,128)(2,1)S(1)}, u32[]{:S(2)}, u32[]{:S(2)}) collective-permute-start(bf16[2,256,256]{2,1,0:T(8,128)(2,1)S(1)} %fusion.31), channel_id=1, source_target_pairs={{0,4},{4,0},{8,12},{12,8},{16,20},{20,16},{24,28},{28,24},{32,36},... | collective-permute-start | bytes 786440 | tf_op jit(solution)/shard_map/ppermute | solution.py:17
  129.3 25.0 %collective-permute-start.14 = (bf16[1024,256]{1,0:T(8,128)(2,1)S(1)}, bf16[1024,256]{1,0:T(8,128)(2,1)S(1)}, u32[]{:S(2)}, u32[]{:S(2)}) collective-permute-start(bf16[1024,256]{1,0:T(8,128)(2,1)S(1)} %get-tuple-element.44), channel_id=1, source_target_pairs={{0,96},{4,100},{8,104},{12,108},{16,112},{20,116},{24,120},{28,124... | collective-permute-start | bytes 1572872 | tf_op jit(solution)/shard_map/ppermute | solution.py:17
  133.4 33.9 %collective-permute-start.10 = (bf16[2048,256]{1,0:T(8,128)(2,1)S(1)}, bf16[2048,256]{1,0:T(8,128)(2,1)S(1)}, u32[]{:S(2)}, u32[]{:S(2)}) collective-permute-start(bf16[2048,256]{1,0:T(8,128)(2,1)S(1)} %bitcast.68), channel_id=1, source_target_pairs={{0,96},{4,100},{8,104},{12,108},{16,112},{20,116},{24,120},{28,124... | collective-permute-start | bytes 3145736 | tf_op jit(solution)/shard_map/ppermute | solution.py:17
  135.8 32.5 %collective-permute-start.13 = (bf16[1024,256]{1,0:T(8,128)(2,1)S(1)}, bf16[1024,256]{1,0:T(8,128)(2,1)S(1)}, u32[]{:S(2)}, u32[]{:S(2)}) collective-permute-start(bf16[1024,256]{1,0:T(8,128)(2,1)S(1)} %get-tuple-element.43), channel_id=1, source_target_pairs={{0,32},{4,36},{8,40},{12,44},{16,48},{20,52},{24,56},{28,60},{32,6... | collective-permute-start | bytes 1572872 | tf_op jit(solution)/shard_map/ppermute | solution.py:17
  140.6 16.9 %collective-permute-start.19 = (bf16[1,256,256]{2,1,0:T(8,128)(2,1)S(1)}, bf16[1,256,256]{2,1,0:T(8,128)(2,1)S(1)}, u32[]{:S(2)}, u32[]{:S(2)}) collective-permute-start(bf16[1,256,256]{2,1,0:T(8,128)(2,1)S(1)} %fusion.34), channel_id=1, source_target_pairs={{0,8},{4,12},{8,0},{12,4},{16,24},{20,28},{24,16},{28,20},{32,40},... | collective-permute-start | bytes 393224 | tf_op jit(solution)/shard_map/ppermute | solution.py:17
  149.4 30.1 %collective-permute-start.9 = (bf16[2048,256]{1,0:T(8,128)(2,1)S(1)}, bf16[2048,256]{1,0:T(8,128)(2,1)S(1)}, u32[]{:S(2)}, u32[]{:S(2)}) collective-permute-start(bf16[2048,256]{1,0:T(8,128)(2,1)S(1)} %collective-permute-done.8), channel_id=1, source_target_pairs={{0,32},{4,36},{8,40},{12,44},{16,48},{20,52},{24,56},{28,60},{32,6... | collective-permute-start | bytes 3145736 | tf_op jit(solution)/shard_map/ppermute | solution.py:17
  154.4 18.5 %collective-permute-start.15 = (bf16[1024,256]{1,0:T(8,128)(2,1)S(1)}, bf16[1024,256]{1,0:T(8,128)(2,1)S(1)}, u32[]{:S(2)}, u32[]{:S(2)}) collective-permute-start(bf16[1024,256]{1,0:T(8,128)(2,1)S(1)} %add_convert_fusion.1), channel_id=1, source_target_pairs={{0,96},{4,100},{8,104},{12,108},{16,112},{20,116},{24,120},{28,124... | collective-permute-start | bytes 1572872 | tf_op jit(solution)/shard_map/ppermute | solution.py:17
  157.5 46.3 %collective-permute-start.20 = (bf16[256,256]{1,0:T(8,128)(2,1)S(1)}, bf16[256,256]{1,0:T(8,128)(2,1)S(1)}, u32[]{:S(2)}, u32[]{:S(2)}) collective-permute-start(bf16[256,256]{1,0:T(8,128)(2,1)S(1)} %fusion.35), channel_id=1, source_target_pairs={{0,16},{4,20},{8,24},{12,28},{16,0},{20,4},{24,8},{28,12},{32,48},... | collective-permute-start | bytes 393224 | tf_op jit(solution)/shard_map/ppermute | solution.py:17
  174.0 29.7 %all-to-all-start = ((bf16[4,256,256]{2,1,0:T(8,128)(2,1)}), bf16[4,256,256]{2,1,0:T(8,128)(2,1)S(1)}, u32[]{:S(2)}, u32[]{:S(2)}) async-start(bf16[4,256,256]{2,1,0:T(8,128)(2,1)} %bitcast.13), calls=%async_computation | async-start | bytes 1048576 | tf_op jit(solution)/shard_map/all_to_all | solution.py:123
  179.6 4.1 %copy-start.2 = (bf16[128,1024]{1,0:T(8,128)(2,1)S(1)}, bf16[128,1024]{1,0:T(8,128)(2,1)}, u32[]{:S(2)}) copy-start(bf16[128,1024]{1,0:T(8,128)(2,1)} %copy-done.1) | copy-start | bytes 786436
  179.7 4.1 %copy-start.4 = (bf16[128,1024]{1,0:T(8,128)(2,1)S(1)}, bf16[128,1024]{1,0:T(8,128)(2,1)}, u32[]{:S(2)}) copy-start(bf16[128,1024]{1,0:T(8,128)(2,1)} %copy-done.3) | copy-start | bytes 786436
  179.7 4.1 %copy-start.6 = (bf16[1024,256]{1,0:T(8,128)(2,1)S(1)}, bf16[1024,256]{1,0:T(8,128)(2,1)}, u32[]{:S(2)}) copy-start(bf16[1024,256]{1,0:T(8,128)(2,1)} %get-tuple-element.59) | copy-start | bytes 1572868
  179.7 4.1 %copy-start.7 = (bf16[1024,256]{1,0:T(8,128)(2,1)S(1)}, bf16[1024,256]{1,0:T(8,128)(2,1)}, u32[]{:S(2)}) copy-start(bf16[1024,256]{1,0:T(8,128)(2,1)} %get-tuple-element.57) | copy-start | bytes 1572868
  179.7 4.1 %copy-start.8 = (bf16[1024,256]{1,0:T(8,128)(2,1)S(1)}, bf16[1024,256]{1,0:T(8,128)(2,1)}, u32[]{:S(2)}) copy-start(bf16[1024,256]{1,0:T(8,128)(2,1)} %get-tuple-element.55) | copy-start | bytes 1572868
  183.8 20.2 %copy-start.12 = (f32[1,256,2,128]{3,2,1,0:T(2,128)S(1)}, f32[1,256,2,128]{3,2,1,0:T(2,128)}, u32[]{:S(2)}) copy-start(f32[1,256,2,128]{3,2,1,0:T(2,128)} %param.11) | copy-start | bytes 786436
  183.8 20.2 %copy-start.13 = (f32[1,256,2,128]{3,2,1,0:T(2,128)S(1)}, f32[1,256,2,128]{3,2,1,0:T(2,128)}, u32[]{:S(2)}) copy-start(f32[1,256,2,128]{3,2,1,0:T(2,128)} %param.12) | copy-start | bytes 786436

commit v4 on v3

v4 whole, which is shorter than its diff:
```python
import jax
import jax.numpy as jnp
from jax import lax
from jax.sharding import PartitionSpec as P

NX, NZ, NY = 4, 8, 4
HALF = NZ // 2
BF16, F32 = jnp.bfloat16, jnp.float32
ALONG_X = [[NZ * x + z for x in range(NX)] for z in range(NZ)]
IN_HALF = [[NZ * x + HALF * h + k for k in range(HALF)] for x in range(NX) for h in range(2)]


def move_y(value, shift):
    return lax.ppermute(value, "tensor", [(y, (y + shift) % NY) for y in range(NY)])


def swap_z(value, bit):
    pairs = [(NZ * x + z, NZ * x + (z ^ bit)) for x in range(NX) for z in range(NZ)]
    return lax.ppermute(value, "fsdp", pairs)


def exchange(value, groups):
    return lax.all_to_all(value, "fsdp", 0, 0, axis_index_groups=groups)


def move_x(value, shift):
    pairs = [(NZ * x + z, NZ * ((x + shift) % NX) + z) for x in range(NX) for z in range(NZ)]
    return lax.ppermute(value, "fsdp", pairs)


def swap_replica(value, bit):
    return lax.ppermute(value, "replica", [(r, r ^ bit) for r in range(lax.axis_size("replica"))])


def body(
    tokens, cotangent, weights, first_moment, second_moment, frag_global, frag_moment, frag_local
):
    rows = tokens.shape[0]
    depth = weights.shape[1]
    columns = weights.shape[2] * weights.shape[3]
    part = HALF * depth
    x = lax.axis_index("fsdp") // NZ
    z = lax.axis_index("fsdp") % NZ
    side = z // HALF
    y = lax.axis_index("tensor")

    def pick(value, index):
        return lax.dynamic_index_in_dim(value, index, axis=0, keepdims=False)

    def lot(half):
        starts = [i * NZ * depth + half * part for i in range(NX)]
        return jnp.concatenate(
            [lax.dynamic_slice_in_dim(tokens, start, part, axis=1) for start in starts], axis=1
        )

    far_own, near_own = lot(1 - side), lot(side)
    far_own, block, local = lax.optimization_barrier((far_own, weights[0], frag_local[0]))
    far_before, far_behind = move_y(far_own, 1), move_y(far_own, -1)

    def joined(value, bit, axis):
        moved = swap_z(value, bit)
        low = (z & bit) == 0
        pair = (jnp.where(low, value, moved), jnp.where(low, moved, value))
        return jnp.concatenate(pair, axis=axis)

    block = block.reshape(1, depth, columns)
    two = jnp.concatenate([block, swap_z(block, 4)])
    four = joined(two, 2, 1)

    core = lax.axis_index("replica") % 2
    halves = local.reshape(2, depth // 2, *local.shape[1:])
    mine, other = pick(halves, core), pick(halves, 1 - core)
    pair = (mine.astype(F32) + swap_replica(other, 1).astype(F32)).astype(BF16)
    total = pair.astype(F32) + swap_replica(pair, 2).astype(F32)

    far_before, far_behind, near_own, four, total = lax.optimization_barrier(
        (far_before, far_behind, near_own, four, total)
    )
    far_opposite = move_y(far_before, 1)
    near_behind = move_y(near_own, -1)
    eight = joined(four.reshape(2, 2, depth, columns), 1, 2).reshape(2, part, columns)
    near_behind, far_opposite, near_own, eight = lax.optimization_barrier(
        (near_behind, far_opposite, near_own, eight)
    )
    near_opposite = move_y(near_behind, -1)
    near_before = move_y(near_own, 1)
    far_held = (far_own, far_before, far_behind, far_opposite)
    low, high = move_x(eight, 1), move_x(eight, -1)
    planes = (eight, high, move_x(low, 1), low)
    cot = cotangent.reshape(NY, rows, columns)
    cot = jnp.concatenate(
        [lax.dynamic_slice_in_dim(cot, (y + k) % NY, 1, axis=0) for k in (0, 3, 1, 2)], axis=0
    ).reshape(NY * rows, columns)

    def terms(held):
        terms = lax.dot_general(held, cot, (((0,), (0,)), ((), ())), preferred_element_type=F32)
        return terms.astype(BF16).reshape(NX, part, columns)

    def halve(value, bit):
        value = value.reshape(-1, 2, depth, columns)
        low = (z & bit) == 0
        kept = jnp.where(low, value[:, 0], value[:, 1])
        given = jnp.where(low, value[:, 1], value[:, 0])
        return kept + swap_z(given.astype(BF16), bit).astype(F32)

    far = terms(jnp.concatenate(far_held, axis=0))
    far, total, near_own, near_behind, far_held = lax.optimization_barrier(
        (far, total, near_own, near_behind, far_held)
    )
    blank = jnp.zeros_like(near_own)
    near_rest = jnp.concatenate([near_own, blank, near_behind, blank], axis=0)
    far_held = jnp.concatenate(far_held, axis=0)
    far_held, near_rest = lax.optimization_barrier((far_held, near_rest))
    far = exchange(far, ALONG_X)
    far, near_before, near_opposite = lax.optimization_barrier((far, near_before, near_opposite))
    near_held = lax.dynamic_update_slice(near_rest, near_before, (rows, 0))
    near_held = lax.dynamic_update_slice(near_held, near_opposite, (3 * rows, 0))
    far = far.astype(F32).sum(axis=0)
    crossing = swap_z(halve(halve(far, 1), 2)[0].astype(BF16), 4)
    near = exchange(terms(near_held), ALONG_X).astype(F32).sum(axis=0).astype(BF16)
    near = exchange(near.reshape(HALF, depth, columns), IN_HALF)

    def matrix(other):
        halves = [plane[other] for plane in planes]
        return jnp.concatenate([lax.select_n((i - x) % NX, *halves) for i in range(NX)], axis=0)

    far_matrix, near_matrix = lax.optimization_barrier((matrix(1), matrix(0)))
    projected = jnp.dot(far_held, far_matrix, preferred_element_type=F32)
    projected = projected + jnp.dot(near_held, near_matrix, preferred_element_type=F32)
    projected = projected.astype(BF16).reshape(NY, rows, columns)
    ordered = []
    for row in range(NY):
        k = (row - y) % NY
        place = jnp.where(k == 0, 0, k % 3 + 1)
        ordered.append(lax.dynamic_slice_in_dim(projected, place, 1, axis=0))
    keys_values = jnp.concatenate(ordered, axis=0).reshape(cotangent.shape)

    near, keys_values = lax.optimization_barrier((near, keys_values))
    gradient = near.astype(F32).sum(axis=0) + crossing.astype(F32)
    gradient = gradient.reshape(first_moment.shape)
    first_next = 0.9 * first_moment + 0.1 * gradient
    second_next = 0.95 * second_moment + 0.05 * gradient * gradient
    weight_float = weights.astype(F32)
    update = first_next / (1.0 - 0.9**10) / (jnp.sqrt(second_next / (1.0 - 0.95**10)) + 1e-08)
    weights_next = (weight_float - 0.001 * (update + 0.1 * weight_float)).astype(BF16)

    local_float = frag_local[0].astype(F32)
    total = jnp.stack([total, swap_replica(total, 1)])
    summed = jnp.where(core == 0, total, total[::-1]).reshape(frag_global.shape)
    outer_step = frag_global - summed / lax.axis_size("replica")
    moment_next = 0.9 * frag_moment + outer_step
    global_next = frag_global - 0.7 * (outer_step + 0.9 * moment_next)
    local_next = (0.5 * local_float + 0.5 * global_next).astype(BF16)[None]
    return (
        keys_values,
        weights_next,
        first_next,
        second_next,
        global_next,
        moment_next,
        local_next,
    )


def solution(mesh):
    return jax.shard_map(
        body,
        mesh=mesh,
        in_specs=(
            P(("replica", "fsdp", "tensor"), None),
            P(("replica", "fsdp"), None, "tensor"),
            P("replica", "fsdp", None, "tensor"),
            P("replica", "fsdp", None, "tensor"),
            P("replica", "fsdp", None, "tensor"),
            P("fsdp", None, "tensor"),
            P("fsdp", None, "tensor"),
            P("replica", "fsdp", None, "tensor"),
        ),
        out_specs=(
            P(("replica", "fsdp"), None, "tensor"),
            P("replica", "fsdp", None, "tensor"),
            P("replica", "fsdp", None, "tensor"),
            P("replica", "fsdp", None, "tensor"),
            P("fsdp", None, "tensor"),
            P("fsdp", None, "tensor"),
            P("replica", "fsdp", None, "tensor"),
        ),
        check_vma=False,
    )
```

time: 207 us -> 209 us (level)
  other arithmetic: 10 us -> 29.7 us
  matrix products: 29.6 us -> 11.9 us
  starting transfers between devices: 95.9 us -> 81.3 us
  waiting for transfers between devices: 58.7 us -> 70.6 us
    dot_general x2, matrix products: 23 us -> 2.51 us  [the longest x1 1.27 us: body(): jnp.dot(near_held, near_matrix, preferred_element_type=F32)]
    ppermute x15 -> x9, starting transfers between devices: 46.8 us -> 33.6 us  [the longest x6 23.5 us: swap_z(): return lax.ppermute(value, 'fsdp', pairs)]
    ppermute x2 -> x3, starting transfers between devices: 25.5 us -> 14.7 us  [swap_replica(): lax.ppermute(value, 'replica', [(r, r ^ bit) for r in range(lax.axis_size...]
    select_n x3 -> x5, other arithmetic: 0.65 us -> 10.7 us  [the longest x3 8.6 us: matrix(): lax.select_n((i - x) % NX, *halves)]
    all_to_all x1 -> x3, starting transfers between devices: 3.65 us -> 13.1 us  [exchange(): return lax.all_to_all(value, 'fsdp', 0, 0, axis_index_groups=groups)]
    concatenate x0 -> x4, other arithmetic: none -> 8.51 us  [the longest x1 5.73 us: body(): far_held = jnp.concatenate(far_held, axis=0)]
    ppermute x6, waiting for transfers between devices: 2.15 us -> 9.54 us  [move_y(): lax.ppermute(value, 'tensor', [(y, (y + shift) % NY) for y in range(NY)])]
    all_to_all x1 -> x3, waiting for transfers between devices: 0.01 us -> 6.15 us  [exchange(): return lax.all_to_all(value, 'fsdp', 0, 0, axis_index_groups=groups)]
  transfers between devices with their start and end apart: 24 -> 21, of which waited for: 9 -> 10; matrix products, arithmetic and copies ran while one was open for 19% -> 20% of each run, Pallas kernels for 0% -> 0%
where the time goes in v4:
time: 209 us; the launch traced here: 206 us
  starting transfers between devices  81.3 us (39%)
  waiting for transfers between devices  70.6 us (34%)
  other arithmetic  29.7 us (14%)
  matrix products  11.9 us (6%)
  local copies, waits for them, and re-layouts  10.7 us (5%)
    ppermute x6, waiting for transfers between devices, swap_z(): return lax.ppermute(value, 'fsdp', pairs)  28.5 us
    ppermute x3, waiting for transfers between devices, move_x(): return lax.ppermute(value, 'fsdp', pairs)  24.4 us
    ppermute x6, starting transfers between devices, swap_z(): return lax.ppermute(value, 'fsdp', pairs)  23.5 us
    ppermute x6, starting transfers between devices, move_y(): lax.ppermute(value, 'tensor', [(y, (y + shift) % NY) for y in range(NY)])  19.9 us
    ppermute x3, starting transfers between devices, swap_replica(): lax.ppermute(value, 'replica', [(r, r ^ bit) for r in range(lax.axis_size...  14.7 us
    all_to_all x3, starting transfers between devices, exchange(): return lax.all_to_all(value, 'fsdp', 0, 0, axis_index_groups=groups)  13.1 us
    ppermute x3, starting transfers between devices, move_x(): return lax.ppermute(value, 'fsdp', pairs)  10.1 us
    ppermute x6, waiting for transfers between devices, move_y(): lax.ppermute(value, 'tensor', [(y, (y + shift) % NY) for y in range(NY)])  9.54 us
  transfers between devices with their start and end apart: 21, of which 10 were waited for; matrix products, arithmetic and copies ran while one was open for 20% of the time, Pallas kernels for 0%

profile of v4, /device:TPU:6, one launch (start us, length us, event | category | flops | bytes accessed | tf_op | source)
XLA Modules:
  0.0 205.7 jit_solution(1984374632774867637)
XLA Ops:
  0.7 1.8 constant_dynamic-slice_fusion.11
  2.6 3.5 %collective-permute-start = (bf16[128,4096]{1,0:T(8,128)(2,1)S(1)}, bf16[128,4096]{1,0:T(8,128)(2,1)}, u32[]{:S(2)}, u32[]{:S(2)}) collective-permute-start(bf16[128,4096]{1,0:T(8,128)(2,1)S(1)} %pad_maximum_fusion.4), channel_id=1, source_target_pairs={{0,1},{1,2},{2,3},{3,0},{4,5},{5,6},{6,7},{7,4},{8,9},{9,10},{10,1... | collective-permute-start | bytes 3145736 | tf_op jit(solution)/shard_map/ppermute | solution.py:14
  6.1 3.6 %collective-permute-start.1 = (bf16[128,4096]{1,0:T(8,128)(2,1)S(1)}, bf16[128,4096]{1,0:T(8,128)(2,1)}, u32[]{:S(2)}, u32[]{:S(2)}) collective-permute-start(bf16[128,4096]{1,0:T(8,128)(2,1)S(1)} %pad_maximum_fusion.4), channel_id=1, source_target_pairs={{0,3},{1,0},{2,1},{3,2},{4,7},{5,4},{6,5},{7,6},{8,11},{9,8},{10,9... | collective-permute-start | bytes 3145736 | tf_op jit(solution)/shard_map/ppermute | solution.py:14
  9.7 0.1 reshape.200
  9.8 9.1 %collective-permute-start.2 = (bf16[1,256,256]{2,1,0:T(8,128)(2,1)S(1)}, bf16[1,256,256]{2,1,0:T(8,128)(2,1)S(1)}, u32[]{:S(2)}, u32[]{:S(2)}) collective-permute-start(bf16[1,256,256]{2,1,0:T(8,128)(2,1)S(1)} %reshape.200), channel_id=1, source_target_pairs={{0,16},{4,20},{8,24},{12,28},{16,0},{20,4},{24,8},{28,12},{32,48},... | collective-permute-start | bytes 393224 | tf_op jit(solution)/shard_map/ppermute | solution.py:19
  19.0 1.9 collective-permute-start.4
  20.9 1.2 collective-permute-done.4
  22.1 0.7 fusion.19
  22.8 10.9 %collective-permute-start.5 = (bf16[128,2,128]{2,1,0:T(2,128)(2,1)}, bf16[128,2,128]{2,1,0:T(2,128)(2,1)}, u32[]{:S(2)}, u32[]{:S(2)}) collective-permute-start(bf16[128,2,128]{2,1,0:T(2,128)(2,1)} %fusion.19), channel_id=1, source_target_pairs={{0,256},{128,384},{256,0},{384,128},{1,257},{129,385},{257,1},{385... | collective-permute-start | bytes 196616 | tf_op jit(solution)/shard_map/ppermute | solution.py:32
  33.8 3.4 %collective-permute-start.3 = (bf16[2,256,256]{2,1,0:T(8,128)(2,1)S(1)}, bf16[2,256,256]{2,1,0:T(8,128)(2,1)}, u32[]{:S(2)}, u32[]{:S(2)}) collective-permute-start(bf16[2,256,256]{2,1,0:T(8,128)(2,1)S(1)} %constant_dynamic-update-slice_fusion), channel_id=1, source_target_pairs={{0,8},{4,12},{8,0},{12,4},{16,24},{20,28},{24,16},{28,20},{32,40},... | collective-permute-start | bytes 786440 | tf_op jit(solution)/shard_map/ppermute | solution.py:19
  37.3 0.9 collective-permute-done.5
  38.1 1.5 convert_add_fusion.2
  39.7 14.0 %collective-permute-done.3 = bf16[2,256,256]{2,1,0:T(8,128)(2,1)} collective-permute-done((bf16[2,256,256]{2,1,0:T(8,128)(2,1)S(1)}, bf16[2,256,256]{2,1,0:T(8,128)(2,1)}, u32[]{:S(2)}, u32[]{:S(2)}) %collective-permute-start.3) | collective-permute-done | bytes 262176 | tf_op jit(solution)/shard_map/ppermute | solution.py:19
  53.7 1.0 broadcast_select_fusion.3
  54.7 3.7 %collective-permute-start.6 = (bf16[128,4096]{1,0:T(8,128)(2,1)S(1)}, bf16[128,4096]{1,0:T(8,128)(2,1)}, u32[]{:S(2)}, u32[]{:S(2)}) collective-permute-start(bf16[128,4096]{1,0:T(8,128)(2,1)S(1)} %pad_maximum_fusion.5), channel_id=1, source_target_pairs={{0,3},{1,0},{2,1},{3,2},{4,7},{5,4},{6,5},{7,6},{8,11},{9,8},{10,9... | collective-permute-start | bytes 3145736 | tf_op jit(solution)/shard_map/ppermute | solution.py:14
  58.4 2.1 %collective-permute-start.7 = (bf16[128,4096]{1,0:T(8,128)(2,1)}, bf16[128,4096]{1,0:T(8,128)(2,1)}, u32[]{:S(2)}, u32[]{:S(2)}) collective-permute-start(bf16[128,4096]{1,0:T(8,128)(2,1)} %collective-permute-done), channel_id=1, source_target_pairs={{0,1},{1,2},{2,3},{3,0},{4,5},{5,6},{6,7},{7,4},{8,9},{9,10},{10,1... | collective-permute-start | bytes 3145736 | tf_op jit(solution)/shard_map/ppermute | solution.py:14
  60.6 1.9 collective-permute-start.8
  62.6 1.1 reshape.204
  63.8 12.1 %collective-permute-done.8 = bf16[2,2,256,256]{3,2,1,0:T(8,128)(2,1)} collective-permute-done((bf16[2,2,256,256]{3,2,1,0:T(8,128)(2,1)S(1)}, bf16[2,2,256,256]{3,2,1,0:T(8,128)(2,1)}, u32[]{:S(2)}, u32[]{:S(2)}) %collective-permute-start.8) | collective-permute-done | bytes 524320 | tf_op jit(solution)/shard_map/ppermute | solution.py:19
  75.9 1.1 broadcast_select_fusion.1
  77.1 4.7 %collective-permute-done.6 = bf16[128,4096]{1,0:T(8,128)(2,1)} collective-permute-done((bf16[128,4096]{1,0:T(8,128)(2,1)S(1)}, bf16[128,4096]{1,0:T(8,128)(2,1)}, u32[]{:S(2)}, u32[]{:S(2)}) %collective-permute-start.6) | collective-permute-done | bytes 1048608 | tf_op jit(solution)/shard_map/ppermute | solution.py:14
  81.8 4.9 %collective-permute-done.7 = bf16[128,4096]{1,0:T(8,128)(2,1)} collective-permute-done((bf16[128,4096]{1,0:T(8,128)(2,1)}, bf16[128,4096]{1,0:T(8,128)(2,1)}, u32[]{:S(2)}, u32[]{:S(2)}) %collective-permute-start.7) | collective-permute-done | bytes 1048608 | tf_op jit(solution)/shard_map/ppermute | solution.py:14
  86.7 4.5 %convolution_convert_fusion.1 = bf16[4096,256]{1,0:T(8,128)(2,1)} fusion(bf16[512,256]{1,0:T(8,128)(2,1)S(1)} %bitcast.105, bf16[128,4096]{1,0:T(8,128)(2,1)} %collective-permute-done.7, bf16[128,4096]{1,0:T(8,128)(2,1)} %collective-permute-done.1, bf16[128,4096]{1,0:T(8,128)(2,1)} %collective-permute-done, bf16[128,4096]{1,0:T(8,128)(2,1)S(1)} %pad_maximum_fusion.4), kind=kOutput, calls=%fused_computation.1 | convolution fusion | flops 1091567616 | bytes 6553600 | tf_op jit(solution)/shard_map/dot_general | solution.py:96
  91.2 4.9 %all-to-all-start = ((bf16[4,1024,256]{2,1,0:T(8,128)(2,1)}), bf16[4,1024,256]{2,1,0:T(8,128)(2,1)S(1)}, u32[]{:S(2)}, u32[]{:S(2)}) async-start(bf16[4,1024,256]{2,1,0:T(8,128)(2,1)} %bitcast.98), calls=%async_computation | async-start | bytes 4194304 | tf_op jit(solution)/shard_map/all_to_all | solution.py:23
  96.1 1.9 collective-permute-start.9
  98.0 5.1 %collective-permute-start.10 = (bf16[128,4096]{1,0:T(8,128)(2,1)}, bf16[128,4096]{1,0:T(8,128)(2,1)}, u32[]{:S(2)}, u32[]{:S(2)}) collective-permute-start(bf16[128,4096]{1,0:T(8,128)(2,1)} %collective-permute-done.6), channel_id=1, source_target_pairs={{0,3},{1,0},{2,1},{3,2},{4,7},{5,4},{6,5},{7,6},{8,11},{9,8},{10,9... | collective-permute-start | bytes 3145736 | tf_op jit(solution)/shard_map/ppermute | solution.py:14
  103.2 1.9 collective-permute-start.12
  105.1 3.9 %collective-permute-start.11 = (bf16[2,1024,256]{2,1,0:T(8,128)(2,1)S(1)}, bf16[2,1024,256]{2,1,0:T(8,128)(2,1)}, u32[]{:S(2)}, u32[]{:S(2)}) collective-permute-start(bf16[2,1024,256]{2,1,0:T(8,128)(2,1)S(1)} %bitcast.90), channel_id=1, source_target_pairs={{0,96},{4,100},{8,104},{12,108},{16,112},{20,116},{24,120},{28,124... | collective-permute-start | bytes 3145736 | tf_op jit(solution)/shard_map/ppermute | solution.py:28
  109.0 1.9 collective-permute-start.17
  111.0 0.1 broadcast_in_dim.6
  111.1 5.7 %pad_maximum_fusion = (bf16[512,4096]{1,0:T(8,128)(2,1)}, bf16[512,4096]{1,0:T(8,128)(2,1)}) fusion(bf16[128,4096]{1,0:T(8,128)(2,1)} %collective-permute-done.7, bf16[128,4096]{1,0:T(8,128)(2,1)} %collective-permute-done.1, bf16[128,4096]{1,0:T(8,128)(2,1)} %collective-permute-done, bf16[128,4096]{1,0:T(8,128)(2,1)} %copy-done.3, ...), kind=kLoop, calls=%fused_computation.9 | loop fusion | flops 33554432 | bytes 15728640 | tf_op jit(solution)/shard_map/concatenate | solution.py:112
  116.8 0.1 pad_maximum_fusion.10
  116.9 0.1 fusion.12
  117.0 24.4 %collective-permute-done.12 = bf16[2,1024,256]{2,1,0:T(8,128)(2,1)} collective-permute-done((bf16[2,1024,256]{2,1,0:T(8,128)(2,1)S(1)}, bf16[2,1024,256]{2,1,0:T(8,128)(2,1)}, u32[]{:S(2)}, u32[]{:S(2)}) %collective-permute-start.12) | collective-permute-done | bytes 1048608 | tf_op jit(solution)/shard_map/ppermute | solution.py:28
  141.4 4.2 %collective-permute-start.13 = (bf16[2,1024,256]{2,1,0:T(8,128)(2,1)}, bf16[2,1024,256]{2,1,0:T(8,128)(2,1)}, u32[]{:S(2)}, u32[]{:S(2)}) collective-permute-start(bf16[2,1024,256]{2,1,0:T(8,128)(2,1)} %collective-permute-done.12), channel_id=1, source_target_pairs={{0,32},{4,36},{8,40},{12,44},{16,48},{20,52},{24,56},{28,60},{32,6... | collective-permute-start | bytes 3145736 | tf_op jit(solution)/shard_map/ppermute | solution.py:28
  145.7 1.0 copy-done.5
  146.7 0.3 convert_reduce_fusion
  147.0 1.0 copy-done
  148.0 0.8 fusion.13
  148.7 1.9 collective-permute-start.14
  150.6 1.1 constant_dynamic-update-slice_fusion.3
  151.7 2.4 %constant_dynamic-update-slice_fusion.2 = bf16[512,4096]{1,0:T(8,128)(2,1)} fusion(bf16[512,4096]{1,0:T(8,128)(2,1)} %constant_dynamic-update-slice_fusion.3, bf16[128,4096]{1,0:T(8,128)(2,1)} %collective-permute-done.10), kind=kLoop, calls=%fused_computation.73 | loop fusion | bytes 2097152 | tf_op jit(solution)/shard_map/dynamic_update_slice | solution.py:117
  154.1 4.9 %convolution_convert_fusion = bf16[4096,256]{1,0:T(8,128)(2,1)} fusion(bf16[512,4096]{1,0:T(8,128)(2,1)} %constant_dynamic-update-slice_fusion.2, bf16[512,256]{1,0:T(8,128)(2,1)S(1)} %bitcast.106), kind=kOutput, calls=%fused_computation | convolution fusion | flops 1074790400 | bytes 6553600 | tf_op jit(solution)/shard_map/dot_general | solution.py:96
  159.0 4.5 %all-to-all-start.1 = ((bf16[4,1024,256]{2,1,0:T(8,128)(2,1)}), bf16[4,1024,256]{2,1,0:T(8,128)(2,1)S(1)}, u32[]{:S(2)}, u32[]{:S(2)}) async-start(bf16[4,1024,256]{2,1,0:T(8,128)(2,1)} %bitcast.99), calls=%async_computation.1 | async-start | bytes 4194304 | tf_op jit(solution)/shard_map/all_to_all | solution.py:23
  163.5 1.4 fusion.8
  164.9 3.1 %collective-permute-start.15 = (bf16[1,256,256]{2,1,0:T(8,128)(2,1)S(1)}, bf16[1,256,256]{2,1,0:T(8,128)(2,1)S(1)}, u32[]{:S(2)}, u32[]{:S(2)}) collective-permute-start(bf16[1,256,256]{2,1,0:T(8,128)(2,1)S(1)} %fusion.16), channel_id=1, source_target_pairs={{0,8},{4,12},{8,0},{12,4},{16,24},{20,28},{24,16},{28,20},{32,40},... | collective-permute-start | bytes 393224 | tf_op jit(solution)/shard_map/ppermute | solution.py:19
  168.0 2.3 %fusion.17 = (bf16[1,256,2,128]{3,2,1,0:T(2,128)(2,1)}, f32[256,2,128]{2,1,0:T(2,128)}, f32[256,2,128]{2,1,0:T(2,128)}) fusion(bf16[1,256,2,128]{3,2,1,0:T(2,128)(2,1)S(1)} %copy-done.7, f32[256,2,128]{2,1,0:T(2,128)} %param.13, f32[2,128,2,128]{3,2,1,0:T(2,128)S(1)} %fusion.12, f32[256,2,128]{2,1,0:T(2,128)} %param.14), kind=kLoop, calls=%fused_computation.61 | loop fusion | flops 720896 | bytes 1572864 | tf_op jit(solution)/shard_map/broadcast_in_dim | solution.py:153
  170.3 2.3 %collective-permute-done.15 = bf16[1,256,256]{2,1,0:T(8,128)(2,1)S(1)} collective-permute-done((bf16[1,256,256]{2,1,0:T(8,128)(2,1)S(1)}, bf16[1,256,256]{2,1,0:T(8,128)(2,1)S(1)}, u32[]{:S(2)}, u32[]{:S(2)}) %collective-permute-start.15) | collective-permute-done | bytes 131104 | tf_op jit(solution)/shard_map/ppermute | solution.py:19
  172.7 4.1 %collective-permute-start.16 = (bf16[256,256]{1,0:T(8,128)(2,1)S(1)}, bf16[256,256]{1,0:T(8,128)(2,1)S(1)}, u32[]{:S(2)}, u32[]{:S(2)}) collective-permute-start(bf16[256,256]{1,0:T(8,128)(2,1)S(1)} %fusion.18), channel_id=1, source_target_pairs={{0,16},{4,20},{8,24},{12,28},{16,0},{20,4},{24,8},{28,12},{32,48},... | collective-permute-start | bytes 393224 | tf_op jit(solution)/shard_map/ppermute | solution.py:19
  176.8 2.5 %select_bitcast_fusion.7 = (bf16[1024,256]{1,0:T(8,128)(2,1)}, bf16[1024,256]{1,0:T(8,128)(2,1)}) fusion(pred[]{:T(512)S(6)} %select_n.480, pred[]{:T(512)S(6)} %select_n.477, pred[]{:T(512)S(6)} %select_n.475, bf16[2,1024,256]{2,1,0:T(8,128)(2,1)} %collective-permute-done.12, bf16[2,1024,256]{2,1,0:T(8,128)(2,1)} %collective-permute-done.13, ...), kind=kLoop, calls=%fused_computation.33 | loop fusion | flops 1572864 | bytes 3145734 | tf_op jit(solution)/shard_map/select_n | solution.py:125
  179.2 3.1 %select_bitcast_fusion.1 = (bf16[1024,256]{1,0:T(8,128)(2,1)}, bf16[1024,256]{1,0:T(8,128)(2,1)}, bf16[1024,256]{1,0:T(8,128)(2,1)}) fusion(pred[]{:T(512)S(6)} %select_n.502, pred[]{:T(512)S(6)} %select_n.499, pred[]{:T(512)S(6)} %select_n.497, bf16[2,1024,256]{2,1,0:T(8,128)(2,1)} %collective-permute-done.12, ...), kind=kLoop, calls=%fused_computation.27 | loop fusion | flops 2359296 | bytes 5767174 | tf_op jit(solution)/shard_map/select_n | solution.py:125
  182.3 3.1 %select_bitcast_fusion.3 = (bf16[1024,256]{1,0:T(8,128)(2,1)}, bf16[1024,256]{1,0:T(8,128)(2,1)}, bf16[1024,256]{1,0:T(8,128)(2,1)}) fusion(pred[]{:T(512)S(6)} %select_n.480, pred[]{:T(512)S(6)} %select_n.477, pred[]{:T(512)S(6)} %select_n.475, bf16[2,1024,256]{2,1,0:T(8,128)(2,1)} %collective-permute-done.12, ...), kind=kLoop, calls=%fused_computation.29 | loop fusion | flops 2359296 | bytes 5767174 | tf_op jit(solution)/shard_map/select_n | solution.py:125
  185.4 3.3 %all-to-all-done.1 = bf16[4,1024,256]{2,1,0:T(8,128)(2,1)S(1)} async-done(((bf16[4,1024,256]{2,1,0:T(8,128)(2,1)}), bf16[4,1024,256]{2,1,0:T(8,128)(2,1)S(1)}, u32[]{:S(2)}, u32[]{:S(2)}) %all-to-all-start.1) | async-done | bytes 2097184 | tf_op jit(solution)/shard_map/all_to_all | solution.py:23
  188.7 1.3 reduce_sum.30
  189.9 3.6 %all-to-all-start.2 = ((bf16[4,256,256]{2,1,0:T(8,128)(2,1)}), bf16[4,256,256]{2,1,0:T(8,128)(2,1)S(1)}, u32[]{:S(2)}, u32[]{:S(2)}) async-start(bf16[4,256,256]{2,1,0:T(8,128)(2,1)} %bitcast.10), calls=%async_computation.2 | async-start | bytes 1048576 | tf_op jit(solution)/shard_map/all_to_all | solution.py:23
  193.6 2.7 %pad_maximum_fusion.2 = (bf16[4096,256]{1,0:T(8,128)(2,1)S(1)}, bf16[4096,256]{1,0:T(8,128)(2,1)S(1)}) fusion(bf16[1024,256]{1,0:T(8,128)(2,1)} %get-tuple-element.75, bf16[1024,256]{1,0:T(8,128)(2,1)} %get-tuple-element.78, bf16[1024,256]{1,0:T(8,128)(2,1)} %get-tuple-element.72, bf16[1024,256]{1,0:T(8,128)(2,1)} %get-tuple-element.77, ...), kind=kLoop, calls=%fused_computation.12 | loop fusion | flops 16777216 | bytes 8388608 | tf_op jit(solution)/shard_map/concatenate | solution.py:125
  196.3 0.7 copy-done.1
  197.0 1.2 fusion.22
  198.3 0.4 copy-done.2
  198.7 1.3 fusion.7
  200.0 0.8 reshape.210
  200.8 2.9 %all-to-all-done.2 = bf16[4,256,256]{2,1,0:T(8,128)(2,1)S(1)} async-done(((bf16[4,256,256]{2,1,0:T(8,128)(2,1)}), bf16[4,256,256]{2,1,0:T(8,128)(2,1)S(1)}, u32[]{:S(2)}, u32[]{:S(2)}) %all-to-all-start.2) | async-done | bytes 524320 | tf_op jit(solution)/shard_map/all_to_all | solution.py:23
  203.8 0.1 reshape.213
  204.0 1.7 fusion.15
  (52 shorter events, 0.7 us)
Async XLA Ops:
  0.6 9.1 %copy-start.8 = (bf16[1,256,2,128]{3,2,1,0:T(2,128)(2,1)S(1)}, bf16[1,256,2,128]{3,2,1,0:T(2,128)(2,1)}, u32[]{:S(2)}) copy-start(bf16[1,256,2,128]{3,2,1,0:T(2,128)(2,1)} %param.10) | copy-start | bytes 393220
  0.6 18.3 %copy-start.7 = (bf16[1,256,2,128]{3,2,1,0:T(2,128)(2,1)S(1)}, bf16[1,256,2,128]{3,2,1,0:T(2,128)(2,1)}, u32[]{:S(2)}) copy-start(bf16[1,256,2,128]{3,2,1,0:T(2,128)(2,1)} %param.15) | copy-start | bytes 393220
  2.6 84.1 %copy-start.3 = (bf16[128,4096]{1,0:T(8,128)(2,1)}, bf16[128,4096]{1,0:T(8,128)(2,1)S(1)}, u32[]{:S(2)}) copy-start(bf16[128,4096]{1,0:T(8,128)(2,1)S(1)} %pad_maximum_fusion.4) | copy-start | bytes 3145732
  2.6 52.1 %collective-permute-start = (bf16[128,4096]{1,0:T(8,128)(2,1)S(1)}, bf16[128,4096]{1,0:T(8,128)(2,1)}, u32[]{:S(2)}, u32[]{:S(2)}) collective-permute-start(bf16[128,4096]{1,0:T(8,128)(2,1)S(1)} %pad_maximum_fusion.4), channel_id=1, source_target_pairs={{0,1},{1,2},{2,3},{3,0},{4,5},{5,6},{6,7},{7,4},{8,9},{9,10},{10,1... | collective-permute-start | bytes 3145736 | tf_op jit(solution)/shard_map/ppermute | solution.py:14
  6.1 48.6 %collective-permute-start.1 = (bf16[128,4096]{1,0:T(8,128)(2,1)S(1)}, bf16[128,4096]{1,0:T(8,128)(2,1)}, u32[]{:S(2)}, u32[]{:S(2)}) collective-permute-start(bf16[128,4096]{1,0:T(8,128)(2,1)S(1)} %pad_maximum_fusion.4), channel_id=1, source_target_pairs={{0,3},{1,0},{2,1},{3,2},{4,7},{5,4},{6,5},{7,6},{8,11},{9,8},{10,9... | collective-permute-start | bytes 3145736 | tf_op jit(solution)/shard_map/ppermute | solution.py:14
  9.8 24.0 %collective-permute-start.2 = (bf16[1,256,256]{2,1,0:T(8,128)(2,1)S(1)}, bf16[1,256,256]{2,1,0:T(8,128)(2,1)S(1)}, u32[]{:S(2)}, u32[]{:S(2)}) collective-permute-start(bf16[1,256,256]{2,1,0:T(8,128)(2,1)S(1)} %reshape.200), channel_id=1, source_target_pairs={{0,16},{4,20},{8,24},{12,28},{16,0},{20,4},{24,8},{28,12},{32,48},... | collective-permute-start | bytes 393224 | tf_op jit(solution)/shard_map/ppermute | solution.py:19
  19.0 3.1 %collective-permute-start.4 = (bf16[128,2,128]{2,1,0:T(2,128)(2,1)S(1)}, bf16[128,2,128]{2,1,0:T(2,128)(2,1)S(1)}, u32[]{:S(2)}, u32[]{:S(2)}) collective-permute-start(bf16[128,2,128]{2,1,0:T(2,128)(2,1)S(1)} %dynamic-slice_bitcast_fusion), channel_id=1, source_target_pairs={{0,128},{128,0},{256,384},{384,256},{1,129},{129,1},{257,385},{385... | collective-permute-start | bytes 196616 | tf_op jit(solution)/shard_map/ppermute | solution.py:32
  22.8 15.3 %collective-permute-start.5 = (bf16[128,2,128]{2,1,0:T(2,128)(2,1)}, bf16[128,2,128]{2,1,0:T(2,128)(2,1)}, u32[]{:S(2)}, u32[]{:S(2)}) collective-permute-start(bf16[128,2,128]{2,1,0:T(2,128)(2,1)} %fusion.19), channel_id=1, source_target_pairs={{0,256},{128,384},{256,0},{384,128},{1,257},{129,385},{257,1},{385... | collective-permute-start | bytes 196616 | tf_op jit(solution)/shard_map/ppermute | solution.py:32
  33.8 19.9 %collective-permute-start.3 = (bf16[2,256,256]{2,1,0:T(8,128)(2,1)S(1)}, bf16[2,256,256]{2,1,0:T(8,128)(2,1)}, u32[]{:S(2)}, u32[]{:S(2)}) collective-permute-start(bf16[2,256,256]{2,1,0:T(8,128)(2,1)S(1)} %constant_dynamic-update-slice_fusion), channel_id=1, source_target_pairs={{0,8},{4,12},{8,0},{12,4},{16,24},{20,28},{24,16},{28,20},{32,40},... | collective-permute-start | bytes 786440 | tf_op jit(solution)/shard_map/ppermute | solution.py:19
  37.3 53.9 %copy-start.4 = (bf16[128,4096]{1,0:T(8,128)(2,1)}, bf16[128,4096]{1,0:T(8,128)(2,1)S(1)}, u32[]{:S(2)}) copy-start(bf16[128,4096]{1,0:T(8,128)(2,1)S(1)} %pad_maximum_fusion.5) | copy-start | bytes 3145732
  54.7 27.1 %collective-permute-start.6 = (bf16[128,4096]{1,0:T(8,128)(2,1)S(1)}, bf16[128,4096]{1,0:T(8,128)(2,1)}, u32[]{:S(2)}, u32[]{:S(2)}) collective-permute-start(bf16[128,4096]{1,0:T(8,128)(2,1)S(1)} %pad_maximum_fusion.5), channel_id=1, source_target_pairs={{0,3},{1,0},{2,1},{3,2},{4,7},{5,4},{6,5},{7,6},{8,11},{9,8},{10,9... | collective-permute-start | bytes 3145736 | tf_op jit(solution)/shard_map/ppermute | solution.py:14
  58.4 28.2 %collective-permute-start.7 = (bf16[128,4096]{1,0:T(8,128)(2,1)}, bf16[128,4096]{1,0:T(8,128)(2,1)}, u32[]{:S(2)}, u32[]{:S(2)}) collective-permute-start(bf16[128,4096]{1,0:T(8,128)(2,1)} %collective-permute-done), channel_id=1, source_target_pairs={{0,1},{1,2},{2,3},{3,0},{4,5},{5,6},{6,7},{7,4},{8,9},{9,10},{10,1... | collective-permute-start | bytes 3145736 | tf_op jit(solution)/shard_map/ppermute | solution.py:14
  60.6 15.4 %collective-permute-start.8 = (bf16[2,2,256,256]{3,2,1,0:T(8,128)(2,1)S(1)}, bf16[2,2,256,256]{3,2,1,0:T(8,128)(2,1)}, u32[]{:S(2)}, u32[]{:S(2)}) collective-permute-start(bf16[2,2,256,256]{3,2,1,0:T(8,128)(2,1)S(1)} %bitcast.96), channel_id=1, source_target_pairs={{0,4},{4,0},{8,12},{12,8},{16,20},{20,16},{24,28},{28,24},{32,36},... | collective-permute-start | bytes 1572872 | tf_op jit(solution)/shard_map/ppermute | solution.py:19
  63.8 22.9 %copy-start.11 = (bf16[4,128,256]{2,1,0:T(8,128)(2,1)}, bf16[4,128,256]{2,1,0:T(8,128)(2,1)S(1)}, u32[]{:S(2)}) copy-start(bf16[4,128,256]{2,1,0:T(8,128)(2,1)S(1)} %pad_maximum_fusion.8) | copy-start | bytes 786436
  91.2 17.8 %copy-start.10 = (f32[32,8,128]{2,1,0:T(8,128)S(1)}, f32[32,8,128]{2,1,0:T(8,128)}, u32[]{:S(2)}) copy-start(f32[32,8,128]{2,1,0:T(8,128)} %convert_add_fusion.2) | copy-start | bytes 393220
  91.2 55.4 %all-to-all-start = ((bf16[4,1024,256]{2,1,0:T(8,128)(2,1)}), bf16[4,1024,256]{2,1,0:T(8,128)(2,1)S(1)}, u32[]{:S(2)}, u32[]{:S(2)}) async-start(bf16[4,1024,256]{2,1,0:T(8,128)(2,1)} %bitcast.98), calls=%async_computation | async-start | bytes 4194304 | tf_op jit(solution)/shard_map/all_to_all | solution.py:23
  96.1 49.5 %collective-permute-start.9 = (bf16[128,4096]{1,0:T(8,128)(2,1)}, bf16[128,4096]{1,0:T(8,128)(2,1)S(1)}, u32[]{:S(2)}, u32[]{:S(2)}) collective-permute-start(bf16[128,4096]{1,0:T(8,128)(2,1)} %copy-done.4), channel_id=1, source_target_pairs={{0,1},{1,2},{2,3},{3,0},{4,5},{5,6},{6,7},{7,4},{8,9},{9,10},{10,1... | collective-permute-start | bytes 3145736 | tf_op jit(solution)/shard_map/ppermute | solution.py:14
  98.0 48.6 %collective-permute-start.10 = (bf16[128,4096]{1,0:T(8,128)(2,1)}, bf16[128,4096]{1,0:T(8,128)(2,1)}, u32[]{:S(2)}, u32[]{:S(2)}) collective-permute-start(bf16[128,4096]{1,0:T(8,128)(2,1)} %collective-permute-done.6), channel_id=1, source_target_pairs={{0,3},{1,0},{2,1},{3,2},{4,7},{5,4},{6,5},{7,6},{8,11},{9,8},{10,9... | collective-permute-start | bytes 3145736 | tf_op jit(solution)/shard_map/ppermute | solution.py:14
  103.2 38.2 %collective-permute-start.12 = (bf16[2,1024,256]{2,1,0:T(8,128)(2,1)S(1)}, bf16[2,1024,256]{2,1,0:T(8,128)(2,1)}, u32[]{:S(2)}, u32[]{:S(2)}) collective-permute-start(bf16[2,1024,256]{2,1,0:T(8,128)(2,1)S(1)} %bitcast.89), channel_id=1, source_target_pairs={{0,32},{4,36},{8,40},{12,44},{16,48},{20,52},{24,56},{28,60},{32,6... | collective-permute-start | bytes 3145736 | tf_op jit(solution)/shard_map/ppermute | solution.py:28
  105.1 71.7 %collective-permute-start.11 = (bf16[2,1024,256]{2,1,0:T(8,128)(2,1)S(1)}, bf16[2,1024,256]{2,1,0:T(8,128)(2,1)}, u32[]{:S(2)}, u32[]{:S(2)}) collective-permute-start(bf16[2,1024,256]{2,1,0:T(8,128)(2,1)S(1)} %bitcast.90), channel_id=1, source_target_pairs={{0,96},{4,100},{8,104},{12,108},{16,112},{20,116},{24,120},{28,124... | collective-permute-start | bytes 3145736 | tf_op jit(solution)/shard_map/ppermute | solution.py:28
  109.0 7.8 %collective-permute-start.17 = (f32[128,2,128]{2,1,0:T(2,128)S(1)}, f32[128,2,128]{2,1,0:T(2,128)S(1)}, u32[]{:S(2)}, u32[]{:S(2)}) collective-permute-start(f32[128,2,128]{2,1,0:T(2,128)S(1)} %bitcast.103), channel_id=1, source_target_pairs={{0,128},{128,0},{256,384},{384,256},{1,129},{129,1},{257,385},{385... | collective-permute-start | bytes 393224 | tf_op jit(solution)/shard_map/ppermute | solution.py:32
  141.4 35.4 %collective-permute-start.13 = (bf16[2,1024,256]{2,1,0:T(8,128)(2,1)}, bf16[2,1024,256]{2,1,0:T(8,128)(2,1)}, u32[]{:S(2)}, u32[]{:S(2)}) collective-permute-start(bf16[2,1024,256]{2,1,0:T(8,128)(2,1)} %collective-permute-done.12), channel_id=1, source_target_pairs={{0,32},{4,36},{8,40},{12,44},{16,48},{20,52},{24,56},{28,60},{32,6... | collective-permute-start | bytes 3145736 | tf_op jit(solution)/shard_map/ppermute | solution.py:28
  145.6 1.0 copy-start.5
  146.6 4.0 %copy-start.6 = (bf16[128,4096]{1,0:T(8,128)(2,1)S(1)}, bf16[128,4096]{1,0:T(8,128)(2,1)}, u32[]{:S(2)}) copy-start(bf16[128,4096]{1,0:T(8,128)(2,1)} %copy-done.5) | copy-start | bytes 3145732
  146.6 7.5 %copy-start.12 = (bf16[4,128,256]{2,1,0:T(8,128)(2,1)S(1)}, bf16[4,128,256]{2,1,0:T(8,128)(2,1)}, u32[]{:S(2)}) copy-start(bf16[4,128,256]{2,1,0:T(8,128)(2,1)} %copy-done.11) | copy-start | bytes 786436
  147.0 1.0 copy-start
  148.7 14.8 %collective-permute-start.14 = (bf16[2,256,256]{2,1,0:T(8,128)(2,1)}, bf16[2,256,256]{2,1,0:T(8,128)(2,1)}, u32[]{:S(2)}, u32[]{:S(2)}) collective-permute-start(bf16[2,256,256]{2,1,0:T(8,128)(2,1)} %fusion.13), channel_id=1, source_target_pairs={{0,4},{4,0},{8,12},{12,8},{16,20},{20,16},{24,28},{28,24},{32,36},... | collective-permute-start | bytes 786440 | tf_op jit(solution)/shard_map/ppermute | solution.py:19
  159.0 29.7 %all-to-all-start.1 = ((bf16[4,1024,256]{2,1,0:T(8,128)(2,1)}), bf16[4,1024,256]{2,1,0:T(8,128)(2,1)S(1)}, u32[]{:S(2)}, u32[]{:S(2)}) async-start(bf16[4,1024,256]{2,1,0:T(8,128)(2,1)} %bitcast.99), calls=%async_computation.1 | async-start | bytes 4194304 | tf_op jit(solution)/shard_map/all_to_all | solution.py:23
  164.9 7.8 %collective-permute-start.15 = (bf16[1,256,256]{2,1,0:T(8,128)(2,1)S(1)}, bf16[1,256,256]{2,1,0:T(8,128)(2,1)S(1)}, u32[]{:S(2)}, u32[]{:S(2)}) collective-permute-start(bf16[1,256,256]{2,1,0:T(8,128)(2,1)S(1)} %fusion.16), channel_id=1, source_target_pairs={{0,8},{4,12},{8,0},{12,4},{16,24},{20,28},{24,16},{28,20},{32,40},... | collective-permute-start | bytes 393224 | tf_op jit(solution)/shard_map/ppermute | solution.py:19
  172.7 31.1 %collective-permute-start.16 = (bf16[256,256]{1,0:T(8,128)(2,1)S(1)}, bf16[256,256]{1,0:T(8,128)(2,1)S(1)}, u32[]{:S(2)}, u32[]{:S(2)}) collective-permute-start(bf16[256,256]{1,0:T(8,128)(2,1)S(1)} %fusion.18), channel_id=1, source_target_pairs={{0,16},{4,20},{8,24},{12,28},{16,0},{20,4},{24,8},{28,12},{32,48},... | collective-permute-start | bytes 393224 | tf_op jit(solution)/shard_map/ppermute | solution.py:19
  189.9 13.7 %all-to-all-start.2 = ((bf16[4,256,256]{2,1,0:T(8,128)(2,1)}), bf16[4,256,256]{2,1,0:T(8,128)(2,1)S(1)}, u32[]{:S(2)}, u32[]{:S(2)}) async-start(bf16[4,256,256]{2,1,0:T(8,128)(2,1)} %bitcast.10), calls=%async_computation.2 | async-start | bytes 1048576 | tf_op jit(solution)/shard_map/all_to_all | solution.py:23
  193.6 3.4 %copy-start.1 = (bf16[512,4096]{1,0:T(8,128)(2,1)S(1)}, bf16[512,4096]{1,0:T(8,128)(2,1)}, u32[]{:S(2)}) copy-start(bf16[512,4096]{1,0:T(8,128)(2,1)} %get-tuple-element.57) | copy-start | bytes 12582916
  196.3 2.4 %copy-start.2 = (bf16[512,4096]{1,0:T(8,128)(2,1)S(1)}, bf16[512,4096]{1,0:T(8,128)(2,1)}, u32[]{:S(2)}) copy-start(bf16[512,4096]{1,0:T(8,128)(2,1)} %constant_dynamic-update-slice_fusion.2) | copy-start | bytes 12582916
  198.7 5.3 %copy-start.9 = (bf16[1,256,2,128]{3,2,1,0:T(2,128)(2,1)S(1)}, bf16[1,256,2,128]{3,2,1,0:T(2,128)(2,1)}, u32[]{:S(2)}) copy-start(bf16[1,256,2,128]{3,2,1,0:T(2,128)(2,1)} %param.10) | copy-start | bytes 393220
  198.7 5.3 %copy-start.13 = (f32[1,256,2,128]{3,2,1,0:T(2,128)S(1)}, f32[1,256,2,128]{3,2,1,0:T(2,128)}, u32[]{:S(2)}) copy-start(f32[1,256,2,128]{3,2,1,0:T(2,128)} %param.11) | copy-start | bytes 786436
  198.7 5.3 %copy-start.14 = (f32[1,256,2,128]{3,2,1,0:T(2,128)S(1)}, f32[1,256,2,128]{3,2,1,0:T(2,128)}, u32[]{:S(2)}) copy-start(f32[1,256,2,128]{3,2,1,0:T(2,128)} %param.12) | copy-start | bytes 786436

commit v5 on v3

--- a/solution.py
+++ b/solution.py
@@ -99,7 +99,8 @@
 
     opposite, up, down, here = terms(far_held)
     up, reverse = send_x(opposite, up, down, 1)
-    up, plane = lax.optimization_barrier((up, plane))
+    far_rows = lax.optimization_barrier(far_held)
+    up, plane, far_rows = lax.optimization_barrier((up, plane, far_rows))
     forward = move_x(up, 1)
     far = here.astype(F32) + reverse.astype(F32) + forward.astype(F32)
     def halve(value, bit):
@@ -117,6 +118,8 @@
 
     opposite, up, down, here = terms(near_held)
     down, reverse = send_x(opposite, up, down, -1)
+    near_rows = lax.optimization_barrier(near_held)
+    down, near_rows = lax.optimization_barrier((down, near_rows))
     forward = move_x(down, -1)
     near = here.astype(F32) + reverse.astype(F32) + forward.astype(F32)
     groups = [[NZ * i + HALF * h + k for k in range(HALF)] for i in range(NX) for h in range(2)]
@@ -127,11 +130,13 @@
     def half_plane(j, other):
         return lax.dynamic_slice_in_dim(planes[j], (side ^ other) * part, part, axis=0)
 
-    def project(held, other):
-        matrix = jnp.concatenate([half_plane(j, other) for j in (2, 1, 3, 0)], axis=0)
-        return jnp.dot(held, matrix, preferred_element_type=F32)
-
-    projected = (project(far_held, 1) + project(near_held, 0)).astype(BF16)
+    def matrix(other):
+        return jnp.concatenate([half_plane(j, other) for j in (2, 1, 3, 0)], axis=0)
+
+    far_matrix, near_matrix = lax.optimization_barrier((matrix(1), matrix(0)))
+    projected = jnp.dot(far_rows, far_matrix, preferred_element_type=F32)
+    projected = projected + jnp.dot(near_rows, near_matrix, preferred_element_type=F32)
+    projected = projected.astype(BF16)
     projected = projected.reshape(NY, rows, columns)
     ordered = []
     for row in range(NY):
@@ -140,6 +145,7 @@
         ordered.append(lax.dynamic_slice_in_dim(projected, place, 1, axis=0))
     keys_values = jnp.concatenate(ordered, axis=0).reshape(cotangent.shape)
 
+    pieces, keys_values = lax.optimization_barrier((pieces, keys_values))
     gradient = pieces.astype(F32).sum(axis=0) + crossing
 
     gradient = gradient.reshape(first_moment.shape)

time: 207 us -> 195 us (0.942)
  matrix products: 29.6 us -> 5.15 us
  other arithmetic: 10 us -> 18.2 us
  waiting for transfers between devices: 58.7 us -> 61.3 us
    dot_general x2, matrix products: 23 us -> 2.51 us  [the longest x1 1.27 us: body(): jnp.dot(near_rows, near_matrix, preferred_element_type=F32)]
    concatenate x0 -> x2, other arithmetic: none -> 9.29 us  [the longest x1 7.43 us: body(): jnp.concatenate([far_own, far_before, far_behind, far_opposite], axis=0)]
    dot_general x2, matrix products: 6.56 us -> 2.63 us  [terms(): lax.dot_general(held, cot, (((0,), (0,)), ((), ())), preferred_element_ty...]
    unnamed x31 -> x23, local copies, waits for them, and re-layouts: 0.95 us -> 3.85 us
    ppermute x15, waiting for transfers between devices: 56.6 us -> 58.9 us  [move(): return lax.ppermute(value, 'fsdp', pairs)]
  transfers between devices with their start and end apart: 24 -> 24, of which waited for: 9 -> 10; matrix products, arithmetic and copies ran while one was open for 19% -> 10% of each run, Pallas kernels for 0% -> 0%
where the time goes in v5:
time: 195 us; the launch traced here: 194 us
  starting transfers between devices  95.9 us (49%)
  waiting for transfers between devices  61.3 us (31%)
  other arithmetic  18.2 us (9%)
  local copies, waits for them, and re-layouts  11.6 us (6%)
  matrix products  5.15 us (3%)
    ppermute x15, waiting for transfers between devices, move(): return lax.ppermute(value, 'fsdp', pairs)  58.9 us
    ppermute x15, starting transfers between devices, move(): return lax.ppermute(value, 'fsdp', pairs)  47 us
    ppermute x2, starting transfers between devices, swap_replica(): lax.ppermute(value, 'replica', [(r, r ^ bit) for r in range(lax.axis_size...  25.5 us
    ppermute x6, starting transfers between devices, move_y(): lax.ppermute(value, 'tensor', [(y, (y + shift) % NY) for y in range(NY)])  19.9 us
    concatenate x1, other arithmetic, body(): jnp.concatenate([far_own, far_before, far_behind, far_opposite], axis=0)  7.43 us
  transfers between devices with their start and end apart: 24, of which 10 were waited for; matrix products, arithmetic and copies ran while one was open for 10% of the time, Pallas kernels for 0%

profile of v5, /device:TPU:6, one launch (start us, length us, event | category | flops | bytes accessed | tf_op | source)
XLA Modules:
  0.0 193.9 jit_solution(18202454590148607980)
XLA Ops:
  0.8 1.8 constant_dynamic-slice_fusion.19
  2.6 1.1 pad_maximum_fusion.4
  3.7 3.5 %collective-permute-start = (bf16[128,4096]{1,0:T(8,128)(2,1)}, bf16[128,4096]{1,0:T(8,128)(2,1)}, u32[]{:S(2)}, u32[]{:S(2)}) collective-permute-start(bf16[128,4096]{1,0:T(8,128)(2,1)} %pad_maximum_fusion.4), channel_id=1, source_target_pairs={{0,1},{1,2},{2,3},{3,0},{4,5},{5,6},{6,7},{7,4},{8,9},{9,10},{10,1... | collective-permute-start | bytes 3145736 | tf_op jit(solution)/shard_map/ppermute | solution.py:25
  7.2 3.6 %collective-permute-start.1 = (bf16[128,4096]{1,0:T(8,128)(2,1)}, bf16[128,4096]{1,0:T(8,128)(2,1)}, u32[]{:S(2)}, u32[]{:S(2)}) collective-permute-start(bf16[128,4096]{1,0:T(8,128)(2,1)} %pad_maximum_fusion.4), channel_id=1, source_target_pairs={{0,3},{1,0},{2,1},{3,2},{4,7},{5,4},{6,5},{7,6},{8,11},{9,8},{10,9... | collective-permute-start | bytes 3145736 | tf_op jit(solution)/shard_map/ppermute | solution.py:25
  10.8 9.1 %collective-permute-start.2 = (bf16[1,256,256]{2,1,0:T(8,128)(2,1)S(1)}, bf16[1,256,256]{2,1,0:T(8,128)(2,1)S(1)}, u32[]{:S(2)}, u32[]{:S(2)}) collective-permute-start(bf16[1,256,256]{2,1,0:T(8,128)(2,1)S(1)} %reshape.156), channel_id=1, source_target_pairs={{0,16},{4,20},{8,24},{12,28},{16,0},{20,4},{24,8},{28,12},{32,48},... | collective-permute-start | bytes 393224 | tf_op jit(solution)/shard_map/ppermute | solution.py:17
  20.0 11.3 %collective-permute-done.2 = bf16[1,256,256]{2,1,0:T(8,128)(2,1)S(1)} collective-permute-done((bf16[1,256,256]{2,1,0:T(8,128)(2,1)S(1)}, bf16[1,256,256]{2,1,0:T(8,128)(2,1)S(1)}, u32[]{:S(2)}, u32[]{:S(2)}) %collective-permute-start.2) | collective-permute-done | bytes 131104 | tf_op jit(solution)/shard_map/ppermute | solution.py:17
  31.4 1.9 collective-permute-start.3
  33.4 11.7 %collective-permute-done.3 = bf16[2,1,256,256]{3,2,0,1:T(8,128)(2,1)S(1)} collective-permute-done((bf16[2,1,256,256]{3,2,0,1:T(8,128)(2,1)S(1)}, bf16[2,1,256,256]{3,2,0,1:T(8,128)(2,1)S(1)}, u32[]{:S(2)}, u32[]{:S(2)}) %collective-permute-start.3) | collective-permute-done | bytes 262176 | tf_op jit(solution)/shard_map/ppermute | solution.py:17
  45.2 3.6 %collective-permute-start.4 = (bf16[128,4096]{1,0:T(8,128)(2,1)S(1)}, bf16[128,4096]{1,0:T(8,128)(2,1)}, u32[]{:S(2)}, u32[]{:S(2)}) collective-permute-start(bf16[128,4096]{1,0:T(8,128)(2,1)S(1)} %pad_maximum_fusion.3), channel_id=1, source_target_pairs={{0,3},{1,0},{2,1},{3,2},{4,7},{5,4},{6,5},{7,6},{8,11},{9,8},{10,9... | collective-permute-start | bytes 3145736 | tf_op jit(solution)/shard_map/ppermute | solution.py:25
  48.8 2.2 %collective-permute-start.5 = (bf16[128,4096]{1,0:T(8,128)(2,1)}, bf16[128,4096]{1,0:T(8,128)(2,1)}, u32[]{:S(2)}, u32[]{:S(2)}) collective-permute-start(bf16[128,4096]{1,0:T(8,128)(2,1)} %collective-permute-done), channel_id=1, source_target_pairs={{0,1},{1,2},{2,3},{3,0},{4,5},{5,6},{6,7},{7,4},{8,9},{9,10},{10,1... | collective-permute-start | bytes 3145736 | tf_op jit(solution)/shard_map/ppermute | solution.py:25
  51.0 1.9 collective-permute-start.6
  53.0 1.9 collective-permute-start.21
  55.0 1.1 reshape.158
  56.4 1.0 fusion.6
  57.4 7.0 %collective-permute-done.6 = bf16[2,2,1,256,256]{4,3,0,1,2:T(8,128)(2,1)} collective-permute-done((bf16[2,2,1,256,256]{4,3,0,1,2:T(8,128)(2,1)S(1)}, bf16[2,2,1,256,256]{4,3,0,1,2:T(8,128)(2,1)}, u32[]{:S(2)}, u32[]{:S(2)}) %collective-permute-start.6) | collective-permute-done | bytes 524320 | tf_op jit(solution)/shard_map/ppermute | solution.py:17
  64.5 1.1 maximum_bitcast_fusion
  65.6 2.1 %collective-permute-done.5 = bf16[128,4096]{1,0:T(8,128)(2,1)} collective-permute-done((bf16[128,4096]{1,0:T(8,128)(2,1)}, bf16[128,4096]{1,0:T(8,128)(2,1)}, u32[]{:S(2)}, u32[]{:S(2)}) %collective-permute-start.5) | collective-permute-done | bytes 1048608 | tf_op jit(solution)/shard_map/ppermute | solution.py:25
  67.8 7.4 %pad_maximum_fusion = bf16[512,4096]{1,0:T(8,128)(2,1)S(1)} fusion(bf16[128,4096]{1,0:T(8,128)(2,1)} %collective-permute-done.5, bf16[128,4096]{1,0:T(8,128)(2,1)} %collective-permute-done.1, bf16[128,4096]{1,0:T(8,128)(2,1)} %collective-permute-done, bf16[128,1024]{1,0:T(8,128)(2,1)S(1)} %get-tuple-element.65, bf16[128,1024]{1,0:T(8,128)(2,1)S(1)} %get-tuple-element.66, ...), kind=kLoop, calls=%fused_computation.2 | loop fusion | flops 29360128 | bytes 8388608 | tf_op jit(solution)/shard_map/concatenate | solution.py:76
  75.2 1.3 convolution_convert_fusion
  76.5 0.6 copy-done
  77.2 2.4 %collective-permute-start.12 = (bf16[1024,256]{1,0:T(8,128)(2,1)S(1)}, bf16[1024,256]{1,0:T(8,128)(2,1)S(1)}, u32[]{:S(2)}, u32[]{:S(2)}) collective-permute-start(bf16[1024,256]{1,0:T(8,128)(2,1)S(1)} %get-tuple-element.56), channel_id=1, source_target_pairs={{0,32},{4,36},{8,40},{12,44},{16,48},{20,52},{24,56},{28,60},{32,6... | collective-permute-start | bytes 1572872 | tf_op jit(solution)/shard_map/ppermute | solution.py:17
  79.6 3.5 %collective-permute-start.16 = (bf16[1024,256]{1,0:T(8,128)(2,1)S(1)}, bf16[1024,256]{1,0:T(8,128)(2,1)S(1)}, u32[]{:S(2)}, u32[]{:S(2)}) collective-permute-start(bf16[1024,256]{1,0:T(8,128)(2,1)S(1)} %get-tuple-element.55), channel_id=1, source_target_pairs={{0,96},{4,100},{8,104},{12,108},{16,112},{20,116},{24,120},{28,124... | collective-permute-start | bytes 1572872 | tf_op jit(solution)/shard_map/ppermute | solution.py:17
  83.1 1.9 collective-permute-start.7
  85.0 5.1 %collective-permute-start.8 = (bf16[128,4096]{1,0:T(8,128)(2,1)}, bf16[128,4096]{1,0:T(8,128)(2,1)S(1)}, u32[]{:S(2)}, u32[]{:S(2)}) collective-permute-start(bf16[128,4096]{1,0:T(8,128)(2,1)} %collective-permute-done.4), channel_id=1, source_target_pairs={{0,3},{1,0},{2,1},{3,2},{4,7},{5,4},{6,5},{7,6},{8,11},{9,8},{10,9... | collective-permute-start | bytes 3145736 | tf_op jit(solution)/shard_map/ppermute | solution.py:25
  90.2 0.2 reverse_select_fusion.2
  90.4 0.2 reverse_select_fusion.1
  90.6 0.2 reverse_select_fusion
  90.8 23.6 %collective-permute-start.22 = (bf16[256,2,128]{2,1,0:T(2,128)(2,1)S(1)}, bf16[256,2,128]{2,1,0:T(2,128)(2,1)S(1)}, u32[]{:S(2)}, u32[]{:S(2)}) collective-permute-start(bf16[256,2,128]{2,1,0:T(2,128)(2,1)S(1)} %fusion.6), channel_id=1, source_target_pairs={{0,256},{128,384},{256,0},{384,128},{1,257},{129,385},{257,1},{385... | collective-permute-start | bytes 393224 | tf_op jit(solution)/shard_map/ppermute | solution.py:33
  114.5 0.1 add_convert_fusion
  114.6 3.6 %collective-permute-start.17 = (bf16[1024,256]{1,0:T(8,128)(2,1)S(1)}, bf16[1024,256]{1,0:T(8,128)(2,1)S(1)}, u32[]{:S(2)}, u32[]{:S(2)}) collective-permute-start(bf16[1024,256]{1,0:T(8,128)(2,1)S(1)} %add_convert_fusion), channel_id=1, source_target_pairs={{0,32},{4,36},{8,40},{12,44},{16,48},{20,52},{24,56},{28,60},{32,6... | collective-permute-start | bytes 1572872 | tf_op jit(solution)/shard_map/ppermute | solution.py:17
  118.2 2.2 %collective-permute-start.13 = (bf16[2048,256]{1,0:T(8,128)(2,1)S(1)}, bf16[2048,256]{1,0:T(8,128)(2,1)}, u32[]{:S(2)}, u32[]{:S(2)}) collective-permute-start(bf16[2048,256]{1,0:T(8,128)(2,1)S(1)} %bitcast.71), channel_id=1, source_target_pairs={{0,32},{4,36},{8,40},{12,44},{16,48},{20,52},{24,56},{28,60},{32,6... | collective-permute-start | bytes 3145736 | tf_op jit(solution)/shard_map/ppermute | solution.py:17
  120.5 1.3 constant_dynamic-update-slice_fusion.1
  121.9 1.3 convolution_convert_fusion.1
  123.3 0.7 copy-done.4
  124.0 7.4 %collective-permute-done.17 = bf16[1024,256]{1,0:T(8,128)(2,1)S(1)} collective-permute-done((bf16[1024,256]{1,0:T(8,128)(2,1)S(1)}, bf16[1024,256]{1,0:T(8,128)(2,1)S(1)}, u32[]{:S(2)}, u32[]{:S(2)}) %collective-permute-start.17) | collective-permute-done | bytes 524320 | tf_op jit(solution)/shard_map/ppermute | solution.py:17
  131.4 0.2 convert_add_fusion
  131.6 1.9 collective-permute-start.18
  133.6 2.7 %collective-permute-start.10 = (bf16[1024,256]{1,0:T(8,128)(2,1)S(1)}, bf16[1024,256]{1,0:T(8,128)(2,1)S(1)}, u32[]{:S(2)}, u32[]{:S(2)}) collective-permute-start(bf16[1024,256]{1,0:T(8,128)(2,1)S(1)} %get-tuple-element.58), channel_id=1, source_target_pairs={{0,96},{4,100},{8,104},{12,108},{16,112},{20,116},{24,120},{28,124... | collective-permute-start | bytes 1572872 | tf_op jit(solution)/shard_map/ppermute | solution.py:17
  136.4 1.3 fusion.15
  137.7 2.4 %collective-permute-start.15 = (bf16[2048,256]{1,0:T(8,128)(2,1)S(1)}, bf16[2048,256]{1,0:T(8,128)(2,1)S(1)}, u32[]{:S(2)}, u32[]{:S(2)}) collective-permute-start(bf16[2048,256]{1,0:T(8,128)(2,1)S(1)} %bitcast.72), channel_id=1, source_target_pairs={{0,96},{4,100},{8,104},{12,108},{16,112},{20,116},{24,120},{28,124... | collective-permute-start | bytes 3145736 | tf_op jit(solution)/shard_map/ppermute | solution.py:17
  140.1 4.8 %collective-permute-start.9 = (bf16[1024,256]{1,0:T(8,128)(2,1)S(1)}, bf16[1024,256]{1,0:T(8,128)(2,1)S(1)}, u32[]{:S(2)}, u32[]{:S(2)}) collective-permute-start(bf16[1024,256]{1,0:T(8,128)(2,1)S(1)} %get-tuple-element.57), channel_id=1, source_target_pairs={{0,32},{4,36},{8,40},{12,44},{16,48},{20,52},{24,56},{28,60},{32,6... | collective-permute-start | bytes 1572872 | tf_op jit(solution)/shard_map/ppermute | solution.py:17
  145.1 1.9 collective-permute-start.19
  147.0 6.9 %collective-permute-done.13 = bf16[2048,256]{1,0:T(8,128)(2,1)} collective-permute-done((bf16[2048,256]{1,0:T(8,128)(2,1)S(1)}, bf16[2048,256]{1,0:T(8,128)(2,1)}, u32[]{:S(2)}, u32[]{:S(2)}) %collective-permute-start.13) | collective-permute-done | bytes 1048608 | tf_op jit(solution)/shard_map/ppermute | solution.py:17
  153.9 4.8 %collective-permute-start.14 = (bf16[2048,256]{1,0:T(8,128)(2,1)}, bf16[2048,256]{1,0:T(8,128)(2,1)}, u32[]{:S(2)}, u32[]{:S(2)}) collective-permute-start(bf16[2048,256]{1,0:T(8,128)(2,1)} %collective-permute-done.13), channel_id=1, source_target_pairs={{0,32},{4,36},{8,40},{12,44},{16,48},{20,52},{24,56},{28,60},{32,6... | collective-permute-start | bytes 3145736 | tf_op jit(solution)/shard_map/ppermute | solution.py:17
  158.8 0.1 add_convert_fusion.2
  158.9 1.9 collective-permute-start.11
  161.0 1.9 collective-permute-start.20
  162.9 1.3 constant_dynamic-slice_fusion.5
  164.2 7.4 %collective-permute-done.15 = bf16[2048,256]{1,0:T(8,128)(2,1)S(1)} collective-permute-done((bf16[2048,256]{1,0:T(8,128)(2,1)S(1)}, bf16[2048,256]{1,0:T(8,128)(2,1)S(1)}, u32[]{:S(2)}, u32[]{:S(2)}) %collective-permute-start.15) | collective-permute-done | bytes 1048608 | tf_op jit(solution)/shard_map/ppermute | solution.py:17
  171.6 0.9 constant_dynamic-slice_fusion.6
  172.4 4.7 %collective-permute-done.11 = bf16[1024,256]{1,0:T(8,128)(2,1)S(1)} collective-permute-done((bf16[1024,256]{1,0:T(8,128)(2,1)S(1)}, bf16[1024,256]{1,0:T(8,128)(2,1)S(1)}, u32[]{:S(2)}, u32[]{:S(2)}) %collective-permute-start.11) | collective-permute-done | bytes 524320 | tf_op jit(solution)/shard_map/ppermute | solution.py:17
  177.2 1.0 add_convert_fusion.1
  178.2 3.5 %all-to-all-start = ((bf16[4,256,256]{2,1,0:T(8,128)(2,1)}), bf16[4,256,256]{2,1,0:T(8,128)(2,1)S(1)}, u32[]{:S(2)}, u32[]{:S(2)}) async-start(bf16[4,256,256]{2,1,0:T(8,128)(2,1)} %bitcast.75), calls=%async_computation | async-start | bytes 1048576 | tf_op jit(solution)/shard_map/all_to_all | solution.py:126
  181.7 2.4 %collective-permute-done.14 = bf16[2048,256]{1,0:T(8,128)(2,1)} collective-permute-done((bf16[2048,256]{1,0:T(8,128)(2,1)}, bf16[2048,256]{1,0:T(8,128)(2,1)}, u32[]{:S(2)}, u32[]{:S(2)}) %collective-permute-start.14) | collective-permute-done | bytes 1048608 | tf_op jit(solution)/shard_map/ppermute | solution.py:17
  184.1 1.3 constant_dynamic-slice_fusion.7
  185.3 1.9 pad_maximum_fusion.1
  187.2 0.5 copy-done.1
  187.7 1.2 fusion.20
  188.9 0.6 copy-done.5
  189.5 1.3 fusion
  190.9 0.8 reshape.163
  191.7 0.3 all-to-all-done
  192.0 0.1 reshape.166
  192.2 1.7 fusion.12
  (51 shorter events, 1.3 us)
Async XLA Ops:
  0.6 10.1 %copy-start.2 = (bf16[1,256,2,128]{3,2,1,0:T(2,128)(2,1)S(1)}, bf16[1,256,2,128]{3,2,1,0:T(2,128)(2,1)}, u32[]{:S(2)}) copy-start(bf16[1,256,2,128]{3,2,1,0:T(2,128)(2,1)} %param.10) | copy-start | bytes 393220
  2.6 50.4 %copy-start.3 = (bf16[1,256,2,128]{3,2,1,0:T(2,128)(2,1)S(1)}, bf16[1,256,2,128]{3,2,1,0:T(2,128)(2,1)}, u32[]{:S(2)}) copy-start(bf16[1,256,2,128]{3,2,1,0:T(2,128)(2,1)} %param.15) | copy-start | bytes 393220
  3.7 41.5 %collective-permute-start = (bf16[128,4096]{1,0:T(8,128)(2,1)}, bf16[128,4096]{1,0:T(8,128)(2,1)}, u32[]{:S(2)}, u32[]{:S(2)}) collective-permute-start(bf16[128,4096]{1,0:T(8,128)(2,1)} %pad_maximum_fusion.4), channel_id=1, source_target_pairs={{0,1},{1,2},{2,3},{3,0},{4,5},{5,6},{6,7},{7,4},{8,9},{9,10},{10,1... | collective-permute-start | bytes 3145736 | tf_op jit(solution)/shard_map/ppermute | solution.py:25
  7.2 38.0 %collective-permute-start.1 = (bf16[128,4096]{1,0:T(8,128)(2,1)}, bf16[128,4096]{1,0:T(8,128)(2,1)}, u32[]{:S(2)}, u32[]{:S(2)}) collective-permute-start(bf16[128,4096]{1,0:T(8,128)(2,1)} %pad_maximum_fusion.4), channel_id=1, source_target_pairs={{0,3},{1,0},{2,1},{3,2},{4,7},{5,4},{6,5},{7,6},{8,11},{9,8},{10,9... | collective-permute-start | bytes 3145736 | tf_op jit(solution)/shard_map/ppermute | solution.py:25
  10.8 20.5 %collective-permute-start.2 = (bf16[1,256,256]{2,1,0:T(8,128)(2,1)S(1)}, bf16[1,256,256]{2,1,0:T(8,128)(2,1)S(1)}, u32[]{:S(2)}, u32[]{:S(2)}) collective-permute-start(bf16[1,256,256]{2,1,0:T(8,128)(2,1)S(1)} %reshape.156), channel_id=1, source_target_pairs={{0,16},{4,20},{8,24},{12,28},{16,0},{20,4},{24,8},{28,12},{32,48},... | collective-permute-start | bytes 393224 | tf_op jit(solution)/shard_map/ppermute | solution.py:17
  31.4 13.7 %collective-permute-start.3 = (bf16[2,1,256,256]{3,2,0,1:T(8,128)(2,1)S(1)}, bf16[2,1,256,256]{3,2,0,1:T(8,128)(2,1)S(1)}, u32[]{:S(2)}, u32[]{:S(2)}) collective-permute-start(bf16[2,1,256,256]{3,2,0,1:T(8,128)(2,1)S(1)} %get-tuple-element.84), channel_id=1, source_target_pairs={{0,8},{4,12},{8,0},{12,4},{16,24},{20,28},{24,16},{28,20},{32,40},... | collective-permute-start | bytes 786440 | tf_op jit(solution)/shard_map/ppermute | solution.py:17
  45.2 20.4 %collective-permute-start.4 = (bf16[128,4096]{1,0:T(8,128)(2,1)S(1)}, bf16[128,4096]{1,0:T(8,128)(2,1)}, u32[]{:S(2)}, u32[]{:S(2)}) collective-permute-start(bf16[128,4096]{1,0:T(8,128)(2,1)S(1)} %pad_maximum_fusion.3), channel_id=1, source_target_pairs={{0,3},{1,0},{2,1},{3,2},{4,7},{5,4},{6,5},{7,6},{8,11},{9,8},{10,9... | collective-permute-start | bytes 3145736 | tf_op jit(solution)/shard_map/ppermute | solution.py:25
  48.8 18.9 %collective-permute-start.5 = (bf16[128,4096]{1,0:T(8,128)(2,1)}, bf16[128,4096]{1,0:T(8,128)(2,1)}, u32[]{:S(2)}, u32[]{:S(2)}) collective-permute-start(bf16[128,4096]{1,0:T(8,128)(2,1)} %collective-permute-done), channel_id=1, source_target_pairs={{0,1},{1,2},{2,3},{3,0},{4,5},{5,6},{6,7},{7,4},{8,9},{9,10},{10,1... | collective-permute-start | bytes 3145736 | tf_op jit(solution)/shard_map/ppermute | solution.py:25
  51.0 13.4 %collective-permute-start.6 = (bf16[2,2,1,256,256]{4,3,0,1,2:T(8,128)(2,1)S(1)}, bf16[2,2,1,256,256]{4,3,0,1,2:T(8,128)(2,1)}, u32[]{:S(2)}, u32[]{:S(2)}) collective-permute-start(bf16[2,2,1,256,256]{4,3,0,1,2:T(8,128)(2,1)S(1)} %pad_maximum_fusion.5), channel_id=1, source_target_pairs={{0,4},{4,0},{8,12},{12,8},{16,20},{20,16},{24,28},{28,24},{32,36},... | collective-permute-start | bytes 1572872 | tf_op jit(solution)/shard_map/ppermute | solution.py:17
  53.0 3.4 %collective-permute-start.21 = (bf16[256,2,128]{2,1,0:T(2,128)(2,1)S(1)}, bf16[256,2,128]{2,1,0:T(2,128)(2,1)}, u32[]{:S(2)}, u32[]{:S(2)}) collective-permute-start(bf16[256,2,128]{2,1,0:T(2,128)(2,1)S(1)} %bitcast.78), channel_id=1, source_target_pairs={{0,128},{128,0},{256,384},{384,256},{1,129},{129,1},{257,385},{385... | collective-permute-start | bytes 393224 | tf_op jit(solution)/shard_map/ppermute | solution.py:33
  75.2 2.0 %copy-start = (bf16[512,4096]{1,0:T(8,128)(2,1)}, bf16[512,4096]{1,0:T(8,128)(2,1)S(1)}, u32[]{:S(2)}) copy-start(bf16[512,4096]{1,0:T(8,128)(2,1)S(1)} %pad_maximum_fusion) | copy-start | bytes 12582916
  77.2 37.2 %collective-permute-start.12 = (bf16[1024,256]{1,0:T(8,128)(2,1)S(1)}, bf16[1024,256]{1,0:T(8,128)(2,1)S(1)}, u32[]{:S(2)}, u32[]{:S(2)}) collective-permute-start(bf16[1024,256]{1,0:T(8,128)(2,1)S(1)} %get-tuple-element.56), channel_id=1, source_target_pairs={{0,32},{4,36},{8,40},{12,44},{16,48},{20,52},{24,56},{28,60},{32,6... | collective-permute-start | bytes 1572872 | tf_op jit(solution)/shard_map/ppermute | solution.py:17
  79.6 44.3 %collective-permute-start.16 = (bf16[1024,256]{1,0:T(8,128)(2,1)S(1)}, bf16[1024,256]{1,0:T(8,128)(2,1)S(1)}, u32[]{:S(2)}, u32[]{:S(2)}) collective-permute-start(bf16[1024,256]{1,0:T(8,128)(2,1)S(1)} %get-tuple-element.55), channel_id=1, source_target_pairs={{0,96},{4,100},{8,104},{12,108},{16,112},{20,116},{24,120},{28,124... | collective-permute-start | bytes 1572872 | tf_op jit(solution)/shard_map/ppermute | solution.py:17
  83.1 35.1 %collective-permute-start.7 = (bf16[128,4096]{1,0:T(8,128)(2,1)S(1)}, bf16[128,4096]{1,0:T(8,128)(2,1)S(1)}, u32[]{:S(2)}, u32[]{:S(2)}) collective-permute-start(bf16[128,4096]{1,0:T(8,128)(2,1)S(1)} %pad_maximum_fusion.3), channel_id=1, source_target_pairs={{0,1},{1,2},{2,3},{3,0},{4,5},{5,6},{6,7},{7,4},{8,9},{9,10},{10,1... | collective-permute-start | bytes 3145736 | tf_op jit(solution)/shard_map/ppermute | solution.py:25
  85.0 36.8 %collective-permute-start.8 = (bf16[128,4096]{1,0:T(8,128)(2,1)}, bf16[128,4096]{1,0:T(8,128)(2,1)S(1)}, u32[]{:S(2)}, u32[]{:S(2)}) collective-permute-start(bf16[128,4096]{1,0:T(8,128)(2,1)} %collective-permute-done.4), channel_id=1, source_target_pairs={{0,3},{1,0},{2,1},{3,2},{4,7},{5,4},{6,5},{7,6},{8,11},{9,8},{10,9... | collective-permute-start | bytes 3145736 | tf_op jit(solution)/shard_map/ppermute | solution.py:25
  90.8 45.6 %collective-permute-start.22 = (bf16[256,2,128]{2,1,0:T(2,128)(2,1)S(1)}, bf16[256,2,128]{2,1,0:T(2,128)(2,1)S(1)}, u32[]{:S(2)}, u32[]{:S(2)}) collective-permute-start(bf16[256,2,128]{2,1,0:T(2,128)(2,1)S(1)} %fusion.6), channel_id=1, source_target_pairs={{0,256},{128,384},{256,0},{384,128},{1,257},{129,385},{257,1},{385... | collective-permute-start | bytes 393224 | tf_op jit(solution)/shard_map/ppermute | solution.py:33
  114.6 16.8 %collective-permute-start.17 = (bf16[1024,256]{1,0:T(8,128)(2,1)S(1)}, bf16[1024,256]{1,0:T(8,128)(2,1)S(1)}, u32[]{:S(2)}, u32[]{:S(2)}) collective-permute-start(bf16[1024,256]{1,0:T(8,128)(2,1)S(1)} %add_convert_fusion), channel_id=1, source_target_pairs={{0,32},{4,36},{8,40},{12,44},{16,48},{20,52},{24,56},{28,60},{32,6... | collective-permute-start | bytes 1572872 | tf_op jit(solution)/shard_map/ppermute | solution.py:17
  118.2 35.7 %collective-permute-start.13 = (bf16[2048,256]{1,0:T(8,128)(2,1)S(1)}, bf16[2048,256]{1,0:T(8,128)(2,1)}, u32[]{:S(2)}, u32[]{:S(2)}) collective-permute-start(bf16[2048,256]{1,0:T(8,128)(2,1)S(1)} %bitcast.71), channel_id=1, source_target_pairs={{0,32},{4,36},{8,40},{12,44},{16,48},{20,52},{24,56},{28,60},{32,6... | collective-permute-start | bytes 3145736 | tf_op jit(solution)/shard_map/ppermute | solution.py:17
  121.9 2.0 %copy-start.4 = (bf16[512,4096]{1,0:T(8,128)(2,1)}, bf16[512,4096]{1,0:T(8,128)(2,1)S(1)}, u32[]{:S(2)}) copy-start(bf16[512,4096]{1,0:T(8,128)(2,1)S(1)} %constant_dynamic-update-slice_fusion) | copy-start | bytes 12582916
  124.0 12.4 %copy-start.6 = (f32[256,2,128]{2,1,0:T(2,128)S(1)}, f32[256,2,128]{2,1,0:T(2,128)}, u32[]{:S(2)}) copy-start(f32[256,2,128]{2,1,0:T(2,128)} %param.13) | copy-start | bytes 786436
  124.0 12.4 %copy-start.7 = (f32[256,2,128]{2,1,0:T(2,128)S(1)}, f32[256,2,128]{2,1,0:T(2,128)}, u32[]{:S(2)}) copy-start(f32[256,2,128]{2,1,0:T(2,128)} %param.14) | copy-start | bytes 786436
  131.6 13.3 %collective-permute-start.18 = (bf16[2,256,256]{2,1,0:T(8,128)(2,1)S(1)}, bf16[2,256,256]{2,1,0:T(8,128)(2,1)S(1)}, u32[]{:S(2)}, u32[]{:S(2)}) collective-permute-start(bf16[2,256,256]{2,1,0:T(8,128)(2,1)S(1)} %fusion.10), channel_id=1, source_target_pairs={{0,4},{4,0},{8,12},{12,8},{16,20},{20,16},{24,28},{28,24},{32,36},... | collective-permute-start | bytes 786440 | tf_op jit(solution)/shard_map/ppermute | solution.py:17
  133.6 25.1 %collective-permute-start.10 = (bf16[1024,256]{1,0:T(8,128)(2,1)S(1)}, bf16[1024,256]{1,0:T(8,128)(2,1)S(1)}, u32[]{:S(2)}, u32[]{:S(2)}) collective-permute-start(bf16[1024,256]{1,0:T(8,128)(2,1)S(1)} %get-tuple-element.58), channel_id=1, source_target_pairs={{0,96},{4,100},{8,104},{12,108},{16,112},{20,116},{24,120},{28,124... | collective-permute-start | bytes 1572872 | tf_op jit(solution)/shard_map/ppermute | solution.py:17
  137.7 33.9 %collective-permute-start.15 = (bf16[2048,256]{1,0:T(8,128)(2,1)S(1)}, bf16[2048,256]{1,0:T(8,128)(2,1)S(1)}, u32[]{:S(2)}, u32[]{:S(2)}) collective-permute-start(bf16[2048,256]{1,0:T(8,128)(2,1)S(1)} %bitcast.72), channel_id=1, source_target_pairs={{0,96},{4,100},{8,104},{12,108},{16,112},{20,116},{24,120},{28,124... | collective-permute-start | bytes 3145736 | tf_op jit(solution)/shard_map/ppermute | solution.py:17
  140.1 32.3 %collective-permute-start.9 = (bf16[1024,256]{1,0:T(8,128)(2,1)S(1)}, bf16[1024,256]{1,0:T(8,128)(2,1)S(1)}, u32[]{:S(2)}, u32[]{:S(2)}) collective-permute-start(bf16[1024,256]{1,0:T(8,128)(2,1)S(1)} %get-tuple-element.57), channel_id=1, source_target_pairs={{0,32},{4,36},{8,40},{12,44},{16,48},{20,52},{24,56},{28,60},{32,6... | collective-permute-start | bytes 1572872 | tf_op jit(solution)/shard_map/ppermute | solution.py:17
  145.1 15.9 %collective-permute-start.19 = (bf16[1,256,256]{2,1,0:T(8,128)(2,1)S(1)}, bf16[1,256,256]{2,1,0:T(8,128)(2,1)S(1)}, u32[]{:S(2)}, u32[]{:S(2)}) collective-permute-start(bf16[1,256,256]{2,1,0:T(8,128)(2,1)S(1)} %fusion.13), channel_id=1, source_target_pairs={{0,8},{4,12},{8,0},{12,4},{16,24},{20,28},{24,16},{28,20},{32,40},... | collective-permute-start | bytes 393224 | tf_op jit(solution)/shard_map/ppermute | solution.py:17
  153.9 30.1 %collective-permute-start.14 = (bf16[2048,256]{1,0:T(8,128)(2,1)}, bf16[2048,256]{1,0:T(8,128)(2,1)}, u32[]{:S(2)}, u32[]{:S(2)}) collective-permute-start(bf16[2048,256]{1,0:T(8,128)(2,1)} %collective-permute-done.13), channel_id=1, source_target_pairs={{0,32},{4,36},{8,40},{12,44},{16,48},{20,52},{24,56},{28,60},{32,6... | collective-permute-start | bytes 3145736 | tf_op jit(solution)/shard_map/ppermute | solution.py:17
  158.9 18.3 %collective-permute-start.11 = (bf16[1024,256]{1,0:T(8,128)(2,1)S(1)}, bf16[1024,256]{1,0:T(8,128)(2,1)S(1)}, u32[]{:S(2)}, u32[]{:S(2)}) collective-permute-start(bf16[1024,256]{1,0:T(8,128)(2,1)S(1)} %add_convert_fusion.2), channel_id=1, source_target_pairs={{0,96},{4,100},{8,104},{12,108},{16,112},{20,116},{24,120},{28,124... | collective-permute-start | bytes 1572872 | tf_op jit(solution)/shard_map/ppermute | solution.py:17
  161.0 31.0 %collective-permute-start.20 = (bf16[256,256]{1,0:T(8,128)(2,1)S(1)}, bf16[256,256]{1,0:T(8,128)(2,1)S(1)}, u32[]{:S(2)}, u32[]{:S(2)}) collective-permute-start(bf16[256,256]{1,0:T(8,128)(2,1)S(1)} %fusion.14), channel_id=1, source_target_pairs={{0,16},{4,20},{8,24},{12,28},{16,0},{20,4},{24,8},{28,12},{32,48},... | collective-permute-start | bytes 393224 | tf_op jit(solution)/shard_map/ppermute | solution.py:17
  178.2 13.7 %all-to-all-start = ((bf16[4,256,256]{2,1,0:T(8,128)(2,1)}), bf16[4,256,256]{2,1,0:T(8,128)(2,1)S(1)}, u32[]{:S(2)}, u32[]{:S(2)}) async-start(bf16[4,256,256]{2,1,0:T(8,128)(2,1)} %bitcast.75), calls=%async_computation | async-start | bytes 1048576 | tf_op jit(solution)/shard_map/all_to_all | solution.py:126
  185.3 2.3 %copy-start.1 = (bf16[512,4096]{1,0:T(8,128)(2,1)S(1)}, bf16[512,4096]{1,0:T(8,128)(2,1)}, u32[]{:S(2)}) copy-start(bf16[512,4096]{1,0:T(8,128)(2,1)} %copy-done) | copy-start | bytes 12582916
  187.2 2.3 %copy-start.5 = (bf16[512,4096]{1,0:T(8,128)(2,1)S(1)}, bf16[512,4096]{1,0:T(8,128)(2,1)}, u32[]{:S(2)}) copy-start(bf16[512,4096]{1,0:T(8,128)(2,1)} %copy-done.4) | copy-start | bytes 12582916
  189.5 2.7 %copy-start.8 = (f32[1,256,2,128]{3,2,1,0:T(2,128)S(1)}, f32[1,256,2,128]{3,2,1,0:T(2,128)}, u32[]{:S(2)}) copy-start(f32[1,256,2,128]{3,2,1,0:T(2,128)} %param.11) | copy-start | bytes 786436
  189.5 2.7 %copy-start.9 = (f32[1,256,2,128]{3,2,1,0:T(2,128)S(1)}, f32[1,256,2,128]{3,2,1,0:T(2,128)}, u32[]{:S(2)}) copy-start(f32[1,256,2,128]{3,2,1,0:T(2,128)} %param.12) | copy-start | bytes 786436

commit v6 on v5

--- a/solution.py
+++ b/solution.py
@@ -100,7 +100,7 @@
     opposite, up, down, here = terms(far_held)
     up, reverse = send_x(opposite, up, down, 1)
     far_rows = lax.optimization_barrier(far_held)
-    up, plane, far_rows = lax.optimization_barrier((up, plane, far_rows))
+    up, far_rows = lax.optimization_barrier((up, far_rows))
     forward = move_x(up, 1)
     far = here.astype(F32) + reverse.astype(F32) + forward.astype(F32)
     def halve(value, bit):
@@ -157,7 +157,8 @@
 
     local_float = frag_local[0].astype(F32)
     pair = (local_float + swap_replica(frag_local[0], 1).astype(F32)).astype(BF16)
-    summed = pair.astype(F32) + swap_replica(after(pair, eight), 2).astype(F32)
+    pair = after(pair, up)
+    summed = pair.astype(F32) + swap_replica(pair, 2).astype(F32)
     outer_step = frag_global - summed / lax.axis_size("replica")
     moment_next = 0.9 * frag_moment + outer_step
     global_next = frag_global - 0.7 * (outer_step + 0.9 * moment_next)

time: 195 us -> 205 us (1.051); the launches traced: 194 us -> 201 us
  waiting for transfers between devices: 61.3 us -> 72.9 us
  starting transfers between devices: 95.9 us -> 91.8 us
    ppermute x6, waiting for transfers between devices: 2.15 us -> 16.7 us  [move_y(): lax.ppermute(value, 'tensor', [(y, (y + shift) % NY) for y in range(NY)])]
    ppermute x15, waiting for transfers between devices: 58.9 us -> 46.1 us  [move(): return lax.ppermute(value, 'fsdp', pairs)]
    all_to_all x1, waiting for transfers between devices: 0.27 us -> 10.2 us  [body(): lax.all_to_all(near.astype(BF16).reshape(HALF, depth, columns), 'fsdp', 0...]
    ppermute x2, starting transfers between devices: 25.5 us -> 19 us  [swap_replica(): lax.ppermute(value, 'replica', [(r, r ^ bit) for r in range(lax.axis_size...]
  transfers between devices with their start and end apart: 24 -> 24, of which waited for: 10 -> 12; matrix products, arithmetic and copies ran while one was open for 10% -> 13% of each run, Pallas kernels for 0% -> 0%
where the time goes in v6:
time: 205 us; the launch traced here: 201 us
  starting transfers between devices  91.8 us (45%)
  waiting for transfers between devices  72.9 us (36%)
  other arithmetic  18 us (9%)
  local copies, waits for them, and re-layouts  11.4 us (6%)
  matrix products  5.13 us (3%)
    ppermute x15, starting transfers between devices, move(): return lax.ppermute(value, 'fsdp', pairs)  49 us
    ppermute x15, waiting for transfers between devices, move(): return lax.ppermute(value, 'fsdp', pairs)  46.1 us
    ppermute x6, starting transfers between devices, move_y(): lax.ppermute(value, 'tensor', [(y, (y + shift) % NY) for y in range(NY)])  19.7 us
    ppermute x2, starting transfers between devices, swap_replica(): lax.ppermute(value, 'replica', [(r, r ^ bit) for r in range(lax.axis_size...  19 us
    ppermute x6, waiting for transfers between devices, move_y(): lax.ppermute(value, 'tensor', [(y, (y + shift) % NY) for y in range(NY)])  16.7 us
    all_to_all x1, waiting for transfers between devices, body(): lax.all_to_all(near.astype(BF16).reshape(HALF, depth, columns), 'fsdp', 0...  10.2 us
    concatenate x1, other arithmetic, body(): jnp.concatenate([far_own, far_before, far_behind, far_opposite], axis=0)  7.44 us
    unnamed x23, local copies, waits for them, and re-layouts  4.46 us
  transfers between devices with their start and end apart: 24, of which 12 were waited for; matrix products, arithmetic and copies ran while one was open for 13% of the time, Pallas kernels for 0%

profile of v6, /device:TPU:6, one launch (start us, length us, event | category | flops | bytes accessed | tf_op | source)
XLA Modules:
  0.0 200.9 jit_solution(14910136528979292748)
XLA Ops:
  0.8 1.8 constant_dynamic-slice_fusion.19
  2.6 1.1 pad_maximum_fusion.4
  3.7 4.9 %collective-permute-start.1 = (bf16[128,4096]{1,0:T(8,128)(2,1)}, bf16[128,4096]{1,0:T(8,128)(2,1)}, u32[]{:S(2)}, u32[]{:S(2)}) collective-permute-start(bf16[128,4096]{1,0:T(8,128)(2,1)} %pad_maximum_fusion.4), channel_id=1, source_target_pairs={{0,3},{1,0},{2,1},{3,2},{4,7},{5,4},{6,5},{7,6},{8,11},{9,8},{10,9... | collective-permute-start | bytes 3145736 | tf_op jit(solution)/shard_map/ppermute | solution.py:25
  8.6 1.9 collective-permute-start
  10.6 9.1 %collective-permute-start.2 = (bf16[1,256,256]{2,1,0:T(8,128)(2,1)S(1)}, bf16[1,256,256]{2,1,0:T(8,128)(2,1)S(1)}, u32[]{:S(2)}, u32[]{:S(2)}) collective-permute-start(bf16[1,256,256]{2,1,0:T(8,128)(2,1)S(1)} %reshape.156), channel_id=1, source_target_pairs={{0,16},{4,20},{8,24},{12,28},{16,0},{20,4},{24,8},{28,12},{32,48},... | collective-permute-start | bytes 393224 | tf_op jit(solution)/shard_map/ppermute | solution.py:17
  19.8 11.5 %collective-permute-done.2 = bf16[1,256,256]{2,1,0:T(8,128)(2,1)S(1)} collective-permute-done((bf16[1,256,256]{2,1,0:T(8,128)(2,1)S(1)}, bf16[1,256,256]{2,1,0:T(8,128)(2,1)S(1)}, u32[]{:S(2)}, u32[]{:S(2)}) %collective-permute-start.2) | collective-permute-done | bytes 131104 | tf_op jit(solution)/shard_map/ppermute | solution.py:17
  31.4 1.9 collective-permute-start.3
  33.4 13.6 %collective-permute-done.3 = bf16[2,1,256,256]{3,2,0,1:T(8,128)(2,1)S(1)} collective-permute-done((bf16[2,1,256,256]{3,2,0,1:T(8,128)(2,1)S(1)}, bf16[2,1,256,256]{3,2,0,1:T(8,128)(2,1)S(1)}, u32[]{:S(2)}, u32[]{:S(2)}) %collective-permute-start.3) | collective-permute-done | bytes 262176 | tf_op jit(solution)/shard_map/ppermute | solution.py:17
  47.1 3.0 %collective-permute-start.4 = (bf16[128,4096]{1,0:T(8,128)(2,1)S(1)}, bf16[128,4096]{1,0:T(8,128)(2,1)}, u32[]{:S(2)}, u32[]{:S(2)}) collective-permute-start(bf16[128,4096]{1,0:T(8,128)(2,1)S(1)} %pad_maximum_fusion.3), channel_id=1, source_target_pairs={{0,3},{1,0},{2,1},{3,2},{4,7},{5,4},{6,5},{7,6},{8,11},{9,8},{10,9... | collective-permute-start | bytes 3145736 | tf_op jit(solution)/shard_map/ppermute | solution.py:25
  50.1 2.9 %collective-permute-start.5 = (bf16[128,4096]{1,0:T(8,128)(2,1)}, bf16[128,4096]{1,0:T(8,128)(2,1)}, u32[]{:S(2)}, u32[]{:S(2)}) collective-permute-start(bf16[128,4096]{1,0:T(8,128)(2,1)} %collective-permute-done), channel_id=1, source_target_pairs={{0,1},{1,2},{2,3},{3,0},{4,5},{5,6},{6,7},{7,4},{8,9},{9,10},{10,1... | collective-permute-start | bytes 3145736 | tf_op jit(solution)/shard_map/ppermute | solution.py:25
  52.9 1.9 collective-permute-start.6
  54.9 1.9 collective-permute-start.21
  56.8 1.1 reshape.158
  58.3 0.1 fusion.6
  58.4 8.8 %collective-permute-done.6 = bf16[2,2,1,256,256]{4,3,0,1,2:T(8,128)(2,1)} collective-permute-done((bf16[2,2,1,256,256]{4,3,0,1,2:T(8,128)(2,1)S(1)}, bf16[2,2,1,256,256]{4,3,0,1,2:T(8,128)(2,1)}, u32[]{:S(2)}, u32[]{:S(2)}) %collective-permute-start.6) | collective-permute-done | bytes 524320 | tf_op jit(solution)/shard_map/ppermute | solution.py:17
  67.2 1.1 maximum_bitcast_fusion
  68.3 4.8 %collective-permute-done.4 = bf16[128,4096]{1,0:T(8,128)(2,1)} collective-permute-done((bf16[128,4096]{1,0:T(8,128)(2,1)S(1)}, bf16[128,4096]{1,0:T(8,128)(2,1)}, u32[]{:S(2)}, u32[]{:S(2)}) %collective-permute-start.4) | collective-permute-done | bytes 1048608 | tf_op jit(solution)/shard_map/ppermute | solution.py:25
  73.1 3.4 %collective-permute-done.5 = bf16[128,4096]{1,0:T(8,128)(2,1)} collective-permute-done((bf16[128,4096]{1,0:T(8,128)(2,1)}, bf16[128,4096]{1,0:T(8,128)(2,1)}, u32[]{:S(2)}, u32[]{:S(2)}) %collective-permute-start.5) | collective-permute-done | bytes 1048608 | tf_op jit(solution)/shard_map/ppermute | solution.py:25
  76.5 2.4 %collective-permute-start.7 = (bf16[128,4096]{1,0:T(8,128)(2,1)S(1)}, bf16[128,4096]{1,0:T(8,128)(2,1)S(1)}, u32[]{:S(2)}, u32[]{:S(2)}) collective-permute-start(bf16[128,4096]{1,0:T(8,128)(2,1)S(1)} %pad_maximum_fusion.3), channel_id=1, source_target_pairs={{0,1},{1,2},{2,3},{3,0},{4,5},{5,6},{6,7},{7,4},{8,9},{9,10},{10,1... | collective-permute-start | bytes 3145736 | tf_op jit(solution)/shard_map/ppermute | solution.py:25
  78.9 7.4 %pad_maximum_fusion = bf16[512,4096]{1,0:T(8,128)(2,1)S(1)} fusion(bf16[128,4096]{1,0:T(8,128)(2,1)} %collective-permute-done.5, bf16[128,4096]{1,0:T(8,128)(2,1)} %collective-permute-done.1, bf16[128,4096]{1,0:T(8,128)(2,1)} %collective-permute-done, bf16[128,1024]{1,0:T(8,128)(2,1)S(1)} %get-tuple-element.63, bf16[128,1024]{1,0:T(8,128)(2,1)S(1)} %get-tuple-element.64, ...), kind=kLoop, calls=%fused_computation.2 | loop fusion | flops 29360128 | bytes 8388608 | tf_op jit(solution)/shard_map/concatenate | solution.py:76
  86.4 1.3 convolution_convert_fusion
  87.7 0.6 copy-done
  88.4 1.9 collective-permute-start.12
  90.3 0.2 reverse_select_fusion.2
  90.6 0.2 reverse_select_fusion.1
  90.8 0.2 reverse_select_fusion
  91.1 3.9 %collective-permute-start.15 = (bf16[2048,256]{1,0:T(8,128)(2,1)S(1)}, bf16[2048,256]{1,0:T(8,128)(2,1)S(1)}, u32[]{:S(2)}, u32[]{:S(2)}) collective-permute-start(bf16[2048,256]{1,0:T(8,128)(2,1)S(1)} %bitcast.72), channel_id=1, source_target_pairs={{0,96},{4,100},{8,104},{12,108},{16,112},{20,116},{24,120},{28,124... | collective-permute-start | bytes 3145736 | tf_op jit(solution)/shard_map/ppermute | solution.py:17
  95.0 3.1 %collective-permute-start.13 = (bf16[2048,256]{1,0:T(8,128)(2,1)S(1)}, bf16[2048,256]{1,0:T(8,128)(2,1)}, u32[]{:S(2)}, u32[]{:S(2)}) collective-permute-start(bf16[2048,256]{1,0:T(8,128)(2,1)S(1)} %bitcast.73), channel_id=1, source_target_pairs={{0,32},{4,36},{8,40},{12,44},{16,48},{20,52},{24,56},{28,60},{32,6... | collective-permute-start | bytes 3145736 | tf_op jit(solution)/shard_map/ppermute | solution.py:17
  98.2 4.6 %collective-permute-start.8 = (bf16[128,4096]{1,0:T(8,128)(2,1)}, bf16[128,4096]{1,0:T(8,128)(2,1)S(1)}, u32[]{:S(2)}, u32[]{:S(2)}) collective-permute-start(bf16[128,4096]{1,0:T(8,128)(2,1)} %collective-permute-done.4), channel_id=1, source_target_pairs={{0,3},{1,0},{2,1},{3,2},{4,7},{5,4},{6,5},{7,6},{8,11},{9,8},{10,9... | collective-permute-start | bytes 3145736 | tf_op jit(solution)/shard_map/ppermute | solution.py:25
  102.9 2.3 %collective-permute-done.12 = bf16[1024,256]{1,0:T(8,128)(2,1)S(1)} collective-permute-done((bf16[1024,256]{1,0:T(8,128)(2,1)S(1)}, bf16[1024,256]{1,0:T(8,128)(2,1)S(1)}, u32[]{:S(2)}, u32[]{:S(2)}) %collective-permute-start.12) | collective-permute-done | bytes 524320 | tf_op jit(solution)/shard_map/ppermute | solution.py:17
  105.2 2.7 %collective-permute-start.16 = (bf16[1024,256]{1,0:T(8,128)(2,1)S(1)}, bf16[1024,256]{1,0:T(8,128)(2,1)S(1)}, u32[]{:S(2)}, u32[]{:S(2)}) collective-permute-start(bf16[1024,256]{1,0:T(8,128)(2,1)S(1)} %get-tuple-element.53), channel_id=1, source_target_pairs={{0,96},{4,100},{8,104},{12,108},{16,112},{20,116},{24,120},{28,124... | collective-permute-start | bytes 1572872 | tf_op jit(solution)/shard_map/ppermute | solution.py:17
  108.1 4.3 %collective-permute-start.17 = (bf16[1024,256]{1,0:T(8,128)(2,1)S(1)}, bf16[1024,256]{1,0:T(8,128)(2,1)S(1)}, u32[]{:S(2)}, u32[]{:S(2)}) collective-permute-start(bf16[1024,256]{1,0:T(8,128)(2,1)S(1)} %add_convert_fusion), channel_id=1, source_target_pairs={{0,32},{4,36},{8,40},{12,44},{16,48},{20,52},{24,56},{28,60},{32,6... | collective-permute-start | bytes 1572872 | tf_op jit(solution)/shard_map/ppermute | solution.py:17
  112.5 1.3 constant_dynamic-update-slice_fusion.1
  113.8 8.5 %collective-permute-done.8 = bf16[128,4096]{1,0:T(8,128)(2,1)S(1)} collective-permute-done((bf16[128,4096]{1,0:T(8,128)(2,1)}, bf16[128,4096]{1,0:T(8,128)(2,1)S(1)}, u32[]{:S(2)}, u32[]{:S(2)}) %collective-permute-start.8) | collective-permute-done | bytes 1048608 | tf_op jit(solution)/shard_map/ppermute | solution.py:25
  122.4 1.3 convolution_convert_fusion.1
  123.7 0.7 copy-done.4
  124.5 2.4 %collective-permute-start.9 = (bf16[1024,256]{1,0:T(8,128)(2,1)S(1)}, bf16[1024,256]{1,0:T(8,128)(2,1)S(1)}, u32[]{:S(2)}, u32[]{:S(2)}) collective-permute-start(bf16[1024,256]{1,0:T(8,128)(2,1)S(1)} %get-tuple-element.55), channel_id=1, source_target_pairs={{0,32},{4,36},{8,40},{12,44},{16,48},{20,52},{24,56},{28,60},{32,6... | collective-permute-start | bytes 1572872 | tf_op jit(solution)/shard_map/ppermute | solution.py:17
  126.9 1.2 collective-permute-done.16
  128.0 17.0 %collective-permute-start.22 = (bf16[256,2,128]{2,1,0:T(2,128)(2,1)S(1)}, bf16[256,2,128]{2,1,0:T(2,128)(2,1)S(1)}, u32[]{:S(2)}, u32[]{:S(2)}) collective-permute-start(bf16[256,2,128]{2,1,0:T(2,128)(2,1)S(1)} %fusion.6), channel_id=1, source_target_pairs={{0,256},{128,384},{256,0},{384,128},{1,257},{129,385},{257,1},{385... | collective-permute-start | bytes 393224 | tf_op jit(solution)/shard_map/ppermute | solution.py:33
  145.1 2.9 %collective-permute-start.10 = (bf16[1024,256]{1,0:T(8,128)(2,1)S(1)}, bf16[1024,256]{1,0:T(8,128)(2,1)S(1)}, u32[]{:S(2)}, u32[]{:S(2)}) collective-permute-start(bf16[1024,256]{1,0:T(8,128)(2,1)S(1)} %get-tuple-element.56), channel_id=1, source_target_pairs={{0,96},{4,100},{8,104},{12,108},{16,112},{20,116},{24,120},{28,124... | collective-permute-start | bytes 1572872 | tf_op jit(solution)/shard_map/ppermute | solution.py:17
  148.0 0.2 convert_add_fusion
  148.2 2.1 %collective-permute-start.18 = (bf16[2,256,256]{2,1,0:T(8,128)(2,1)S(1)}, bf16[2,256,256]{2,1,0:T(8,128)(2,1)S(1)}, u32[]{:S(2)}, u32[]{:S(2)}) collective-permute-start(bf16[2,256,256]{2,1,0:T(8,128)(2,1)S(1)} %fusion.10), channel_id=1, source_target_pairs={{0,4},{4,0},{8,12},{12,8},{16,20},{20,16},{24,28},{28,24},{32,36},... | collective-permute-start | bytes 786440 | tf_op jit(solution)/shard_map/ppermute | solution.py:17
  150.3 1.3 constant_dynamic-slice_fusion.5
  151.6 4.2 %collective-permute-start.14 = (bf16[2048,256]{1,0:T(8,128)(2,1)}, bf16[2048,256]{1,0:T(8,128)(2,1)}, u32[]{:S(2)}, u32[]{:S(2)}) collective-permute-start(bf16[2048,256]{1,0:T(8,128)(2,1)} %collective-permute-done.13), channel_id=1, source_target_pairs={{0,32},{4,36},{8,40},{12,44},{16,48},{20,52},{24,56},{28,60},{32,6... | collective-permute-start | bytes 3145736 | tf_op jit(solution)/shard_map/ppermute | solution.py:17
  155.9 2.4 %collective-permute-done.18 = bf16[2,256,256]{2,1,0:T(8,128)(2,1)S(1)} collective-permute-done((bf16[2,256,256]{2,1,0:T(8,128)(2,1)S(1)}, bf16[2,256,256]{2,1,0:T(8,128)(2,1)S(1)}, u32[]{:S(2)}, u32[]{:S(2)}) %collective-permute-start.18) | collective-permute-done | bytes 262176 | tf_op jit(solution)/shard_map/ppermute | solution.py:17
  158.3 1.1 collective-permute-done.10
  159.5 2.1 %collective-permute-start.11 = (bf16[1024,256]{1,0:T(8,128)(2,1)S(1)}, bf16[1024,256]{1,0:T(8,128)(2,1)S(1)}, u32[]{:S(2)}, u32[]{:S(2)}) collective-permute-start(bf16[1024,256]{1,0:T(8,128)(2,1)S(1)} %add_convert_fusion.2), channel_id=1, source_target_pairs={{0,96},{4,100},{8,104},{12,108},{16,112},{20,116},{24,120},{28,124... | collective-permute-start | bytes 1572872 | tf_op jit(solution)/shard_map/ppermute | solution.py:17
  161.7 2.2 %collective-permute-start.19 = (bf16[1,256,256]{2,1,0:T(8,128)(2,1)S(1)}, bf16[1,256,256]{2,1,0:T(8,128)(2,1)S(1)}, u32[]{:S(2)}, u32[]{:S(2)}) collective-permute-start(bf16[1,256,256]{2,1,0:T(8,128)(2,1)S(1)} %fusion.13), channel_id=1, source_target_pairs={{0,8},{4,12},{8,0},{12,4},{16,24},{20,28},{24,16},{28,20},{32,40},... | collective-permute-start | bytes 393224 | tf_op jit(solution)/shard_map/ppermute | solution.py:17
  164.0 1.3 fusion.15
  165.3 5.3 %collective-permute-done.19 = bf16[1,256,256]{2,1,0:T(8,128)(2,1)S(1)} collective-permute-done((bf16[1,256,256]{2,1,0:T(8,128)(2,1)S(1)}, bf16[1,256,256]{2,1,0:T(8,128)(2,1)S(1)}, u32[]{:S(2)}, u32[]{:S(2)}) %collective-permute-start.19) | collective-permute-done | bytes 131104 | tf_op jit(solution)/shard_map/ppermute | solution.py:17
  170.6 0.7 fusion.14
  171.3 4.2 %collective-permute-start.20 = (bf16[256,256]{1,0:T(8,128)(2,1)}, bf16[256,256]{1,0:T(8,128)(2,1)S(1)}, u32[]{:S(2)}, u32[]{:S(2)}) collective-permute-start(bf16[256,256]{1,0:T(8,128)(2,1)} %fusion.14), channel_id=1, source_target_pairs={{0,16},{4,20},{8,24},{12,28},{16,0},{20,4},{24,8},{28,12},{32,48},... | collective-permute-start | bytes 393224 | tf_op jit(solution)/shard_map/ppermute | solution.py:17
  175.5 1.0 add_convert_fusion.1
  176.5 4.1 %all-to-all-start = ((bf16[4,256,256]{2,1,0:T(8,128)(2,1)}), bf16[4,256,256]{2,1,0:T(8,128)(2,1)}, u32[]{:S(2)}, u32[]{:S(2)}) async-start(bf16[4,256,256]{2,1,0:T(8,128)(2,1)} %bitcast.75), calls=%async_computation | async-start | bytes 1048576 | tf_op jit(solution)/shard_map/all_to_all | solution.py:126
  180.6 1.3 constant_dynamic-slice_fusion.7
  181.9 0.8 pad_maximum_fusion.1
  182.7 1.4 copy-done.1
  184.1 1.2 fusion.20
  185.4 0.2 copy-done.5
  185.6 1.3 fusion
  187.0 0.8 reshape.163
  187.7 10.2 %all-to-all-done = bf16[4,256,256]{2,1,0:T(8,128)(2,1)} async-done(((bf16[4,256,256]{2,1,0:T(8,128)(2,1)}), bf16[4,256,256]{2,1,0:T(8,128)(2,1)}, u32[]{:S(2)}, u32[]{:S(2)}) %all-to-all-start) | async-done | bytes 524320 | tf_op jit(solution)/shard_map/all_to_all | solution.py:126
  197.9 1.1 convert_reduce_fusion
  199.2 1.7 fusion.12
  (51 shorter events, 1.7 us)
Async XLA Ops:
  0.6 9.9 %copy-start.2 = (bf16[1,256,2,128]{3,2,1,0:T(2,128)(2,1)S(1)}, bf16[1,256,2,128]{3,2,1,0:T(2,128)(2,1)}, u32[]{:S(2)}) copy-start(bf16[1,256,2,128]{3,2,1,0:T(2,128)(2,1)} %param.10) | copy-start | bytes 393220
  2.6 52.2 %copy-start.3 = (bf16[1,256,2,128]{3,2,1,0:T(2,128)(2,1)S(1)}, bf16[1,256,2,128]{3,2,1,0:T(2,128)(2,1)}, u32[]{:S(2)}) copy-start(bf16[1,256,2,128]{3,2,1,0:T(2,128)(2,1)} %param.15) | copy-start | bytes 393220
  3.7 43.4 %collective-permute-start.1 = (bf16[128,4096]{1,0:T(8,128)(2,1)}, bf16[128,4096]{1,0:T(8,128)(2,1)}, u32[]{:S(2)}, u32[]{:S(2)}) collective-permute-start(bf16[128,4096]{1,0:T(8,128)(2,1)} %pad_maximum_fusion.4), channel_id=1, source_target_pairs={{0,3},{1,0},{2,1},{3,2},{4,7},{5,4},{6,5},{7,6},{8,11},{9,8},{10,9... | collective-permute-start | bytes 3145736 | tf_op jit(solution)/shard_map/ppermute | solution.py:25
  8.6 38.5 %collective-permute-start = (bf16[128,4096]{1,0:T(8,128)(2,1)}, bf16[128,4096]{1,0:T(8,128)(2,1)}, u32[]{:S(2)}, u32[]{:S(2)}) collective-permute-start(bf16[128,4096]{1,0:T(8,128)(2,1)} %pad_maximum_fusion.4), channel_id=1, source_target_pairs={{0,1},{1,2},{2,3},{3,0},{4,5},{5,6},{6,7},{7,4},{8,9},{9,10},{10,1... | collective-permute-start | bytes 3145736 | tf_op jit(solution)/shard_map/ppermute | solution.py:25
  10.6 20.7 %collective-permute-start.2 = (bf16[1,256,256]{2,1,0:T(8,128)(2,1)S(1)}, bf16[1,256,256]{2,1,0:T(8,128)(2,1)S(1)}, u32[]{:S(2)}, u32[]{:S(2)}) collective-permute-start(bf16[1,256,256]{2,1,0:T(8,128)(2,1)S(1)} %reshape.156), channel_id=1, source_target_pairs={{0,16},{4,20},{8,24},{12,28},{16,0},{20,4},{24,8},{28,12},{32,48},... | collective-permute-start | bytes 393224 | tf_op jit(solution)/shard_map/ppermute | solution.py:17
  31.4 15.6 %collective-permute-start.3 = (bf16[2,1,256,256]{3,2,0,1:T(8,128)(2,1)S(1)}, bf16[2,1,256,256]{3,2,0,1:T(8,128)(2,1)S(1)}, u32[]{:S(2)}, u32[]{:S(2)}) collective-permute-start(bf16[2,1,256,256]{3,2,0,1:T(8,128)(2,1)S(1)} %get-tuple-element.82), channel_id=1, source_target_pairs={{0,8},{4,12},{8,0},{12,4},{16,24},{20,28},{24,16},{28,20},{32,40},... | collective-permute-start | bytes 786440 | tf_op jit(solution)/shard_map/ppermute | solution.py:17
  47.1 26.1 %collective-permute-start.4 = (bf16[128,4096]{1,0:T(8,128)(2,1)S(1)}, bf16[128,4096]{1,0:T(8,128)(2,1)}, u32[]{:S(2)}, u32[]{:S(2)}) collective-permute-start(bf16[128,4096]{1,0:T(8,128)(2,1)S(1)} %pad_maximum_fusion.3), channel_id=1, source_target_pairs={{0,3},{1,0},{2,1},{3,2},{4,7},{5,4},{6,5},{7,6},{8,11},{9,8},{10,9... | collective-permute-start | bytes 3145736 | tf_op jit(solution)/shard_map/ppermute | solution.py:25
  50.1 26.4 %collective-permute-start.5 = (bf16[128,4096]{1,0:T(8,128)(2,1)}, bf16[128,4096]{1,0:T(8,128)(2,1)}, u32[]{:S(2)}, u32[]{:S(2)}) collective-permute-start(bf16[128,4096]{1,0:T(8,128)(2,1)} %collective-permute-done), channel_id=1, source_target_pairs={{0,1},{1,2},{2,3},{3,0},{4,5},{5,6},{6,7},{7,4},{8,9},{9,10},{10,1... | collective-permute-start | bytes 3145736 | tf_op jit(solution)/shard_map/ppermute | solution.py:25
  52.9 14.3 %collective-permute-start.6 = (bf16[2,2,1,256,256]{4,3,0,1,2:T(8,128)(2,1)S(1)}, bf16[2,2,1,256,256]{4,3,0,1,2:T(8,128)(2,1)}, u32[]{:S(2)}, u32[]{:S(2)}) collective-permute-start(bf16[2,2,1,256,256]{4,3,0,1,2:T(8,128)(2,1)S(1)} %pad_maximum_fusion.5), channel_id=1, source_target_pairs={{0,4},{4,0},{8,12},{12,8},{16,20},{20,16},{24,28},{28,24},{32,36},... | collective-permute-start | bytes 1572872 | tf_op jit(solution)/shard_map/ppermute | solution.py:17
  54.9 3.4 %collective-permute-start.21 = (bf16[256,2,128]{2,1,0:T(2,128)(2,1)S(1)}, bf16[256,2,128]{2,1,0:T(2,128)(2,1)S(1)}, u32[]{:S(2)}, u32[]{:S(2)}) collective-permute-start(bf16[256,2,128]{2,1,0:T(2,128)(2,1)S(1)} %bitcast.78), channel_id=1, source_target_pairs={{0,128},{128,0},{256,384},{384,256},{1,129},{129,1},{257,385},{385... | collective-permute-start | bytes 393224 | tf_op jit(solution)/shard_map/ppermute | solution.py:33
  76.5 31.6 %collective-permute-start.7 = (bf16[128,4096]{1,0:T(8,128)(2,1)S(1)}, bf16[128,4096]{1,0:T(8,128)(2,1)S(1)}, u32[]{:S(2)}, u32[]{:S(2)}) collective-permute-start(bf16[128,4096]{1,0:T(8,128)(2,1)S(1)} %pad_maximum_fusion.3), channel_id=1, source_target_pairs={{0,1},{1,2},{2,3},{3,0},{4,5},{5,6},{6,7},{7,4},{8,9},{9,10},{10,1... | collective-permute-start | bytes 3145736 | tf_op jit(solution)/shard_map/ppermute | solution.py:25
  86.4 2.0 copy-start
  88.4 16.8 %collective-permute-start.12 = (bf16[1024,256]{1,0:T(8,128)(2,1)S(1)}, bf16[1024,256]{1,0:T(8,128)(2,1)S(1)}, u32[]{:S(2)}, u32[]{:S(2)}) collective-permute-start(bf16[1024,256]{1,0:T(8,128)(2,1)S(1)} %get-tuple-element.54), channel_id=1, source_target_pairs={{0,32},{4,36},{8,40},{12,44},{16,48},{20,52},{24,56},{28,60},{32,6... | collective-permute-start | bytes 1572872 | tf_op jit(solution)/shard_map/ppermute | solution.py:17
  91.1 60.5 %collective-permute-start.15 = (bf16[2048,256]{1,0:T(8,128)(2,1)S(1)}, bf16[2048,256]{1,0:T(8,128)(2,1)S(1)}, u32[]{:S(2)}, u32[]{:S(2)}) collective-permute-start(bf16[2048,256]{1,0:T(8,128)(2,1)S(1)} %bitcast.72), channel_id=1, source_target_pairs={{0,96},{4,100},{8,104},{12,108},{16,112},{20,116},{24,120},{28,124... | collective-permute-start | bytes 3145736 | tf_op jit(solution)/shard_map/ppermute | solution.py:17
  95.0 53.2 %collective-permute-start.13 = (bf16[2048,256]{1,0:T(8,128)(2,1)S(1)}, bf16[2048,256]{1,0:T(8,128)(2,1)}, u32[]{:S(2)}, u32[]{:S(2)}) collective-permute-start(bf16[2048,256]{1,0:T(8,128)(2,1)S(1)} %bitcast.73), channel_id=1, source_target_pairs={{0,32},{4,36},{8,40},{12,44},{16,48},{20,52},{24,56},{28,60},{32,6... | collective-permute-start | bytes 3145736 | tf_op jit(solution)/shard_map/ppermute | solution.py:17
  98.2 24.1 %collective-permute-start.8 = (bf16[128,4096]{1,0:T(8,128)(2,1)}, bf16[128,4096]{1,0:T(8,128)(2,1)S(1)}, u32[]{:S(2)}, u32[]{:S(2)}) collective-permute-start(bf16[128,4096]{1,0:T(8,128)(2,1)} %collective-permute-done.4), channel_id=1, source_target_pairs={{0,3},{1,0},{2,1},{3,2},{4,7},{5,4},{6,5},{7,6},{8,11},{9,8},{10,9... | collective-permute-start | bytes 3145736 | tf_op jit(solution)/shard_map/ppermute | solution.py:25
  105.2 22.9 %collective-permute-start.16 = (bf16[1024,256]{1,0:T(8,128)(2,1)S(1)}, bf16[1024,256]{1,0:T(8,128)(2,1)S(1)}, u32[]{:S(2)}, u32[]{:S(2)}) collective-permute-start(bf16[1024,256]{1,0:T(8,128)(2,1)S(1)} %get-tuple-element.53), channel_id=1, source_target_pairs={{0,96},{4,100},{8,104},{12,108},{16,112},{20,116},{24,120},{28,124... | collective-permute-start | bytes 1572872 | tf_op jit(solution)/shard_map/ppermute | solution.py:17
  108.1 37.0 %collective-permute-start.17 = (bf16[1024,256]{1,0:T(8,128)(2,1)S(1)}, bf16[1024,256]{1,0:T(8,128)(2,1)S(1)}, u32[]{:S(2)}, u32[]{:S(2)}) collective-permute-start(bf16[1024,256]{1,0:T(8,128)(2,1)S(1)} %add_convert_fusion), channel_id=1, source_target_pairs={{0,32},{4,36},{8,40},{12,44},{16,48},{20,52},{24,56},{28,60},{32,6... | collective-permute-start | bytes 1572872 | tf_op jit(solution)/shard_map/ppermute | solution.py:17
  122.4 2.0 %copy-start.4 = (bf16[512,4096]{1,0:T(8,128)(2,1)}, bf16[512,4096]{1,0:T(8,128)(2,1)S(1)}, u32[]{:S(2)}) copy-start(bf16[512,4096]{1,0:T(8,128)(2,1)S(1)} %constant_dynamic-update-slice_fusion) | copy-start | bytes 12582916
  124.5 51.0 %collective-permute-start.9 = (bf16[1024,256]{1,0:T(8,128)(2,1)S(1)}, bf16[1024,256]{1,0:T(8,128)(2,1)S(1)}, u32[]{:S(2)}, u32[]{:S(2)}) collective-permute-start(bf16[1024,256]{1,0:T(8,128)(2,1)S(1)} %get-tuple-element.55), channel_id=1, source_target_pairs={{0,32},{4,36},{8,40},{12,44},{16,48},{20,52},{24,56},{28,60},{32,6... | collective-permute-start | bytes 1572872 | tf_op jit(solution)/shard_map/ppermute | solution.py:17
  128.0 35.9 %collective-permute-start.22 = (bf16[256,2,128]{2,1,0:T(2,128)(2,1)S(1)}, bf16[256,2,128]{2,1,0:T(2,128)(2,1)S(1)}, u32[]{:S(2)}, u32[]{:S(2)}) collective-permute-start(bf16[256,2,128]{2,1,0:T(2,128)(2,1)S(1)} %fusion.6), channel_id=1, source_target_pairs={{0,256},{128,384},{256,0},{384,128},{1,257},{129,385},{257,1},{385... | collective-permute-start | bytes 393224 | tf_op jit(solution)/shard_map/ppermute | solution.py:33
  145.1 14.3 %collective-permute-start.10 = (bf16[1024,256]{1,0:T(8,128)(2,1)S(1)}, bf16[1024,256]{1,0:T(8,128)(2,1)S(1)}, u32[]{:S(2)}, u32[]{:S(2)}) collective-permute-start(bf16[1024,256]{1,0:T(8,128)(2,1)S(1)} %get-tuple-element.56), channel_id=1, source_target_pairs={{0,96},{4,100},{8,104},{12,108},{16,112},{20,116},{24,120},{28,124... | collective-permute-start | bytes 1572872 | tf_op jit(solution)/shard_map/ppermute | solution.py:17
  148.2 15.7 %copy-start.6 = (f32[256,2,128]{2,1,0:T(2,128)S(1)}, f32[256,2,128]{2,1,0:T(2,128)}, u32[]{:S(2)}) copy-start(f32[256,2,128]{2,1,0:T(2,128)} %param.13) | copy-start | bytes 786436
  148.2 15.7 %copy-start.7 = (f32[256,2,128]{2,1,0:T(2,128)S(1)}, f32[256,2,128]{2,1,0:T(2,128)}, u32[]{:S(2)}) copy-start(f32[256,2,128]{2,1,0:T(2,128)} %param.14) | copy-start | bytes 786436
  148.2 10.0 %collective-permute-start.18 = (bf16[2,256,256]{2,1,0:T(8,128)(2,1)S(1)}, bf16[2,256,256]{2,1,0:T(8,128)(2,1)S(1)}, u32[]{:S(2)}, u32[]{:S(2)}) collective-permute-start(bf16[2,256,256]{2,1,0:T(8,128)(2,1)S(1)} %fusion.10), channel_id=1, source_target_pairs={{0,4},{4,0},{8,12},{12,8},{16,20},{20,16},{24,28},{28,24},{32,36},... | collective-permute-start | bytes 786440 | tf_op jit(solution)/shard_map/ppermute | solution.py:17
  151.6 29.0 %collective-permute-start.14 = (bf16[2048,256]{1,0:T(8,128)(2,1)}, bf16[2048,256]{1,0:T(8,128)(2,1)}, u32[]{:S(2)}, u32[]{:S(2)}) collective-permute-start(bf16[2048,256]{1,0:T(8,128)(2,1)} %collective-permute-done.13), channel_id=1, source_target_pairs={{0,32},{4,36},{8,40},{12,44},{16,48},{20,52},{24,56},{28,60},{32,6... | collective-permute-start | bytes 3145736 | tf_op jit(solution)/shard_map/ppermute | solution.py:17
  159.5 16.0 %collective-permute-start.11 = (bf16[1024,256]{1,0:T(8,128)(2,1)S(1)}, bf16[1024,256]{1,0:T(8,128)(2,1)S(1)}, u32[]{:S(2)}, u32[]{:S(2)}) collective-permute-start(bf16[1024,256]{1,0:T(8,128)(2,1)S(1)} %add_convert_fusion.2), channel_id=1, source_target_pairs={{0,96},{4,100},{8,104},{12,108},{16,112},{20,116},{24,120},{28,124... | collective-permute-start | bytes 1572872 | tf_op jit(solution)/shard_map/ppermute | solution.py:17
  161.7 8.9 %collective-permute-start.19 = (bf16[1,256,256]{2,1,0:T(8,128)(2,1)S(1)}, bf16[1,256,256]{2,1,0:T(8,128)(2,1)S(1)}, u32[]{:S(2)}, u32[]{:S(2)}) collective-permute-start(bf16[1,256,256]{2,1,0:T(8,128)(2,1)S(1)} %fusion.13), channel_id=1, source_target_pairs={{0,8},{4,12},{8,0},{12,4},{16,24},{20,28},{24,16},{28,20},{32,40},... | collective-permute-start | bytes 393224 | tf_op jit(solution)/shard_map/ppermute | solution.py:17
  171.3 27.7 %collective-permute-start.20 = (bf16[256,256]{1,0:T(8,128)(2,1)}, bf16[256,256]{1,0:T(8,128)(2,1)S(1)}, u32[]{:S(2)}, u32[]{:S(2)}) collective-permute-start(bf16[256,256]{1,0:T(8,128)(2,1)} %fusion.14), channel_id=1, source_target_pairs={{0,16},{4,20},{8,24},{12,28},{16,0},{20,4},{24,8},{28,12},{32,48},... | collective-permute-start | bytes 393224 | tf_op jit(solution)/shard_map/ppermute | solution.py:17
  176.5 21.4 %all-to-all-start = ((bf16[4,256,256]{2,1,0:T(8,128)(2,1)}), bf16[4,256,256]{2,1,0:T(8,128)(2,1)}, u32[]{:S(2)}, u32[]{:S(2)}) async-start(bf16[4,256,256]{2,1,0:T(8,128)(2,1)} %bitcast.75), calls=%async_computation | async-start | bytes 1048576 | tf_op jit(solution)/shard_map/all_to_all | solution.py:126
  181.9 2.2 %copy-start.1 = (bf16[512,4096]{1,0:T(8,128)(2,1)S(1)}, bf16[512,4096]{1,0:T(8,128)(2,1)}, u32[]{:S(2)}) copy-start(bf16[512,4096]{1,0:T(8,128)(2,1)} %copy-done) | copy-start | bytes 12582916
  182.7 2.9 %copy-start.5 = (bf16[512,4096]{1,0:T(8,128)(2,1)S(1)}, bf16[512,4096]{1,0:T(8,128)(2,1)}, u32[]{:S(2)}) copy-start(bf16[512,4096]{1,0:T(8,128)(2,1)} %copy-done.4) | copy-start | bytes 12582916
  185.6 13.6 %copy-start.8 = (f32[1,256,2,128]{3,2,1,0:T(2,128)S(1)}, f32[1,256,2,128]{3,2,1,0:T(2,128)}, u32[]{:S(2)}) copy-start(f32[1,256,2,128]{3,2,1,0:T(2,128)} %param.11) | copy-start | bytes 786436
  185.6 13.6 %copy-start.9 = (f32[1,256,2,128]{3,2,1,0:T(2,128)S(1)}, f32[1,256,2,128]{3,2,1,0:T(2,128)}, u32[]{:S(2)}) copy-start(f32[1,256,2,128]{3,2,1,0:T(2,128)} %param.12) | copy-start | bytes 786436
